TPU v7x, 256 devices: a whole 4x4x8 slice. The times are simulated.
256 devices in a mesh: runs: 16 (over y, z_lo, core), blocks: 16 (over x, z_hi).
Axes of the slice: x: 4, y: 4, z: 8 (z_hi: 4, z_lo: 2; z = z_hi * 2 + z_lo), core: 2. Of those that a mesh axis runs over, the one named last changes fastest.
Arguments:
- signs: bfloat16 [16384, 49152], P('runs', 'blocks'), may hold values from -1 to 1, as said below
- targets: float32 [16384, 128], P('runs'), may hold values from -6 to 6
- weights: float32 [49152, 128], P('blocks'), may hold values from -6 to 6
Outputs:
- fitted: float32 [49152, 128], P('blocks')
- residual: float32 [16384, 128], P(('runs', 'blocks'))
Inputs may be any that keep to these rules, and one draw needn't show every extreme that they name: `signs`: every entry is +1 or -1.
All inputs are finite; a program needn't handle non-finite values.
Results may differ from a plain program's by a relative error of at most 0.004.
Values may be sent and summed in bfloat16 or wider, within the bound.
No kernel may reach another device: no remote copies, remote signals or barrier semaphores. Data moves between devices by JAX's collectives and lax.ppermute only.
A program may use at most 64 MiB of HBM per device.

v0:
```python
import functools
import math

import jax
import jax.numpy as jnp
from jax import lax
from jax.experimental import pallas as pl
from jax.experimental.pallas import tpu as pltpu
from jax.sharding import PartitionSpec as P

ITERS = 3
BF = jnp.bfloat16
F32 = jnp.float32

X_UNIT, ZHI_UNIT = 4, 1
Y_UNIT, ZLO_UNIT, CORE_UNIT = 4, 2, 1
AT_X, AT_ZHI, AT_Y, AT_CORE = range(4)

VMEM_LIMIT = 16 << 20


def shrink(moved, limit_value):
    size = jnp.maximum(jnp.abs(moved) - limit_value, 0.0)
    return jnp.where(moved < 0.0, -size, size)


def swap(array, axis, flip):
    return lax.ppermute(array, axis, [(i, i ^ flip) for i in range(lax.axis_size(axis))])


def swap4(pieces, axis, unit):
    return [swap(pieces[s], axis, s * unit) for s in (1, 2, 3)]


def call(kernel, name, place, args, outs, scratch=(), flops=0, in_hbm=(), outs_in_hbm=False, aliases=None):
    vmem, hbm = (pl.BlockSpec(memory_space=m) for m in (pltpu.VMEM, pltpu.HBM))
    moved = sum(math.prod(a.shape) * a.dtype.itemsize for a in [*args, *outs])
    return pl.pallas_call(
        kernel,
        in_specs=[pl.BlockSpec(memory_space=pltpu.SMEM)] + [hbm if i in in_hbm else vmem for i in range(len(args))],
        out_specs=[hbm if outs_in_hbm else vmem] * len(outs),
        out_shape=list(outs),
        scratch_shapes=list(scratch),
        input_output_aliases=aliases or {},
        compiler_params=pltpu.CompilerParams(vmem_limit_bytes=VMEM_LIMIT),
        cost_estimate=pl.CostEstimate(flops=flops, bytes_accessed=moved, transcendentals=0),
        name=name,
    )(place, *args)


def shape(dims, dtype):
    return jax.ShapeDtypeStruct(dims, dtype)


def part(index, size):
    return pl.ds(pl.multiple_of(index * size, size), size)


def cut(place, chunk_of, acc, outs):
    rows = outs[0].shape[0]

    @pl.loop(0, 4)
    def _(s):
        acc[s] = chunk_of(part(place[AT_X] ^ s, rows))

    for s, out in enumerate(outs):
        out[...] = acc[s].astype(out.dtype)


def first_kernel(place, s_ref, w_ref, p0, p1, p2, p3, own_ref, held, acc):
    width = own_ref.shape[1]
    held[...] = w_ref[...].astype(BF)
    cut(
        place, lambda at: jnp.dot(s_ref[at, :], held[...], preferred_element_type=F32), acc, (p0, p1, p2, p3)
    )
    own_ref[...] = w_ref[part(place[AT_CORE] * 4 + place[AT_Y], width), :].T


ACROSS = (((1,), (1,)), ((), ()))


def pair_kernel(place, a_ref, b_ref, out_ref):
    width = a_ref.shape[1]
    out_ref[:, :width] = a_ref[...]
    out_ref[:, width:] = b_ref[...]


def put_together(place, pieces, held):
    width = held.shape[1] // 4
    for s, piece in enumerate(pieces):
        held[:, part(place[AT_Y] ^ s, width)] = piece


def own_half_kernel(place, s_ref, w0, w1, w2, w3, acc_ref, held):
    put_together(place, (w0[...], w1[...], w2[...], w3[...]), held)
    columns = part(place[AT_CORE], held.shape[1])
    rows = acc_ref.shape[0] // 4

    @pl.loop(0, 4)
    def _(i):
        at = part(i, rows)
        acc_ref[at, :] = lax.dot_general(s_ref[at, columns], held[...], ACROSS, preferred_element_type=F32)


def other_half_kernel(place, s_ref, acc_ref, w03, w12, p0, p1, p2, p3, held, acc):
    width = held.shape[1] // 4
    put_together(place, (w03[:, :width], w12[:, :width], w12[:, width:], w03[:, width:]), held)
    columns = part(place[AT_CORE] ^ 1, held.shape[1])

    def chunk_of(at):
        rest = lax.dot_general(s_ref[at, columns], held[...], ACROSS, preferred_element_type=F32)
        return acc_ref[at, :] + rest

    cut(place, chunk_of, acc, (p0, p1, p2, p3))


def sum_kernel(place, p0, g1, g2, g3, sum_ref, half_ref):
    total = (p0[...] + g1[...].astype(F32)) + (g2[...].astype(F32) + g3[...].astype(F32))
    sum_ref[...] = total
    half_ref[...] = total.astype(BF)


def sum2_kernel(place, a_ref, b_ref, sum_ref, half_ref):
    total = a_ref[...] + b_ref[...].astype(F32)
    sum_ref[...] = total
    half_ref[...] = total.astype(BF)


def residual_kernel(scale, place, a_ref, b_ref, t_ref, half_ref, *own):
    rows = a_ref.shape[0]
    total = a_ref[...] + b_ref[...].astype(F32)
    residual = total * scale - t_ref[part(place[AT_X], rows), :]
    half_ref[...] = residual.T.astype(BF)
    if own:
        own_ref, held = own
        held[...] = residual
        own_ref[...] = held[part(place[AT_ZHI], own_ref.shape[0]), :]


def gradient_kernel(other, place, s_ref, r0, r1, r2, r3, out_ref, held):
    rows, half = r0.shape[1], out_ref.shape[1]
    for s, piece in enumerate((r0, r1, r2, r3)):
        held[:, part(place[AT_X] ^ s, rows)] = piece[...]
    tile = half // 3

    @pl.loop(0, 3)
    def _(i):
        columns = part((place[AT_CORE] ^ other) * 3 + i, tile)
        out_ref[:, part(i, tile)] = jnp.dot(held[...], s_ref[:, columns], preferred_element_type=F32).astype(out_ref.dtype)


def join_kernel(place, kept, got, p0, p1, p2, p3):
    width = p0.shape[1]
    for s, out in enumerate((p0, p1, p2, p3)):
        at = part(place[AT_Y] ^ s, width)
        out[...] = (kept[:, at] + got[:, at].astype(F32)).astype(out.dtype)


def half_kernel(place, p0, g1, g2, g3, half_ref):
    total = (p0[...] + g1[...].astype(F32)) + (g2[...].astype(F32) + g3[...].astype(F32))
    half_ref[...] = total.astype(BF)


def update_kernel(factor, limit_value, place, kept, got, fitted_ref, new_ref, half_ref):
    gradient = kept[...].astype(F32) + got[...].astype(F32)
    fitted = shrink(fitted_ref[...] - factor * gradient, limit_value)
    new_ref[...] = fitted
    half_ref[...] = fitted.astype(BF)


def place_kernel(other, place, *refs):
    out_hbm, held, sems = refs[-3:]
    width = held.shape[1]
    if other:
        w03, w12 = refs[:2]
        pieces = (w03[:, :width], w12[:, :width], w12[:, width:], w03[:, width:])
    else:
        pieces = [ref[...] for ref in refs[:4]]
    copies = []
    for s, piece in enumerate(pieces):
        held[s] = piece.astype(F32).T
        rows = part((place[AT_CORE] ^ other) * 4 + (place[AT_Y] ^ s), width)
        copies.append(pltpu.make_async_copy(held.at[s], out_hbm.at[rows, :], sems.at[s]))
        copies[-1].start()
    for copy in copies:
        copy.wait()


def body(signs, targets, weights):
    run_dev, blk_dev = signs.shape
    k = weights.shape[1]
    total_runs = run_dev * lax.axis_size("runs")
    total_blocks = blk_dev * lax.axis_size("blocks")
    scale_factor = 1.0 / math.sqrt(total_blocks)
    step_size = 1.0 / (1.0 + math.sqrt(total_runs / total_blocks)) ** 2
    limit_value = 0.5 * step_size
    rows, width, share = run_dev // 4, blk_dev // 8, run_dev // lax.axis_size("blocks")
    at_run, at_block = lax.axis_index("runs"), lax.axis_index("blocks")
    place = jnp.stack([at_block >> 2, at_block & 3, at_run >> 2, at_run & 1]).astype(jnp.int32)
    flops = 2 * run_dev * blk_dev * k
    chunk, chunk_half = shape((rows, k), F32), shape((rows, k), BF)
    piece, piece_half = shape((k, width), F32), shape((k, width), BF)
    cuts = [chunk] + [chunk_half] * 3
    acc_held, w_held = pltpu.VMEM((4, rows, k), F32), pltpu.VMEM((k, blk_dev // 2), BF)
    for turn in range(ITERS):
        if turn == 0:
            *pieces, fitted_own = call(
                first_kernel, "first", place, [signs, weights], [*cuts, piece],
                [pltpu.VMEM((blk_dev, k), BF), acc_held], flops,
            )
        else:
            (acc,) = call(
                own_half_kernel, "own_half", place, [signs, *near], [shape((run_dev, k), F32)], [w_held], flops // 2
            )
            pieces = call(
                other_half_kernel, "other_half", place, [signs, acc, *far], cuts, [w_held, acc_held], flops // 2
            )
        got = swap4(pieces, "blocks", X_UNIT)
        summed, half = call(sum_kernel, "sum", place, [pieces[0], *got], [chunk, chunk_half])
        got = swap(half, "blocks", 1 * ZHI_UNIT)
        summed, half = call(sum2_kernel, "sum2", place, [summed, got], [chunk, chunk_half])
        got = swap(half, "blocks", 3 * ZHI_UNIT)
        last = turn == ITERS - 1
        half, *residual_own = call(
            functools.partial(residual_kernel, scale_factor), "residual", place, [summed, got, targets],
            [shape((k, rows), BF)] + [shape((share, k), F32)] * last, [pltpu.VMEM((rows, k), F32)] * last,
        )
        halves = [half] + swap4([half] * 4, "blocks", X_UNIT)
        held = [pltpu.VMEM((k, run_dev), BF)]
        (sent,) = call(
            functools.partial(gradient_kernel, 1), "gradient_sent", place, [signs, *halves],
            [shape((k, blk_dev // 2), BF)], held, flops // 2,
        )
        got = swap(sent, "runs", CORE_UNIT)
        (kept,) = call(
            functools.partial(gradient_kernel, 0), "gradient_kept", place, [signs, *halves],
            [shape((k, blk_dev // 2), F32)], held, flops // 2,
        )
        pieces = call(join_kernel, "join", place, [kept, got], [piece] + [piece_half] * 3)
        got = swap4(pieces, "runs", Y_UNIT)
        (half,) = call(half_kernel, "half", place, [pieces[0], *got], [piece_half])
        got = swap(half, "runs", ZLO_UNIT)
        fitted_own, half = call(
            functools.partial(update_kernel, step_size * scale_factor, limit_value), "update", place,
            [half, got, fitted_own], [piece, piece_half],
        )
        near = [half] + swap4([half] * 4, "runs", Y_UNIT)
        pairs = [call(pair_kernel, "pair", place, two, [shape((k, 2 * width), BF)])[0] for two in (near[::3], near[1:3])]
        far = [swap(pair, "runs", CORE_UNIT) for pair in pairs]
    held = [pltpu.VMEM((4, width, k), F32), pltpu.SemaphoreType.DMA((4,))]
    whole = [shape((blk_dev, k), F32)]
    fitted = call(functools.partial(place_kernel, 0), "place_near", place, near, whole, held, outs_in_hbm=True)
    (fitted,) = call(
        functools.partial(place_kernel, 1), "place_far", place, [*far, *fitted], whole, held,
        in_hbm=(2,), outs_in_hbm=True, aliases={3: 0},
    )
    return (fitted, residual_own[0])


def solution(mesh):
    in_specs = (P("runs", "blocks"), P("runs", None), P("blocks", None))
    out_specs = (P("blocks", None), P(("runs", "blocks"), None))
    return jax.shard_map(body, mesh=mesh, in_specs=in_specs, out_specs=out_specs, check_vma=False)
```

profile of v0, /device:TPU:1, one launch (start us, length us, event | category | flops | bytes accessed | tf_op | source)
XLA Modules:
  0.0 205.9 jit_solution(4465193826211203884)
XLA Ops:
  0.7 2.8 %copy-done = bf16[1024,3072]{1,0:T(8,128)(2,1)S(1)} copy-done((bf16[1024,3072]{1,0:T(8,128)(2,1)S(1)}, bf16[1024,3072]{1,0:T(8,128)(2,1)}, u32[]{:S(2)}) %copy-start) | copy-done | bytes 6291480
  4.9 3.0 %first.1 = (f32[256,128]{1,0:T(8,128)S(1)}, bf16[256,128]{1,0:T(8,128)(2,1)S(1)}, bf16[256,128]{1,0:T(8,128)(2,1)S(1)}, bf16[256,128]{1,0:T(8,128)(2,1)S(1)}, f32[128,384]{1,0:T(8,128)S(1)}) custom-call(s32[4]{0:T(128)S(1)} %pad_add_fusion.place, bf16[1024,3072]{1,0:T(8,128)(2,1)S(1)} %copy-done, f32[3072,128]{1,0:T(8,128)S(1)} %copy-done.3), custom_call_target="tpu_custom_call" | custom-call | flops 805306368 | bytes 8388608 | tf_op jit(solution)/shard_map/first/pallas_call | solution.py:38
  7.9 2.1 %collective-permute-start = (bf16[256,128]{1,0:T(8,128)(2,1)S(1)}, bf16[256,128]{1,0:T(8,128)(2,1)S(1)}, u32[]{:S(2)}, u32[]{:S(2)}) collective-permute-start(bf16[256,128]{1,0:T(8,128)(2,1)S(1)} %get-tuple-element.47), channel_id=1, source_target_pairs={{0,4},{1,5},{2,6},{3,7},{4,0},{5,1},{6,2},{7,3},{8,12},{9,13},{10,... | collective-permute-start | bytes 196616 | tf_op jit(solution)/shard_map/ppermute | solution.py:28
  10.1 2.4 %collective-permute-start.1 = (bf16[256,128]{1,0:T(8,128)(2,1)S(1)}, bf16[256,128]{1,0:T(8,128)(2,1)S(1)}, u32[]{:S(2)}, u32[]{:S(2)}) collective-permute-start(bf16[256,128]{1,0:T(8,128)(2,1)S(1)} %get-tuple-element.48), channel_id=1, source_target_pairs={{0,8},{1,9},{2,10},{3,11},{4,12},{5,13},{6,14},{7,15},{8,0},{9,1},... | collective-permute-start | bytes 196616 | tf_op jit(solution)/shard_map/ppermute | solution.py:28
  12.6 2.6 %collective-permute-done.1.g2 = bf16[256,128]{1,0:T(8,128)(2,1)S(1)} collective-permute-done((bf16[256,128]{1,0:T(8,128)(2,1)S(1)}, bf16[256,128]{1,0:T(8,128)(2,1)S(1)}, u32[]{:S(2)}, u32[]{:S(2)}) %collective-permute-start.1) | collective-permute-done | bytes 65568 | tf_op jit(solution)/shard_map/ppermute | solution.py:28
  15.1 2.0 collective-permute-done.2.g3
  17.7 2.9 %collective-permute-start.3 = (bf16[256,128]{1,0:T(8,128)(2,1)S(1)}, bf16[256,128]{1,0:T(8,128)(2,1)S(1)}, u32[]{:S(2)}, u32[]{:S(2)}) collective-permute-start(bf16[256,128]{1,0:T(8,128)(2,1)S(1)} %get-tuple-element.51), channel_id=1, source_target_pairs={{0,1},{1,0},{2,3},{3,2},{4,5},{5,4},{6,7},{7,6},{8,9},{9,8},{10,11... | collective-permute-start | bytes 196616 | tf_op jit(solution)/shard_map/ppermute | solution.py:28
  20.6 1.7 collective-permute-done.3.b_ref
  22.9 5.6 %collective-permute-start.4 = (bf16[256,128]{1,0:T(8,128)(2,1)S(1)}, bf16[256,128]{1,0:T(8,128)(2,1)S(1)}, u32[]{:S(2)}, u32[]{:S(2)}) collective-permute-start(bf16[256,128]{1,0:T(8,128)(2,1)S(1)} %get-tuple-element.53), channel_id=1, source_target_pairs={{0,3},{1,2},{2,1},{3,0},{4,7},{5,6},{6,5},{7,4},{8,11},{9,10},{10,... | collective-permute-start | bytes 196616 | tf_op jit(solution)/shard_map/ppermute | solution.py:28
  28.4 1.8 collective-permute-done.4.b_ref
  32.4 1.9 collective-permute-start.5
  34.3 1.8 collective-permute-done.7.r3
  36.6 1.5 gradient_sent.3
  38.2 5.7 %collective-permute-start.8 = (bf16[128,1536]{1,0:T(8,128)(2,1)S(1)}, bf16[128,1536]{1,0:T(8,128)(2,1)S(1)}, u32[]{:S(2)}, u32[]{:S(2)}) collective-permute-start(bf16[128,1536]{1,0:T(8,128)(2,1)S(1)} %gradient_sent.3), channel_id=1, source_target_pairs={{0,16},{16,0},{32,48},{48,32},{64,80},{80,64},{96,112},{112,96},{1... | collective-permute-start | bytes 1179656 | tf_op jit(solution)/shard_map/ppermute | solution.py:28
  43.8 1.5 gradient_kept.3.kept
  47.4 2.6 %collective-permute-start.10 = (bf16[128,384]{1,0:T(8,128)(2,1)S(1)}, bf16[128,384]{1,0:T(8,128)(2,1)S(1)}, u32[]{:S(2)}, u32[]{:S(2)}) collective-permute-start(bf16[128,384]{1,0:T(8,128)(2,1)S(1)} %get-tuple-element.56), channel_id=1, source_target_pairs={{0,128},{16,144},{32,160},{48,176},{64,192},{80,208},{96,224},{112... | collective-permute-start | bytes 294920 | tf_op jit(solution)/shard_map/ppermute | solution.py:28
  50.4 4.6 %collective-permute-done.10.g2 = bf16[128,384]{1,0:T(8,128)(2,1)S(1)} collective-permute-done((bf16[128,384]{1,0:T(8,128)(2,1)S(1)}, bf16[128,384]{1,0:T(8,128)(2,1)S(1)}, u32[]{:S(2)}, u32[]{:S(2)}) %collective-permute-start.10) | collective-permute-done | bytes 98336 | tf_op jit(solution)/shard_map/ppermute | solution.py:28
  54.9 2.6 %collective-permute-done.11.g3 = bf16[128,384]{1,0:T(8,128)(2,1)S(1)} collective-permute-done((bf16[128,384]{1,0:T(8,128)(2,1)S(1)}, bf16[128,384]{1,0:T(8,128)(2,1)S(1)}, u32[]{:S(2)}, u32[]{:S(2)}) %collective-permute-start.11) | collective-permute-done | bytes 98336 | tf_op jit(solution)/shard_map/ppermute | solution.py:28
  58.1 1.9 collective-permute-start.12
  60.0 2.7 %collective-permute-done.12.got = bf16[128,384]{1,0:T(8,128)(2,1)S(1)} collective-permute-done((bf16[128,384]{1,0:T(8,128)(2,1)S(1)}, bf16[128,384]{1,0:T(8,128)(2,1)S(1)}, u32[]{:S(2)}, u32[]{:S(2)}) %collective-permute-start.12) | collective-permute-done | bytes 98336 | tf_op jit(solution)/shard_map/ppermute | solution.py:28
  63.6 3.1 %collective-permute-start.13 = (bf16[128,384]{1,0:T(8,128)(2,1)S(1)}, bf16[128,384]{1,0:T(8,128)(2,1)S(1)}, u32[]{:S(2)}, u32[]{:S(2)}) collective-permute-start(bf16[128,384]{1,0:T(8,128)(2,1)S(1)} %get-tuple-element.59.w0.a_ref), channel_id=1, source_target_pairs={{0,64},{16,80},{32,96},{48,112},{64,0},{80,16},{96,32},{112,48},{1... | collective-permute-start | bytes 294920 | tf_op jit(solution)/shard_map/ppermute | solution.py:28
  66.7 3.5 %collective-permute-done.15.w3.b_ref = bf16[128,384]{1,0:T(8,128)(2,1)S(1)} collective-permute-done((bf16[128,384]{1,0:T(8,128)(2,1)S(1)}, bf16[128,384]{1,0:T(8,128)(2,1)S(1)}, u32[]{:S(2)}, u32[]{:S(2)}) %collective-permute-start.15) | collective-permute-done | bytes 98336 | tf_op jit(solution)/shard_map/ppermute | solution.py:28
  70.8 1.8 collective-permute-start.16
  73.5 2.1 own_half.2.acc_ref
  75.6 2.1 %other_half.2 = (f32[256,128]{1,0:T(8,128)S(1)}, bf16[256,128]{1,0:T(8,128)(2,1)S(1)}, bf16[256,128]{1,0:T(8,128)(2,1)S(1)}, bf16[256,128]{1,0:T(8,128)(2,1)S(1)}) custom-call(s32[4]{0:T(128)S(1)} %pad_add_fusion.place, bf16[1024,3072]{1,0:T(8,128)(2,1)S(1)} %copy-done.1, f32[1024,128]{1,0:T(8,128)S(1)} %own_half.2.acc_ref, ...), custom_call_target="tpu_custom_call" | custom-call | flops 402653184 | bytes 7536640 | tf_op jit(solution)/shard_map/other_half/pallas_call | solution.py:38
  78.8 1.8 collective-permute-start.19
  81.6 2.3 %collective-permute-done.19.g2 = bf16[256,128]{1,0:T(8,128)(2,1)S(1)} collective-permute-done((bf16[256,128]{1,0:T(8,128)(2,1)S(1)}, bf16[256,128]{1,0:T(8,128)(2,1)S(1)}, u32[]{:S(2)}, u32[]{:S(2)}) %collective-permute-start.19) | collective-permute-done | bytes 65568 | tf_op jit(solution)/shard_map/ppermute | solution.py:28
  86.0 1.9 collective-permute-start.21
  87.9 2.2 %collective-permute-done.21.b_ref = bf16[256,128]{1,0:T(8,128)(2,1)S(1)} collective-permute-done((bf16[256,128]{1,0:T(8,128)(2,1)S(1)}, bf16[256,128]{1,0:T(8,128)(2,1)S(1)}, u32[]{:S(2)}, u32[]{:S(2)}) %collective-permute-start.21) | collective-permute-done | bytes 65568 | tf_op jit(solution)/shard_map/ppermute | solution.py:28
  90.6 3.2 %collective-permute-start.22 = (bf16[256,128]{1,0:T(8,128)(2,1)S(1)}, bf16[256,128]{1,0:T(8,128)(2,1)S(1)}, u32[]{:S(2)}, u32[]{:S(2)}) collective-permute-start(bf16[256,128]{1,0:T(8,128)(2,1)S(1)} %get-tuple-element.67), channel_id=1, source_target_pairs={{0,3},{1,2},{2,1},{3,0},{4,7},{5,6},{6,5},{7,4},{8,11},{9,10},{10,... | collective-permute-start | bytes 196616 | tf_op jit(solution)/shard_map/ppermute | solution.py:28
  93.8 2.8 %collective-permute-done.22.b_ref = bf16[256,128]{1,0:T(8,128)(2,1)S(1)} collective-permute-done((bf16[256,128]{1,0:T(8,128)(2,1)S(1)}, bf16[256,128]{1,0:T(8,128)(2,1)S(1)}, u32[]{:S(2)}, u32[]{:S(2)}) %collective-permute-start.22) | collective-permute-done | bytes 65568 | tf_op jit(solution)/shard_map/ppermute | solution.py:28
  98.3 2.3 %collective-permute-start.23 = (bf16[128,256]{1,0:T(8,128)(2,1)S(1)}, bf16[128,256]{1,0:T(8,128)(2,1)S(1)}, u32[]{:S(2)}, u32[]{:S(2)}) collective-permute-start(bf16[128,256]{1,0:T(8,128)(2,1)S(1)} %residual.4.r0), channel_id=1, source_target_pairs={{0,4},{1,5},{2,6},{3,7},{4,0},{5,1},{6,2},{7,3},{8,12},{9,13},{10,... | collective-permute-start | bytes 196616 | tf_op jit(solution)/shard_map/ppermute | solution.py:28
  103.0 1.5 gradient_sent.4
  104.5 5.0 %collective-permute-start.26 = (bf16[128,1536]{1,0:T(8,128)(2,1)S(1)}, bf16[128,1536]{1,0:T(8,128)(2,1)S(1)}, u32[]{:S(2)}, u32[]{:S(2)}) collective-permute-start(bf16[128,1536]{1,0:T(8,128)(2,1)S(1)} %gradient_sent.4), channel_id=1, source_target_pairs={{0,16},{16,0},{32,48},{48,32},{64,80},{80,64},{96,112},{112,96},{1... | collective-permute-start | bytes 1179656 | tf_op jit(solution)/shard_map/ppermute | solution.py:28
  109.5 1.5 gradient_kept.4.kept
  111.8 2.0 collective-permute-start.28
  113.8 1.9 collective-permute-start.29
  116.1 2.6 %collective-permute-done.28.g2 = bf16[128,384]{1,0:T(8,128)(2,1)S(1)} collective-permute-done((bf16[128,384]{1,0:T(8,128)(2,1)S(1)}, bf16[128,384]{1,0:T(8,128)(2,1)S(1)}, u32[]{:S(2)}, u32[]{:S(2)}) %collective-permute-start.28) | collective-permute-done | bytes 98336 | tf_op jit(solution)/shard_map/ppermute | solution.py:28
  118.7 2.6 %collective-permute-done.29.g3 = bf16[128,384]{1,0:T(8,128)(2,1)S(1)} collective-permute-done((bf16[128,384]{1,0:T(8,128)(2,1)S(1)}, bf16[128,384]{1,0:T(8,128)(2,1)S(1)}, u32[]{:S(2)}, u32[]{:S(2)}) %collective-permute-start.29) | collective-permute-done | bytes 98336 | tf_op jit(solution)/shard_map/ppermute | solution.py:28
  121.9 1.8 collective-permute-start.30
  123.7 2.7 %collective-permute-done.30.got = bf16[128,384]{1,0:T(8,128)(2,1)S(1)} collective-permute-done((bf16[128,384]{1,0:T(8,128)(2,1)S(1)}, bf16[128,384]{1,0:T(8,128)(2,1)S(1)}, u32[]{:S(2)}, u32[]{:S(2)}) %collective-permute-start.30) | collective-permute-done | bytes 98336 | tf_op jit(solution)/shard_map/ppermute | solution.py:28
  127.1 2.0 collective-permute-start.33
  132.4 3.3 %collective-permute-start.34 = (bf16[128,768]{1,0:T(8,128)(2,1)S(1)}, bf16[128,768]{1,0:T(8,128)(2,1)S(1)}, u32[]{:S(2)}, u32[]{:S(2)}) collective-permute-start(bf16[128,768]{1,0:T(8,128)(2,1)S(1)} %pair.8), channel_id=1, source_target_pairs={{0,16},{16,0},{32,48},{48,32},{64,80},{80,64},{96,112},{112,96},{1... | collective-permute-start | bytes 589832 | tf_op jit(solution)/shard_map/ppermute | solution.py:28
  137.5 2.1 own_half.3.acc_ref
  139.6 2.1 %other_half.3 = (f32[256,128]{1,0:T(8,128)S(1)}, bf16[256,128]{1,0:T(8,128)(2,1)S(1)}, bf16[256,128]{1,0:T(8,128)(2,1)S(1)}, bf16[256,128]{1,0:T(8,128)(2,1)S(1)}) custom-call(s32[4]{0:T(128)S(1)} %pad_add_fusion.place, bf16[1024,3072]{1,0:T(8,128)(2,1)S(1)} %copy-done.1, f32[1024,128]{1,0:T(8,128)S(1)} %own_half.3.acc_ref, ...), custom_call_target="tpu_custom_call" | custom-call | flops 402653184 | bytes 7536640 | tf_op jit(solution)/shard_map/other_half/pallas_call | solution.py:38
  143.1 1.8 collective-permute-start.37
  145.9 2.6 %collective-permute-done.37.g2 = bf16[256,128]{1,0:T(8,128)(2,1)S(1)} collective-permute-done((bf16[256,128]{1,0:T(8,128)(2,1)S(1)}, bf16[256,128]{1,0:T(8,128)(2,1)S(1)}, u32[]{:S(2)}, u32[]{:S(2)}) %collective-permute-start.37) | collective-permute-done | bytes 65568 | tf_op jit(solution)/shard_map/ppermute | solution.py:28
  150.0 1.7 collective-permute-start.39
  151.7 2.4 %collective-permute-done.39.b_ref = bf16[256,128]{1,0:T(8,128)(2,1)S(1)} collective-permute-done((bf16[256,128]{1,0:T(8,128)(2,1)S(1)}, bf16[256,128]{1,0:T(8,128)(2,1)S(1)}, u32[]{:S(2)}, u32[]{:S(2)}) %collective-permute-start.39) | collective-permute-done | bytes 65568 | tf_op jit(solution)/shard_map/ppermute | solution.py:28
  154.6 3.3 %collective-permute-start.40 = (bf16[256,128]{1,0:T(8,128)(2,1)S(1)}, bf16[256,128]{1,0:T(8,128)(2,1)S(1)}, u32[]{:S(2)}, u32[]{:S(2)}) collective-permute-start(bf16[256,128]{1,0:T(8,128)(2,1)S(1)} %get-tuple-element.81), channel_id=1, source_target_pairs={{0,3},{1,2},{2,1},{3,0},{4,7},{5,6},{6,5},{7,4},{8,11},{9,10},{10,... | collective-permute-start | bytes 196616 | tf_op jit(solution)/shard_map/ppermute | solution.py:28
  157.9 2.5 %collective-permute-done.40.b_ref = bf16[256,128]{1,0:T(8,128)(2,1)S(1)} collective-permute-done((bf16[256,128]{1,0:T(8,128)(2,1)S(1)}, bf16[256,128]{1,0:T(8,128)(2,1)S(1)}, u32[]{:S(2)}, u32[]{:S(2)}) %collective-permute-start.40) | collective-permute-done | bytes 65568 | tf_op jit(solution)/shard_map/ppermute | solution.py:28
  163.2 1.7 collective-permute-start.41
  168.8 5.0 %collective-permute-start.44 = (bf16[128,1536]{1,0:T(8,128)(2,1)S(1)}, bf16[128,1536]{1,0:T(8,128)(2,1)S(1)}, u32[]{:S(2)}, u32[]{:S(2)}) collective-permute-start(bf16[128,1536]{1,0:T(8,128)(2,1)S(1)} %gradient_sent.5), channel_id=1, source_target_pairs={{0,16},{16,0},{32,48},{48,32},{64,80},{80,64},{96,112},{112,96},{1... | collective-permute-start | bytes 1179656 | tf_op jit(solution)/shard_map/ppermute | solution.py:28
  173.8 1.5 gradient_kept.5.kept
  176.1 2.5 %collective-permute-start.46 = (bf16[128,384]{1,0:T(8,128)(2,1)S(1)}, bf16[128,384]{1,0:T(8,128)(2,1)S(1)}, u32[]{:S(2)}, u32[]{:S(2)}) collective-permute-start(bf16[128,384]{1,0:T(8,128)(2,1)S(1)} %get-tuple-element.85), channel_id=1, source_target_pairs={{0,128},{16,144},{32,160},{48,176},{64,192},{80,208},{96,224},{112... | collective-permute-start | bytes 294920 | tf_op jit(solution)/shard_map/ppermute | solution.py:28
  180.3 3.2 %collective-permute-done.46.g2 = bf16[128,384]{1,0:T(8,128)(2,1)S(1)} collective-permute-done((bf16[128,384]{1,0:T(8,128)(2,1)S(1)}, bf16[128,384]{1,0:T(8,128)(2,1)S(1)}, u32[]{:S(2)}, u32[]{:S(2)}) %collective-permute-start.46) | collective-permute-done | bytes 98336 | tf_op jit(solution)/shard_map/ppermute | solution.py:28
  183.5 2.6 %collective-permute-done.47.g3 = bf16[128,384]{1,0:T(8,128)(2,1)S(1)} collective-permute-done((bf16[128,384]{1,0:T(8,128)(2,1)S(1)}, bf16[128,384]{1,0:T(8,128)(2,1)S(1)}, u32[]{:S(2)}, u32[]{:S(2)}) %collective-permute-start.47) | collective-permute-done | bytes 98336 | tf_op jit(solution)/shard_map/ppermute | solution.py:28
  186.7 1.9 collective-permute-start.48
  188.5 2.7 %collective-permute-done.48.got = bf16[128,384]{1,0:T(8,128)(2,1)S(1)} collective-permute-done((bf16[128,384]{1,0:T(8,128)(2,1)S(1)}, bf16[128,384]{1,0:T(8,128)(2,1)S(1)}, u32[]{:S(2)}, u32[]{:S(2)}) %collective-permute-start.48) | collective-permute-done | bytes 98336 | tf_op jit(solution)/shard_map/ppermute | solution.py:28
  192.6 1.9 collective-permute-start.51
  195.8 1.7 collective-permute-done.52.b_ref.refs_2_
  199.0 2.1 %collective-permute-start.53 = (bf16[128,768]{1,0:T(8,128)(2,1)S(1)}, bf16[128,768]{1,0:T(8,128)(2,1)S(1)}, u32[]{:S(2)}, u32[]{:S(2)}) collective-permute-start(bf16[128,768]{1,0:T(8,128)(2,1)S(1)} %pair.11), channel_id=1, source_target_pairs={{0,16},{16,0},{32,48},{48,32},{64,80},{80,64},{96,112},{112,96},{1... | collective-permute-start | bytes 589832 | tf_op jit(solution)/shard_map/ppermute | solution.py:28
  202.6 1.5 place_near.1.refs_2_
  204.1 1.6 place_far.1
  (90 shorter events, 46.3 us)
Async XLA Ops:
  0.7 2.8 %copy-start = (bf16[1024,3072]{1,0:T(8,128)(2,1)S(1)}, bf16[1024,3072]{1,0:T(8,128)(2,1)}, u32[]{:S(2)}) copy-start(bf16[1024,3072]{1,0:T(8,128)(2,1)} %s_ref.21) | copy-start | bytes 18874372
  3.5 1.4 copy-start.3
  4.9 25.4 %copy-start.2 = (f32[1024,128]{1,0:T(8,128)S(1)}, f32[1024,128]{1,0:T(8,128)}, u32[]{:S(2)}) copy-start(f32[1024,128]{1,0:T(8,128)} %t_ref.5) | copy-start | bytes 1572868
  4.9 31.7 %copy-start.1 = (bf16[1024,3072]{1,0:T(8,128)(2,1)S(1)}, bf16[1024,3072]{1,0:T(8,128)(2,1)}, u32[]{:S(2)}) copy-start(bf16[1024,3072]{1,0:T(8,128)(2,1)} %s_ref.21) | copy-start | bytes 18874372
  7.9 4.6 %collective-permute-start = (bf16[256,128]{1,0:T(8,128)(2,1)S(1)}, bf16[256,128]{1,0:T(8,128)(2,1)S(1)}, u32[]{:S(2)}, u32[]{:S(2)}) collective-permute-start(bf16[256,128]{1,0:T(8,128)(2,1)S(1)} %get-tuple-element.47), channel_id=1, source_target_pairs={{0,4},{1,5},{2,6},{3,7},{4,0},{5,1},{6,2},{7,3},{8,12},{9,13},{10,... | collective-permute-start | bytes 196616 | tf_op jit(solution)/shard_map/ppermute | solution.py:28
  10.1 5.0 %collective-permute-start.1 = (bf16[256,128]{1,0:T(8,128)(2,1)S(1)}, bf16[256,128]{1,0:T(8,128)(2,1)S(1)}, u32[]{:S(2)}, u32[]{:S(2)}) collective-permute-start(bf16[256,128]{1,0:T(8,128)(2,1)S(1)} %get-tuple-element.48), channel_id=1, source_target_pairs={{0,8},{1,9},{2,10},{3,11},{4,12},{5,13},{6,14},{7,15},{8,0},{9,1},... | collective-permute-start | bytes 196616 | tf_op jit(solution)/shard_map/ppermute | solution.py:28
  12.5 4.6 %collective-permute-start.2 = (bf16[256,128]{1,0:T(8,128)(2,1)S(1)}, bf16[256,128]{1,0:T(8,128)(2,1)S(1)}, u32[]{:S(2)}, u32[]{:S(2)}) collective-permute-start(bf16[256,128]{1,0:T(8,128)(2,1)S(1)} %get-tuple-element.49), channel_id=1, source_target_pairs={{0,12},{1,13},{2,14},{3,15},{4,8},{5,9},{6,10},{7,11},{8,4},{9,5},... | collective-permute-start | bytes 196616 | tf_op jit(solution)/shard_map/ppermute | solution.py:28
  17.7 4.6 %collective-permute-start.3 = (bf16[256,128]{1,0:T(8,128)(2,1)S(1)}, bf16[256,128]{1,0:T(8,128)(2,1)S(1)}, u32[]{:S(2)}, u32[]{:S(2)}) collective-permute-start(bf16[256,128]{1,0:T(8,128)(2,1)S(1)} %get-tuple-element.51), channel_id=1, source_target_pairs={{0,1},{1,0},{2,3},{3,2},{4,5},{5,4},{6,7},{7,6},{8,9},{9,8},{10,11... | collective-permute-start | bytes 196616 | tf_op jit(solution)/shard_map/ppermute | solution.py:28
  22.9 7.4 %collective-permute-start.4 = (bf16[256,128]{1,0:T(8,128)(2,1)S(1)}, bf16[256,128]{1,0:T(8,128)(2,1)S(1)}, u32[]{:S(2)}, u32[]{:S(2)}) collective-permute-start(bf16[256,128]{1,0:T(8,128)(2,1)S(1)} %get-tuple-element.53), channel_id=1, source_target_pairs={{0,3},{1,2},{2,1},{3,0},{4,7},{5,6},{6,5},{7,4},{8,11},{9,10},{10,... | collective-permute-start | bytes 196616 | tf_op jit(solution)/shard_map/ppermute | solution.py:28
  30.9 5.1 %collective-permute-start.7 = (bf16[128,256]{1,0:T(8,128)(2,1)S(1)}, bf16[128,256]{1,0:T(8,128)(2,1)S(1)}, u32[]{:S(2)}, u32[]{:S(2)}) collective-permute-start(bf16[128,256]{1,0:T(8,128)(2,1)S(1)} %residual.3.r0), channel_id=1, source_target_pairs={{0,12},{1,13},{2,14},{3,15},{4,8},{5,9},{6,10},{7,11},{8,4},{9,5},... | collective-permute-start | bytes 196616 | tf_op jit(solution)/shard_map/ppermute | solution.py:28
  31.2 4.8 %collective-permute-start.6 = (bf16[128,256]{1,0:T(8,128)(2,1)S(1)}, bf16[128,256]{1,0:T(8,128)(2,1)S(1)}, u32[]{:S(2)}, u32[]{:S(2)}) collective-permute-start(bf16[128,256]{1,0:T(8,128)(2,1)S(1)} %residual.3.r0), channel_id=1, source_target_pairs={{0,8},{1,9},{2,10},{3,11},{4,12},{5,13},{6,14},{7,15},{8,0},{9,1},... | collective-permute-start | bytes 196616 | tf_op jit(solution)/shard_map/ppermute | solution.py:28
  32.4 4.2 %collective-permute-start.5 = (bf16[128,256]{1,0:T(8,128)(2,1)S(1)}, bf16[128,256]{1,0:T(8,128)(2,1)S(1)}, u32[]{:S(2)}, u32[]{:S(2)}) collective-permute-start(bf16[128,256]{1,0:T(8,128)(2,1)S(1)} %residual.3.r0), channel_id=1, source_target_pairs={{0,4},{1,5},{2,6},{3,7},{4,0},{5,1},{6,2},{7,3},{8,12},{9,13},{10,... | collective-permute-start | bytes 196616 | tf_op jit(solution)/shard_map/ppermute | solution.py:28
  38.2 7.2 %collective-permute-start.8 = (bf16[128,1536]{1,0:T(8,128)(2,1)S(1)}, bf16[128,1536]{1,0:T(8,128)(2,1)S(1)}, u32[]{:S(2)}, u32[]{:S(2)}) collective-permute-start(bf16[128,1536]{1,0:T(8,128)(2,1)S(1)} %gradient_sent.3), channel_id=1, source_target_pairs={{0,16},{16,0},{32,48},{48,32},{64,80},{80,64},{96,112},{112,96},{1... | collective-permute-start | bytes 1179656 | tf_op jit(solution)/shard_map/ppermute | solution.py:28
  46.0 4.3 %collective-permute-start.9 = (bf16[128,384]{1,0:T(8,128)(2,1)S(1)}, bf16[128,384]{1,0:T(8,128)(2,1)S(1)}, u32[]{:S(2)}, u32[]{:S(2)}) collective-permute-start(bf16[128,384]{1,0:T(8,128)(2,1)S(1)} %get-tuple-element.55), channel_id=1, source_target_pairs={{0,64},{16,80},{32,96},{48,112},{64,0},{80,16},{96,32},{112,48},{1... | collective-permute-start | bytes 294920 | tf_op jit(solution)/shard_map/ppermute | solution.py:28
  47.4 7.5 %collective-permute-start.10 = (bf16[128,384]{1,0:T(8,128)(2,1)S(1)}, bf16[128,384]{1,0:T(8,128)(2,1)S(1)}, u32[]{:S(2)}, u32[]{:S(2)}) collective-permute-start(bf16[128,384]{1,0:T(8,128)(2,1)S(1)} %get-tuple-element.56), channel_id=1, source_target_pairs={{0,128},{16,144},{32,160},{48,176},{64,192},{80,208},{96,224},{112... | collective-permute-start | bytes 294920 | tf_op jit(solution)/shard_map/ppermute | solution.py:28
  50.0 7.5 %collective-permute-start.11 = (bf16[128,384]{1,0:T(8,128)(2,1)S(1)}, bf16[128,384]{1,0:T(8,128)(2,1)S(1)}, u32[]{:S(2)}, u32[]{:S(2)}) collective-permute-start(bf16[128,384]{1,0:T(8,128)(2,1)S(1)} %get-tuple-element.57), channel_id=1, source_target_pairs={{0,192},{16,208},{32,224},{48,240},{64,128},{80,144},{96,160},{112... | collective-permute-start | bytes 294920 | tf_op jit(solution)/shard_map/ppermute | solution.py:28
  58.1 4.7 %collective-permute-start.12 = (bf16[128,384]{1,0:T(8,128)(2,1)S(1)}, bf16[128,384]{1,0:T(8,128)(2,1)S(1)}, u32[]{:S(2)}, u32[]{:S(2)}) collective-permute-start(bf16[128,384]{1,0:T(8,128)(2,1)S(1)} %half.3.kept), channel_id=1, source_target_pairs={{0,32},{16,48},{32,0},{48,16},{64,96},{80,112},{96,64},{112,80},{1... | collective-permute-start | bytes 294920 | tf_op jit(solution)/shard_map/ppermute | solution.py:28
  63.4 6.9 %collective-permute-start.15 = (bf16[128,384]{1,0:T(8,128)(2,1)S(1)}, bf16[128,384]{1,0:T(8,128)(2,1)S(1)}, u32[]{:S(2)}, u32[]{:S(2)}) collective-permute-start(bf16[128,384]{1,0:T(8,128)(2,1)S(1)} %get-tuple-element.59.w0.a_ref), channel_id=1, source_target_pairs={{0,192},{16,208},{32,224},{48,240},{64,128},{80,144},{96,160},{112... | collective-permute-start | bytes 294920 | tf_op jit(solution)/shard_map/ppermute | solution.py:28
  63.6 9.0 %collective-permute-start.14 = (bf16[128,384]{1,0:T(8,128)(2,1)S(1)}, bf16[128,384]{1,0:T(8,128)(2,1)S(1)}, u32[]{:S(2)}, u32[]{:S(2)}) collective-permute-start(bf16[128,384]{1,0:T(8,128)(2,1)S(1)} %get-tuple-element.59.w0.a_ref), channel_id=1, source_target_pairs={{0,128},{16,144},{32,160},{48,176},{64,192},{80,208},{96,224},{112... | collective-permute-start | bytes 294920 | tf_op jit(solution)/shard_map/ppermute | solution.py:28
  63.6 9.0 %collective-permute-start.13 = (bf16[128,384]{1,0:T(8,128)(2,1)S(1)}, bf16[128,384]{1,0:T(8,128)(2,1)S(1)}, u32[]{:S(2)}, u32[]{:S(2)}) collective-permute-start(bf16[128,384]{1,0:T(8,128)(2,1)S(1)} %get-tuple-element.59.w0.a_ref), channel_id=1, source_target_pairs={{0,64},{16,80},{32,96},{48,112},{64,0},{80,16},{96,32},{112,48},{1... | collective-permute-start | bytes 294920 | tf_op jit(solution)/shard_map/ppermute | solution.py:28
  70.8 4.8 %collective-permute-start.16 = (bf16[128,768]{1,0:T(8,128)(2,1)S(1)}, bf16[128,768]{1,0:T(8,128)(2,1)S(1)}, u32[]{:S(2)}, u32[]{:S(2)}) collective-permute-start(bf16[128,768]{1,0:T(8,128)(2,1)S(1)} %pair.6), channel_id=1, source_target_pairs={{0,16},{16,0},{32,48},{48,32},{64,80},{80,64},{96,112},{112,96},{1... | collective-permute-start | bytes 589832 | tf_op jit(solution)/shard_map/ppermute | solution.py:28
  73.2 2.4 %collective-permute-start.17 = (bf16[128,768]{1,0:T(8,128)(2,1)S(1)}, bf16[128,768]{1,0:T(8,128)(2,1)S(1)}, u32[]{:S(2)}, u32[]{:S(2)}) collective-permute-start(bf16[128,768]{1,0:T(8,128)(2,1)S(1)} %pair.7), channel_id=1, source_target_pairs={{0,16},{16,0},{32,48},{48,32},{64,80},{80,64},{96,112},{112,96},{1... | collective-permute-start | bytes 589832 | tf_op jit(solution)/shard_map/ppermute | solution.py:28
  77.7 3.9 %collective-permute-start.18 = (bf16[256,128]{1,0:T(8,128)(2,1)S(1)}, bf16[256,128]{1,0:T(8,128)(2,1)S(1)}, u32[]{:S(2)}, u32[]{:S(2)}) collective-permute-start(bf16[256,128]{1,0:T(8,128)(2,1)S(1)} %get-tuple-element.61), channel_id=1, source_target_pairs={{0,4},{1,5},{2,6},{3,7},{4,0},{5,1},{6,2},{7,3},{8,12},{9,13},{10,... | collective-permute-start | bytes 196616 | tf_op jit(solution)/shard_map/ppermute | solution.py:28
  78.8 5.1 %collective-permute-start.19 = (bf16[256,128]{1,0:T(8,128)(2,1)S(1)}, bf16[256,128]{1,0:T(8,128)(2,1)S(1)}, u32[]{:S(2)}, u32[]{:S(2)}) collective-permute-start(bf16[256,128]{1,0:T(8,128)(2,1)S(1)} %get-tuple-element.62), channel_id=1, source_target_pairs={{0,8},{1,9},{2,10},{3,11},{4,12},{5,13},{6,14},{7,15},{8,0},{9,1},... | collective-permute-start | bytes 196616 | tf_op jit(solution)/shard_map/ppermute | solution.py:28
  80.6 4.7 %collective-permute-start.20 = (bf16[256,128]{1,0:T(8,128)(2,1)S(1)}, bf16[256,128]{1,0:T(8,128)(2,1)S(1)}, u32[]{:S(2)}, u32[]{:S(2)}) collective-permute-start(bf16[256,128]{1,0:T(8,128)(2,1)S(1)} %get-tuple-element.63), channel_id=1, source_target_pairs={{0,12},{1,13},{2,14},{3,15},{4,8},{5,9},{6,10},{7,11},{8,4},{9,5},... | collective-permute-start | bytes 196616 | tf_op jit(solution)/shard_map/ppermute | solution.py:28
  86.0 4.1 %collective-permute-start.21 = (bf16[256,128]{1,0:T(8,128)(2,1)S(1)}, bf16[256,128]{1,0:T(8,128)(2,1)S(1)}, u32[]{:S(2)}, u32[]{:S(2)}) collective-permute-start(bf16[256,128]{1,0:T(8,128)(2,1)S(1)} %get-tuple-element.65), channel_id=1, source_target_pairs={{0,1},{1,0},{2,3},{3,2},{4,5},{5,4},{6,7},{7,6},{8,9},{9,8},{10,11... | collective-permute-start | bytes 196616 | tf_op jit(solution)/shard_map/ppermute | solution.py:28
  90.6 6.0 %collective-permute-start.22 = (bf16[256,128]{1,0:T(8,128)(2,1)S(1)}, bf16[256,128]{1,0:T(8,128)(2,1)S(1)}, u32[]{:S(2)}, u32[]{:S(2)}) collective-permute-start(bf16[256,128]{1,0:T(8,128)(2,1)S(1)} %get-tuple-element.67), channel_id=1, source_target_pairs={{0,3},{1,2},{2,1},{3,0},{4,7},{5,6},{6,5},{7,4},{8,11},{9,10},{10,... | collective-permute-start | bytes 196616 | tf_op jit(solution)/shard_map/ppermute | solution.py:28
  97.3 4.4 %collective-permute-start.25 = (bf16[128,256]{1,0:T(8,128)(2,1)S(1)}, bf16[128,256]{1,0:T(8,128)(2,1)S(1)}, u32[]{:S(2)}, u32[]{:S(2)}) collective-permute-start(bf16[128,256]{1,0:T(8,128)(2,1)S(1)} %residual.4.r0), channel_id=1, source_target_pairs={{0,12},{1,13},{2,14},{3,15},{4,8},{5,9},{6,10},{7,11},{8,4},{9,5},... | collective-permute-start | bytes 196616 | tf_op jit(solution)/shard_map/ppermute | solution.py:28
  98.3 4.6 %collective-permute-start.24 = (bf16[128,256]{1,0:T(8,128)(2,1)S(1)}, bf16[128,256]{1,0:T(8,128)(2,1)S(1)}, u32[]{:S(2)}, u32[]{:S(2)}) collective-permute-start(bf16[128,256]{1,0:T(8,128)(2,1)S(1)} %residual.4.r0), channel_id=1, source_target_pairs={{0,8},{1,9},{2,10},{3,11},{4,12},{5,13},{6,14},{7,15},{8,0},{9,1},... | collective-permute-start | bytes 196616 | tf_op jit(solution)/shard_map/ppermute | solution.py:28
  98.3 4.6 %collective-permute-start.23 = (bf16[128,256]{1,0:T(8,128)(2,1)S(1)}, bf16[128,256]{1,0:T(8,128)(2,1)S(1)}, u32[]{:S(2)}, u32[]{:S(2)}) collective-permute-start(bf16[128,256]{1,0:T(8,128)(2,1)S(1)} %residual.4.r0), channel_id=1, source_target_pairs={{0,4},{1,5},{2,6},{3,7},{4,0},{5,1},{6,2},{7,3},{8,12},{9,13},{10,... | collective-permute-start | bytes 196616 | tf_op jit(solution)/shard_map/ppermute | solution.py:28
  104.5 6.6 %collective-permute-start.26 = (bf16[128,1536]{1,0:T(8,128)(2,1)S(1)}, bf16[128,1536]{1,0:T(8,128)(2,1)S(1)}, u32[]{:S(2)}, u32[]{:S(2)}) collective-permute-start(bf16[128,1536]{1,0:T(8,128)(2,1)S(1)} %gradient_sent.4), channel_id=1, source_target_pairs={{0,16},{16,0},{32,48},{48,32},{64,80},{80,64},{96,112},{112,96},{1... | collective-permute-start | bytes 1179656 | tf_op jit(solution)/shard_map/ppermute | solution.py:28
  111.7 4.3 %collective-permute-start.27 = (bf16[128,384]{1,0:T(8,128)(2,1)S(1)}, bf16[128,384]{1,0:T(8,128)(2,1)S(1)}, u32[]{:S(2)}, u32[]{:S(2)}) collective-permute-start(bf16[128,384]{1,0:T(8,128)(2,1)S(1)} %get-tuple-element.69), channel_id=1, source_target_pairs={{0,64},{16,80},{32,96},{48,112},{64,0},{80,16},{96,32},{112,48},{1... | collective-permute-start | bytes 294920 | tf_op jit(solution)/shard_map/ppermute | solution.py:28
  111.8 6.9 %collective-permute-start.28 = (bf16[128,384]{1,0:T(8,128)(2,1)S(1)}, bf16[128,384]{1,0:T(8,128)(2,1)S(1)}, u32[]{:S(2)}, u32[]{:S(2)}) collective-permute-start(bf16[128,384]{1,0:T(8,128)(2,1)S(1)} %get-tuple-element.70), channel_id=1, source_target_pairs={{0,128},{16,144},{32,160},{48,176},{64,192},{80,208},{96,224},{112... | collective-permute-start | bytes 294920 | tf_op jit(solution)/shard_map/ppermute | solution.py:28
  113.8 7.5 %collective-permute-start.29 = (bf16[128,384]{1,0:T(8,128)(2,1)S(1)}, bf16[128,384]{1,0:T(8,128)(2,1)S(1)}, u32[]{:S(2)}, u32[]{:S(2)}) collective-permute-start(bf16[128,384]{1,0:T(8,128)(2,1)S(1)} %get-tuple-element.71), channel_id=1, source_target_pairs={{0,192},{16,208},{32,224},{48,240},{64,128},{80,144},{96,160},{112... | collective-permute-start | bytes 294920 | tf_op jit(solution)/shard_map/ppermute | solution.py:28
  121.9 4.6 %collective-permute-start.30 = (bf16[128,384]{1,0:T(8,128)(2,1)S(1)}, bf16[128,384]{1,0:T(8,128)(2,1)S(1)}, u32[]{:S(2)}, u32[]{:S(2)}) collective-permute-start(bf16[128,384]{1,0:T(8,128)(2,1)S(1)} %half.4.kept), channel_id=1, source_target_pairs={{0,32},{16,48},{32,0},{48,16},{64,96},{80,112},{96,64},{112,80},{1... | collective-permute-start | bytes 294920 | tf_op jit(solution)/shard_map/ppermute | solution.py:28
  127.1 4.8 %collective-permute-start.33 = (bf16[128,384]{1,0:T(8,128)(2,1)S(1)}, bf16[128,384]{1,0:T(8,128)(2,1)S(1)}, u32[]{:S(2)}, u32[]{:S(2)}) collective-permute-start(bf16[128,384]{1,0:T(8,128)(2,1)S(1)} %get-tuple-element.73.w0.a_ref), channel_id=1, source_target_pairs={{0,192},{16,208},{32,224},{48,240},{64,128},{80,144},{96,160},{112... | collective-permute-start | bytes 294920 | tf_op jit(solution)/shard_map/ppermute | solution.py:28
  129.1 6.6 %collective-permute-start.32 = (bf16[128,384]{1,0:T(8,128)(2,1)S(1)}, bf16[128,384]{1,0:T(8,128)(2,1)S(1)}, u32[]{:S(2)}, u32[]{:S(2)}) collective-permute-start(bf16[128,384]{1,0:T(8,128)(2,1)S(1)} %get-tuple-element.73.w0.a_ref), channel_id=1, source_target_pairs={{0,128},{16,144},{32,160},{48,176},{64,192},{80,208},{96,224},{112... | collective-permute-start | bytes 294920 | tf_op jit(solution)/shard_map/ppermute | solution.py:28
  129.1 6.6 %collective-permute-start.31 = (bf16[128,384]{1,0:T(8,128)(2,1)S(1)}, bf16[128,384]{1,0:T(8,128)(2,1)S(1)}, u32[]{:S(2)}, u32[]{:S(2)}) collective-permute-start(bf16[128,384]{1,0:T(8,128)(2,1)S(1)} %get-tuple-element.73.w0.a_ref), channel_id=1, source_target_pairs={{0,64},{16,80},{32,96},{48,112},{64,0},{80,16},{96,32},{112,48},{1... | collective-permute-start | bytes 294920 | tf_op jit(solution)/shard_map/ppermute | solution.py:28
  132.4 7.2 %collective-permute-start.34 = (bf16[128,768]{1,0:T(8,128)(2,1)S(1)}, bf16[128,768]{1,0:T(8,128)(2,1)S(1)}, u32[]{:S(2)}, u32[]{:S(2)}) collective-permute-start(bf16[128,768]{1,0:T(8,128)(2,1)S(1)} %pair.8), channel_id=1, source_target_pairs={{0,16},{16,0},{32,48},{48,32},{64,80},{80,64},{96,112},{112,96},{1... | collective-permute-start | bytes 589832 | tf_op jit(solution)/shard_map/ppermute | solution.py:28
  136.3 3.3 %collective-permute-start.35 = (bf16[128,768]{1,0:T(8,128)(2,1)S(1)}, bf16[128,768]{1,0:T(8,128)(2,1)S(1)}, u32[]{:S(2)}, u32[]{:S(2)}) collective-permute-start(bf16[128,768]{1,0:T(8,128)(2,1)S(1)} %pair.9), channel_id=1, source_target_pairs={{0,16},{16,0},{32,48},{48,32},{64,80},{80,64},{96,112},{112,96},{1... | collective-permute-start | bytes 589832 | tf_op jit(solution)/shard_map/ppermute | solution.py:28
  141.7 4.2 %collective-permute-start.36 = (bf16[256,128]{1,0:T(8,128)(2,1)S(1)}, bf16[256,128]{1,0:T(8,128)(2,1)S(1)}, u32[]{:S(2)}, u32[]{:S(2)}) collective-permute-start(bf16[256,128]{1,0:T(8,128)(2,1)S(1)} %get-tuple-element.75), channel_id=1, source_target_pairs={{0,4},{1,5},{2,6},{3,7},{4,0},{5,1},{6,2},{7,3},{8,12},{9,13},{10,... | collective-permute-start | bytes 196616 | tf_op jit(solution)/shard_map/ppermute | solution.py:28
  143.1 5.5 %collective-permute-start.37 = (bf16[256,128]{1,0:T(8,128)(2,1)S(1)}, bf16[256,128]{1,0:T(8,128)(2,1)S(1)}, u32[]{:S(2)}, u32[]{:S(2)}) collective-permute-start(bf16[256,128]{1,0:T(8,128)(2,1)S(1)} %get-tuple-element.76), channel_id=1, source_target_pairs={{0,8},{1,9},{2,10},{3,11},{4,12},{5,13},{6,14},{7,15},{8,0},{9,1},... | collective-permute-start | bytes 196616 | tf_op jit(solution)/shard_map/ppermute | solution.py:28
  144.9 4.5 %collective-permute-start.38 = (bf16[256,128]{1,0:T(8,128)(2,1)S(1)}, bf16[256,128]{1,0:T(8,128)(2,1)S(1)}, u32[]{:S(2)}, u32[]{:S(2)}) collective-permute-start(bf16[256,128]{1,0:T(8,128)(2,1)S(1)} %get-tuple-element.77), channel_id=1, source_target_pairs={{0,12},{1,13},{2,14},{3,15},{4,8},{5,9},{6,10},{7,11},{8,4},{9,5},... | collective-permute-start | bytes 196616 | tf_op jit(solution)/shard_map/ppermute | solution.py:28
  150.0 4.1 %collective-permute-start.39 = (bf16[256,128]{1,0:T(8,128)(2,1)S(1)}, bf16[256,128]{1,0:T(8,128)(2,1)S(1)}, u32[]{:S(2)}, u32[]{:S(2)}) collective-permute-start(bf16[256,128]{1,0:T(8,128)(2,1)S(1)} %get-tuple-element.79), channel_id=1, source_target_pairs={{0,1},{1,0},{2,3},{3,2},{4,5},{5,4},{6,7},{7,6},{8,9},{9,8},{10,11... | collective-permute-start | bytes 196616 | tf_op jit(solution)/shard_map/ppermute | solution.py:28
  154.6 5.8 %collective-permute-start.40 = (bf16[256,128]{1,0:T(8,128)(2,1)S(1)}, bf16[256,128]{1,0:T(8,128)(2,1)S(1)}, u32[]{:S(2)}, u32[]{:S(2)}) collective-permute-start(bf16[256,128]{1,0:T(8,128)(2,1)S(1)} %get-tuple-element.81), channel_id=1, source_target_pairs={{0,3},{1,2},{2,1},{3,0},{4,7},{5,6},{6,5},{7,4},{8,11},{9,10},{10,... | collective-permute-start | bytes 196616 | tf_op jit(solution)/shard_map/ppermute | solution.py:28
  161.6 4.3 %collective-permute-start.43 = (bf16[128,256]{1,0:T(8,128)(2,1)S(1)}, bf16[128,256]{1,0:T(8,128)(2,1)S(1)}, u32[]{:S(2)}, u32[]{:S(2)}) collective-permute-start(bf16[128,256]{1,0:T(8,128)(2,1)S(1)} %get-tuple-element.82.r0), channel_id=1, source_target_pairs={{0,12},{1,13},{2,14},{3,15},{4,8},{5,9},{6,10},{7,11},{8,4},{9,5},... | collective-permute-start | bytes 196616 | tf_op jit(solution)/shard_map/ppermute | solution.py:28
  162.6 4.6 %collective-permute-start.42 = (bf16[128,256]{1,0:T(8,128)(2,1)S(1)}, bf16[128,256]{1,0:T(8,128)(2,1)S(1)}, u32[]{:S(2)}, u32[]{:S(2)}) collective-permute-start(bf16[128,256]{1,0:T(8,128)(2,1)S(1)} %get-tuple-element.82.r0), channel_id=1, source_target_pairs={{0,8},{1,9},{2,10},{3,11},{4,12},{5,13},{6,14},{7,15},{8,0},{9,1},... | collective-permute-start | bytes 196616 | tf_op jit(solution)/shard_map/ppermute | solution.py:28
  163.2 4.1 %collective-permute-start.41 = (bf16[128,256]{1,0:T(8,128)(2,1)S(1)}, bf16[128,256]{1,0:T(8,128)(2,1)S(1)}, u32[]{:S(2)}, u32[]{:S(2)}) collective-permute-start(bf16[128,256]{1,0:T(8,128)(2,1)S(1)} %get-tuple-element.82.r0), channel_id=1, source_target_pairs={{0,4},{1,5},{2,6},{3,7},{4,0},{5,1},{6,2},{7,3},{8,12},{9,13},{10,... | collective-permute-start | bytes 196616 | tf_op jit(solution)/shard_map/ppermute | solution.py:28
  168.8 6.5 %collective-permute-start.44 = (bf16[128,1536]{1,0:T(8,128)(2,1)S(1)}, bf16[128,1536]{1,0:T(8,128)(2,1)S(1)}, u32[]{:S(2)}, u32[]{:S(2)}) collective-permute-start(bf16[128,1536]{1,0:T(8,128)(2,1)S(1)} %gradient_sent.5), channel_id=1, source_target_pairs={{0,16},{16,0},{32,48},{48,32},{64,80},{80,64},{96,112},{112,96},{1... | collective-permute-start | bytes 1179656 | tf_op jit(solution)/shard_map/ppermute | solution.py:28
  176.0 4.3 %collective-permute-start.45 = (bf16[128,384]{1,0:T(8,128)(2,1)S(1)}, bf16[128,384]{1,0:T(8,128)(2,1)S(1)}, u32[]{:S(2)}, u32[]{:S(2)}) collective-permute-start(bf16[128,384]{1,0:T(8,128)(2,1)S(1)} %get-tuple-element.84), channel_id=1, source_target_pairs={{0,64},{16,80},{32,96},{48,112},{64,0},{80,16},{96,32},{112,48},{1... | collective-permute-start | bytes 294920 | tf_op jit(solution)/shard_map/ppermute | solution.py:28
  176.1 7.4 %collective-permute-start.46 = (bf16[128,384]{1,0:T(8,128)(2,1)S(1)}, bf16[128,384]{1,0:T(8,128)(2,1)S(1)}, u32[]{:S(2)}, u32[]{:S(2)}) collective-permute-start(bf16[128,384]{1,0:T(8,128)(2,1)S(1)} %get-tuple-element.85), channel_id=1, source_target_pairs={{0,128},{16,144},{32,160},{48,176},{64,192},{80,208},{96,224},{112... | collective-permute-start | bytes 294920 | tf_op jit(solution)/shard_map/ppermute | solution.py:28
  178.6 7.5 %collective-permute-start.47 = (bf16[128,384]{1,0:T(8,128)(2,1)S(1)}, bf16[128,384]{1,0:T(8,128)(2,1)S(1)}, u32[]{:S(2)}, u32[]{:S(2)}) collective-permute-start(bf16[128,384]{1,0:T(8,128)(2,1)S(1)} %get-tuple-element.86), channel_id=1, source_target_pairs={{0,192},{16,208},{32,224},{48,240},{64,128},{80,144},{96,160},{112... | collective-permute-start | bytes 294920 | tf_op jit(solution)/shard_map/ppermute | solution.py:28
  186.7 4.6 %collective-permute-start.48 = (bf16[128,384]{1,0:T(8,128)(2,1)S(1)}, bf16[128,384]{1,0:T(8,128)(2,1)S(1)}, u32[]{:S(2)}, u32[]{:S(2)}) collective-permute-start(bf16[128,384]{1,0:T(8,128)(2,1)S(1)} %half.5.kept), channel_id=1, source_target_pairs={{0,32},{16,48},{32,0},{48,16},{64,96},{80,112},{96,64},{112,80},{1... | collective-permute-start | bytes 294920 | tf_op jit(solution)/shard_map/ppermute | solution.py:28
  192.6 5.0 %collective-permute-start.52 = (bf16[128,384]{1,0:T(8,128)(2,1)S(1)}, bf16[128,384]{1,0:T(8,128)(2,1)S(1)}, u32[]{:S(2)}, u32[]{:S(2)}) collective-permute-start(bf16[128,384]{1,0:T(8,128)(2,1)S(1)} %get-tuple-element.88.a_ref.refs_0_), channel_id=1, source_target_pairs={{0,128},{16,144},{32,160},{48,176},{64,192},{80,208},{96,224},{112... | collective-permute-start | bytes 294920 | tf_op jit(solution)/shard_map/ppermute | solution.py:28
  192.6 5.8 %collective-permute-start.51 = (bf16[128,384]{1,0:T(8,128)(2,1)S(1)}, bf16[128,384]{1,0:T(8,128)(2,1)S(1)}, u32[]{:S(2)}, u32[]{:S(2)}) collective-permute-start(bf16[128,384]{1,0:T(8,128)(2,1)S(1)} %get-tuple-element.88.a_ref.refs_0_), channel_id=1, source_target_pairs={{0,64},{16,80},{32,96},{48,112},{64,0},{80,16},{96,32},{112,48},{1... | collective-permute-start | bytes 294920 | tf_op jit(solution)/shard_map/ppermute | solution.py:28
  194.5 6.6 %collective-permute-start.49 = (bf16[128,384]{1,0:T(8,128)(2,1)S(1)}, bf16[128,384]{1,0:T(8,128)(2,1)S(1)}, u32[]{:S(2)}, u32[]{:S(2)}) collective-permute-start(bf16[128,384]{1,0:T(8,128)(2,1)S(1)} %get-tuple-element.88.a_ref.refs_0_), channel_id=1, source_target_pairs={{0,192},{16,208},{32,224},{48,240},{64,128},{80,144},{96,160},{112... | collective-permute-start | bytes 294920 | tf_op jit(solution)/shard_map/ppermute | solution.py:28
  199.0 5.2 %collective-permute-start.53 = (bf16[128,768]{1,0:T(8,128)(2,1)S(1)}, bf16[128,768]{1,0:T(8,128)(2,1)S(1)}, u32[]{:S(2)}, u32[]{:S(2)}) collective-permute-start(bf16[128,768]{1,0:T(8,128)(2,1)S(1)} %pair.11), channel_id=1, source_target_pairs={{0,16},{16,0},{32,48},{48,32},{64,80},{80,64},{96,112},{112,96},{1... | collective-permute-start | bytes 589832 | tf_op jit(solution)/shard_map/ppermute | solution.py:28
  201.7 2.5 %collective-permute-start.50 = (bf16[128,768]{1,0:T(8,128)(2,1)S(1)}, bf16[128,768]{1,0:T(8,128)(2,1)S(1)}, u32[]{:S(2)}, u32[]{:S(2)}) collective-permute-start(bf16[128,768]{1,0:T(8,128)(2,1)S(1)} %pair.10), channel_id=1, source_target_pairs={{0,16},{16,0},{32,48},{48,32},{64,80},{80,64},{96,112},{112,96},{1... | collective-permute-start | bytes 589832 | tf_op jit(solution)/shard_map/ppermute | solution.py:28
where the time goes:
time: 206 us
  starting transfers between devices  94.2 us (46%)
  waiting for transfers between devices  67.1 us (33%)
  Pallas kernels  39.1 us (19%)
  local copies, waits for them, and re-layouts  4.2 us (2%)
    ppermute x54, starting transfers between devices, swap(): lax.ppermute(array, axis, [(i, i ^ flip) for i in range(lax.axis_size(axi...  94.2 us
    ppermute x54, waiting for transfers between devices, swap(): lax.ppermute(array, axis, [(i, i ^ flip) for i in range(lax.axis_size(axi...  67.1 us
    pallas_call x37, Pallas kernels, call(): pl.pallas_call(kernel, in_specs=[pl.BlockSpec(memory_space=pltpu.SMEM)] +...  39.1 us
    unnamed x8, local copies, waits for them, and re-layouts  4.2 us
  transfers between devices with their start and end apart: 54, of which 34 were waited for; matrix products, arithmetic and copies ran while one was open for 0% of the time, Pallas kernels for 7%

commit v1 on v0

v1 whole, which is shorter than its diff:
```python
import functools
import math

import jax
import jax.numpy as jnp
from jax import lax
from jax.experimental import pallas as pl
from jax.experimental.pallas import tpu as pltpu
from jax.sharding import PartitionSpec as P

ITERS = 3
BF = jnp.bfloat16
F32 = jnp.float32

X_UNIT, ZHI_UNIT = 4, 1
Y_UNIT, ZLO_UNIT, CORE_UNIT = 4, 2, 1
AT_X, AT_ZHI, AT_Y, AT_CORE = range(4)

VMEM_LIMIT = 16 << 20


def shrink(moved, limit_value):
    size = jnp.maximum(jnp.abs(moved) - limit_value, 0.0)
    return jnp.where(moved < 0.0, -size, size)


def swap(array, axis, flip):
    return lax.ppermute(array, axis, [(i, i ^ flip) for i in range(lax.axis_size(axis))])


def swap4(pieces, axis, unit):
    return [swap(pieces[s], axis, s * unit) for s in (1, 2, 3)]


def call(kernel, name, place, args, outs, scratch=(), flops=0, in_hbm=(), in_vmem=(), outs_in_hbm=False, aliases=None):
    vmem, hbm = (pl.BlockSpec(memory_space=m) for m in (pltpu.VMEM, pltpu.HBM))
    moved = sum(math.prod(a.shape) * a.dtype.itemsize for a in [*args, *outs])
    args = list(args)
    for i in in_hbm:
        args[i] = pltpu.with_memory_space_constraint(args[i], pltpu.HBM)
    for i in in_vmem:
        args[i] = pltpu.with_memory_space_constraint(args[i], pltpu.VMEM)
    return pl.pallas_call(
        kernel,
        in_specs=[pl.BlockSpec(memory_space=pltpu.SMEM)] + [hbm if i in in_hbm else vmem for i in range(len(args))],
        out_specs=[hbm if outs_in_hbm else vmem] * len(outs),
        out_shape=list(outs),
        scratch_shapes=list(scratch),
        input_output_aliases=aliases or {},
        compiler_params=pltpu.CompilerParams(vmem_limit_bytes=VMEM_LIMIT),
        cost_estimate=pl.CostEstimate(flops=flops, bytes_accessed=moved, transcendentals=0),
        name=name,
    )(place, *args)


def shape(dims, dtype):
    return jax.ShapeDtypeStruct(dims, dtype)


def part(index, size):
    return pl.ds(pl.multiple_of(index * size, size), size)


def cut(place, acc, outs):
    for s, out in enumerate(outs):
        out[...] = acc[part(place[AT_X] ^ s, out.shape[0]), :].astype(out.dtype)


def first_kernel(place, s_hbm, w_hbm, p0, p1, p2, p3, own_ref, s_ref, w_held, half, sems):
    rows, width = p0.shape[0], own_ref.shape[1]
    load_w = pltpu.make_async_copy(w_hbm, w_held, sems.at[4])
    load_w.start()
    loads = []
    for s in range(4):
        at = part(place[AT_X] ^ s, rows)
        loads.append(pltpu.make_async_copy(s_hbm.at[at, :], s_ref.at[at, :], sems.at[s]))
        loads[s].start()
    load_w.wait()
    half[...] = w_held[...].astype(BF)
    own_ref[...] = w_held[part(place[AT_CORE] * 4 + place[AT_Y], width), :].T
    for s, out in enumerate((p0, p1, p2, p3)):
        loads[s].wait()
        at = part(place[AT_X] ^ s, rows)
        out[...] = jnp.dot(s_ref[at, :], half[...], preferred_element_type=F32).astype(out.dtype)


def load_kernel(place, s_hbm, after, s_ref, sems):
    rows = s_ref.shape[0] // 4
    loads = [pltpu.make_async_copy(s_hbm.at[part(i, rows), :], s_ref.at[part(i, rows), :], sems.at[i]) for i in range(4)]
    for load in loads:
        load.start()
    for load in loads:
        load.wait()


def half_product(place, other, s_ref, pieces, held):
    half = held.shape[1]
    for s, piece in enumerate(pieces):
        held[:, part(place[AT_Y] ^ s, half // 4)] = piece[...]
    columns = part(place[AT_CORE] ^ other, half)
    return lax.dot_general(s_ref[:, columns], held[...], (((1,), (1,)), ((), ())), preferred_element_type=F32)


def own_half_kernel(place, s_ref, w0, w1, w2, w3, acc_ref, held):
    acc_ref[...] = half_product(place, 0, s_ref, (w0, w1, w2, w3), held)


def other_half_kernel(place, s_ref, acc_ref, w0, w1, w2, w3, p0, p1, p2, p3, held, acc):
    acc[...] = acc_ref[...] + half_product(place, 1, s_ref, (w0, w1, w2, w3), held)
    cut(place, acc, (p0, p1, p2, p3))


def sum_kernel(place, p0, g1, g2, g3, sum_ref, half_ref):
    total = (p0[...] + g1[...].astype(F32)) + (g2[...].astype(F32) + g3[...].astype(F32))
    sum_ref[...] = total
    half_ref[...] = total.astype(BF)


def residual_kernel(scale, place, q_ref, z1, z2, z3, t_ref, half_ref, *own):
    rows = q_ref.shape[0]
    total = (q_ref[...] + z1[...].astype(F32)) + (z2[...].astype(F32) + z3[...].astype(F32))
    residual = total * scale - t_ref[part(place[AT_X], rows), :]
    half_ref[...] = residual.T.astype(BF)
    if own:
        own_ref, held = own
        held[...] = residual
        own_ref[...] = held[part(place[AT_ZHI], own_ref.shape[0]), :]


def gradient_kernel(other, place, s_ref, r0, r1, r2, r3, out_ref, held):
    rows, half = r0.shape[1], out_ref.shape[1]
    for s, piece in enumerate((r0, r1, r2, r3)):
        held[:, part(place[AT_X] ^ s, rows)] = piece[...]
    columns = part(place[AT_CORE] ^ other, half)
    out_ref[...] = jnp.dot(held[...], s_ref[:, columns], preferred_element_type=F32).astype(out_ref.dtype)


def join_kernel(place, kept, got, p0, p1, p2, p3):
    width = p0.shape[1]
    for s, out in enumerate((p0, p1, p2, p3)):
        at = part(place[AT_Y] ^ s, width)
        out[...] = (kept[:, at] + got[:, at].astype(F32)).astype(out.dtype)


def half_kernel(place, p0, g1, g2, g3, half_ref):
    total = (p0[...] + g1[...].astype(F32)) + (g2[...].astype(F32) + g3[...].astype(F32))
    half_ref[...] = total.astype(BF)


def update_kernel(factor, limit_value, place, kept, got, fitted_ref, new_ref, half_ref):
    gradient = kept[...].astype(F32) + got[...].astype(F32)
    fitted = shrink(fitted_ref[...] - factor * gradient, limit_value)
    new_ref[...] = fitted
    half_ref[...] = fitted.astype(BF)


def place_kernel(other, place, *refs):
    out_hbm, held, sems = refs[-3:]
    width = held.shape[1]
    copies = []
    for s, piece in enumerate(refs[:4]):
        held[s] = piece[...].astype(F32).T
        rows = part((place[AT_CORE] ^ other) * 4 + (place[AT_Y] ^ s), width)
        copies.append(pltpu.make_async_copy(held.at[s], out_hbm.at[rows, :], sems.at[s]))
        copies[-1].start()
    for copy in copies:
        copy.wait()


def body(signs, targets, weights):
    run_dev, blk_dev = signs.shape
    k = weights.shape[1]
    total_runs = run_dev * lax.axis_size("runs")
    total_blocks = blk_dev * lax.axis_size("blocks")
    scale_factor = 1.0 / math.sqrt(total_blocks)
    step_size = 1.0 / (1.0 + math.sqrt(total_runs / total_blocks)) ** 2
    limit_value = 0.5 * step_size
    rows, width, share = run_dev // 4, blk_dev // 8, run_dev // lax.axis_size("blocks")
    at_run, at_block = lax.axis_index("runs"), lax.axis_index("blocks")
    place = jnp.stack([at_block >> 2, at_block & 3, at_run >> 2, at_run & 1]).astype(jnp.int32)
    flops = 2 * run_dev * blk_dev * k
    chunk, chunk_half = shape((rows, k), F32), shape((rows, k), BF)
    piece, piece_half = shape((k, width), F32), shape((k, width), BF)
    cuts = [chunk] + [chunk_half] * 3
    acc, acc_held, w_held = shape((run_dev, k), F32), pltpu.VMEM((run_dev, k), F32), pltpu.VMEM((k, blk_dev // 2), BF)

    def load(after):
        (loaded,) = call(
            load_kernel, "load", place, [signs, after], [pltpu.VMEM(signs.shape, BF)],
            [pltpu.SemaphoreType.DMA((4,))], in_hbm=(0,),
        )
        return loaded

    def step(pieces, fitted_own, last):
        got = swap4(pieces, "blocks", X_UNIT)
        summed, half = call(sum_kernel, "sum", place, [pieces[0], *got], [chunk, chunk_half])
        got = swap4([half] * 4, "blocks", ZHI_UNIT)
        loaded = load(half)
        half, *residual_own = call(
            functools.partial(residual_kernel, scale_factor), "residual", place, [summed, *got, targets],
            [shape((k, rows), BF)] + [shape((share, k), F32)] * last, [pltpu.VMEM((rows, k), F32)] * last,
        )
        halves = [half] + swap4([half] * 4, "blocks", X_UNIT)
        held = [pltpu.VMEM((k, run_dev), BF)]
        (sent,) = call(
            functools.partial(gradient_kernel, 1), "gradient_sent", place, [loaded, *halves],
            [shape((k, blk_dev // 2), BF)], held, flops // 2, in_vmem=(0,),
        )
        got = swap(sent, "runs", CORE_UNIT)
        (kept,) = call(
            functools.partial(gradient_kernel, 0), "gradient_kept", place, [loaded, *halves],
            [shape((k, blk_dev // 2), F32)], held, flops // 2, in_vmem=(0,),
        )
        pieces = call(join_kernel, "join", place, [kept, got], [piece] + [piece_half] * 3)
        got = swap4(pieces, "runs", Y_UNIT)
        (half,) = call(half_kernel, "half", place, [pieces[0], *got], [piece_half])
        got = swap(half, "runs", ZLO_UNIT)
        fitted_own, half = call(
            functools.partial(update_kernel, step_size * scale_factor, limit_value), "update", place,
            [half, got, fitted_own], [piece, piece_half], aliases={3: 0},
        )
        near = [half] + swap4([half] * 4, "runs", Y_UNIT)
        far = [swap(array, "runs", CORE_UNIT) for array in near]
        return near, far, fitted_own, residual_own, loaded

    def iterate(state):
        turn, pieces, fitted_own = state
        near, far, fitted_own, _, loaded = step(pieces, fitted_own, False)
        (partial,) = call(
            own_half_kernel, "own_half", place, [loaded, *near], [acc], [w_held], flops // 2, in_vmem=(0,)
        )
        pieces = call(
            other_half_kernel, "other_half", place, [loaded, partial, *far], cuts, [w_held, acc_held], flops // 2,
            in_vmem=(0,),
        )
        turn, pieces = lax.optimization_barrier((turn, list(pieces)))
        return turn + 1, pieces, fitted_own

    *pieces, fitted_own = call(
        first_kernel, "first", place, [signs, weights], [*cuts, piece],
        [
            pltpu.VMEM(signs.shape, BF), pltpu.VMEM((blk_dev, k), F32), pltpu.VMEM((blk_dev, k), BF),
            pltpu.SemaphoreType.DMA((5,)),
        ],
        flops, in_hbm=(0, 1),
    )
    _, pieces, fitted_own = lax.while_loop(
        lambda state: state[0] < ITERS - 1, iterate, (jnp.int32(0), pieces, fitted_own)
    )
    near, far, _, residual_own, _ = step(pieces, fitted_own, True)
    held = [pltpu.VMEM((4, width, k), F32), pltpu.SemaphoreType.DMA((4,))]
    whole = [shape((blk_dev, k), F32)]
    fitted = call(functools.partial(place_kernel, 0), "place_near", place, near, whole, held, outs_in_hbm=True)
    (fitted,) = call(
        functools.partial(place_kernel, 1), "place_far", place, [*far, *fitted], whole, held,
        in_hbm=(4,), outs_in_hbm=True, aliases={5: 0},
    )
    return (fitted, residual_own[0])


def solution(mesh):
    in_specs = (P("runs", "blocks"), P("runs", None), P("blocks", None))
    out_specs = (P("blocks", None), P(("runs", "blocks"), None))
    return jax.shard_map(body, mesh=mesh, in_specs=in_specs, out_specs=out_specs, check_vma=False)
```

time: 206 us -> 193 us (0.937)
  waiting for transfers between devices: 67.1 us -> 57.3 us
  local copies, waits for them, and re-layouts: 4.2 us -> 0.01 us
    ppermute x54 -> x63, waiting for transfers between devices: 67.1 us -> 57.3 us  [swap(): lax.ppermute(array, axis, [(i, i ^ flip) for i in range(lax.axis_size(axi...]
    unnamed x8 -> x2, local copies, waits for them, and re-layouts: 4.2 us -> 0.01 us
    pallas_call x37 -> x31, Pallas kernels: 39.1 us -> 41.1 us  [call(): pl.pallas_call(kernel, in_specs=[pl.BlockSpec(memory_space=pltpu.SMEM)] +...]
    ppermute x54 -> x63, starting transfers between devices: 94.2 us -> 92.8 us  [swap(): lax.ppermute(array, axis, [(i, i ^ flip) for i in range(lax.axis_size(axi...]
  transfers between devices with their start and end apart: 54 -> 63, of which waited for: 34 -> 27; matrix products, arithmetic and copies ran while one was open for 0% -> 0% of each run, Pallas kernels for 7% -> 9%
where the time goes in v1:
time: 193 us
  starting transfers between devices  92.8 us (48%)
  waiting for transfers between devices  57.3 us (30%)
  Pallas kernels  41.1 us (21%)
    ppermute x63, starting transfers between devices, swap(): lax.ppermute(array, axis, [(i, i ^ flip) for i in range(lax.axis_size(axi...  92.8 us
    ppermute x63, waiting for transfers between devices, swap(): lax.ppermute(array, axis, [(i, i ^ flip) for i in range(lax.axis_size(axi...  57.3 us
    pallas_call x31, Pallas kernels, call(): pl.pallas_call(kernel, in_specs=[pl.BlockSpec(memory_space=pltpu.SMEM)] +...  41.1 us
  transfers between devices with their start and end apart: 63, of which 27 were waited for; matrix products, arithmetic and copies ran while one was open for 0% of the time, Pallas kernels for 9%

profile of v1, /device:TPU:1, one launch (start us, length us, event | category | flops | bytes accessed | tf_op | source)
XLA Modules:
  0.0 192.7 jit_solution(4918428255241058032)
XLA Ops:
  0.7 4.7 %first.1 = (f32[256,128]{1,0:T(8,128)S(1)}, bf16[256,128]{1,0:T(8,128)(2,1)S(1)}, bf16[256,128]{1,0:T(8,128)(2,1)S(1)}, bf16[256,128]{1,0:T(8,128)(2,1)S(1)}, f32[128,384]{1,0:T(8,128)S(1)}) custom-call(s32[4]{0:T(128)S(1)} %pad_add_fusion.place, bf16[1024,3072]{1,0:T(8,128)(2,1)} %s_hbm.3, f32[3072,128]{1,0:T(8,128)} %w_hbm.1), custom_call_target="tpu_custom_call" | custom-call | flops 805306368 | bytes 8388608 | tf_op jit(solution)/shard_map/first/pallas_call | solution.py:43
  5.5 126.4 %while.18 = (s32[]{:T(128)}, f32[256,128]{1,0:T(8,128)S(1)}, bf16[256,128]{1,0:T(8,128)(2,1)S(1)}, bf16[256,128]{1,0:T(8,128)(2,1)S(1)}, bf16[256,128]{1,0:T(8,1...) while((s32[]{:T(128)}, f32[256,128]{1,0:T(8,128)S(1)}, ...), condition=%wide.region_1.0_spmd, body=%wide.region_0.0_spmd.sunk | while | flops 1610612736 | bytes 54330284 | solution.py:247
  5.5 3.4 %collective-permute-start.2 = (bf16[256,128]{1,0:T(8,128)(2,1)S(1)}, bf16[256,128]{1,0:T(8,128)(2,1)S(1)}, u32[]{:S(2)}, u32[]{:S(2)}) collective-permute-start(bf16[256,128]{1,0:T(8,128)(2,1)S(1)} %get-tuple-element.224), channel_id=1, source_target_pairs={{0,12},{1,13},{2,14},{3,15},{4,8},{5,9},{6,10},{7,11},{8,4},{9,5},... | collective-permute-start | bytes 196616 | tf_op jit(solution)/shard_map/while/body/ppermute | solution.py:28
  10.5 3.0 %collective-permute-done.1.g2 = bf16[256,128]{1,0:T(8,128)(2,1)S(1)} collective-permute-done((bf16[256,128]{1,0:T(8,128)(2,1)S(1)}, bf16[256,128]{1,0:T(8,128)(2,1)S(1)}, u32[]{:S(2)}, u32[]{:S(2)}) %collective-permute-start.1) | collective-permute-done | bytes 65568 | tf_op jit(solution)/shard_map/while/body/ppermute | solution.py:28
  14.1 6.0 %collective-permute-start.5 = (bf16[256,128]{1,0:T(8,128)(2,1)S(1)}, bf16[256,128]{1,0:T(8,128)(2,1)S(1)}, u32[]{:S(2)}, u32[]{:S(2)}) collective-permute-start(bf16[256,128]{1,0:T(8,128)(2,1)S(1)} %get-tuple-element.193.after), channel_id=1, source_target_pairs={{0,3},{1,2},{2,1},{3,0},{4,7},{5,6},{6,5},{7,4},{8,11},{9,10},{10,... | collective-permute-start | bytes 196616 | tf_op jit(solution)/shard_map/while/body/ppermute | solution.py:28
  22.4 5.4 %collective-permute-done.4.z2 = bf16[256,128]{1,0:T(8,128)(2,1)S(1)} collective-permute-done((bf16[256,128]{1,0:T(8,128)(2,1)S(1)}, bf16[256,128]{1,0:T(8,128)(2,1)S(1)}, u32[]{:S(2)}, u32[]{:S(2)}) %collective-permute-start.4) | collective-permute-done | bytes 65568 | tf_op jit(solution)/shard_map/while/body/ppermute | solution.py:28
  28.4 1.4 collective-permute-start.8
  31.8 3.4 %load.3.s_ref = bf16[1024,3072]{1,0:T(8,128)(2,1)S(1)} custom-call(s32[4]{0:T(128)S(1)} %get-tuple-element.236.place, bf16[1024,3072]{1,0:T(8,128)(2,1)} %get-tuple-element.237.s_hbm, bf16[256,128]{1,0:T(8,128)(2,1)S(1)} %get-tuple-element.193.after), custom_call_target="tpu_custom_call" | custom-call | bytes 12648448 | tf_op jit(solution)/shard_map/while/body/load/pallas_call | solution.py:43
  36.4 4.3 %collective-permute-start.9 = (bf16[128,1536]{1,0:T(8,128)(2,1)S(1)}, bf16[128,1536]{1,0:T(8,128)(2,1)S(1)}, u32[]{:S(2)}, u32[]{:S(2)}) collective-permute-start(bf16[128,1536]{1,0:T(8,128)(2,1)S(1)} %gradient_sent.3), channel_id=1, source_target_pairs={{0,16},{16,0},{32,48},{48,32},{64,80},{80,64},{96,112},{112,96},{1... | collective-permute-start | bytes 1179656 | tf_op jit(solution)/shard_map/while/body/ppermute | solution.py:28
  42.7 1.4 collective-permute-start.10
  44.1 2.6 %collective-permute-start.11 = (bf16[128,384]{1,0:T(8,128)(2,1)S(1)}, bf16[128,384]{1,0:T(8,128)(2,1)S(1)}, u32[]{:S(2)}, u32[]{:S(2)}) collective-permute-start(bf16[128,384]{1,0:T(8,128)(2,1)S(1)} %get-tuple-element.197), channel_id=1, source_target_pairs={{0,128},{16,144},{32,160},{48,176},{64,192},{80,208},{96,224},{112... | collective-permute-start | bytes 294920 | tf_op jit(solution)/shard_map/while/body/ppermute | solution.py:28
  46.8 4.6 %collective-permute-done.11.g2 = bf16[128,384]{1,0:T(8,128)(2,1)S(1)} collective-permute-done((bf16[128,384]{1,0:T(8,128)(2,1)S(1)}, bf16[128,384]{1,0:T(8,128)(2,1)S(1)}, u32[]{:S(2)}, u32[]{:S(2)}) %collective-permute-start.11) | collective-permute-done | bytes 98336 | tf_op jit(solution)/shard_map/while/body/ppermute | solution.py:28
  51.3 2.6 %collective-permute-done.12.g3 = bf16[128,384]{1,0:T(8,128)(2,1)S(1)} collective-permute-done((bf16[128,384]{1,0:T(8,128)(2,1)S(1)}, bf16[128,384]{1,0:T(8,128)(2,1)S(1)}, u32[]{:S(2)}, u32[]{:S(2)}) %collective-permute-start.12) | collective-permute-done | bytes 98336 | tf_op jit(solution)/shard_map/while/body/ppermute | solution.py:28
  55.2 2.9 %collective-permute-done.13.got = bf16[128,384]{1,0:T(8,128)(2,1)S(1)} collective-permute-done((bf16[128,384]{1,0:T(8,128)(2,1)S(1)}, bf16[128,384]{1,0:T(8,128)(2,1)S(1)}, u32[]{:S(2)}, u32[]{:S(2)}) %collective-permute-start.13) | collective-permute-done | bytes 98336 | tf_op jit(solution)/shard_map/while/body/ppermute | solution.py:28
  59.6 2.5 %collective-permute-start.14 = (bf16[128,384]{1,0:T(8,128)(2,1)S(1)}, bf16[128,384]{1,0:T(8,128)(2,1)S(1)}, u32[]{:S(2)}, u32[]{:S(2)}) collective-permute-start(bf16[128,384]{1,0:T(8,128)(2,1)S(1)} %get-tuple-element.199.w0), channel_id=1, source_target_pairs={{0,64},{16,80},{32,96},{48,112},{64,0},{80,16},{96,32},{112,48},{1... | collective-permute-start | bytes 294920 | tf_op jit(solution)/shard_map/while/body/ppermute | solution.py:28
  62.1 2.6 %collective-permute-start.17 = (bf16[128,384]{1,0:T(8,128)(2,1)S(1)}, bf16[128,384]{1,0:T(8,128)(2,1)S(1)}, u32[]{:S(2)}, u32[]{:S(2)}) collective-permute-start(bf16[128,384]{1,0:T(8,128)(2,1)S(1)} %get-tuple-element.199.w0), channel_id=1, source_target_pairs={{0,16},{16,0},{32,48},{48,32},{64,80},{80,64},{96,112},{112,96},{1... | collective-permute-start | bytes 294920 | tf_op jit(solution)/shard_map/while/body/ppermute | solution.py:28
  64.7 2.8 %collective-permute-start.20 = (bf16[128,384]{1,0:T(8,128)(2,1)S(1)}, bf16[128,384]{1,0:T(8,128)(2,1)S(1)}, u32[]{:S(2)}, u32[]{:S(2)}) collective-permute-start(bf16[128,384]{1,0:T(8,128)(2,1)S(1)} %collective-permute-done.16.w3), channel_id=1, source_target_pairs={{0,16},{16,0},{32,48},{48,32},{64,80},{80,64},{96,112},{112,96},{1... | collective-permute-start | bytes 294920 | tf_op jit(solution)/shard_map/while/body/ppermute | solution.py:28
  68.3 1.5 own_half.1.acc_ref
  69.9 1.6 other_half.1
  71.5 1.3 collective-permute-start.2
  74.9 1.6 collective-permute-done.2.g3
  78.8 1.9 %collective-permute-start.5 = (bf16[256,128]{1,0:T(8,128)(2,1)S(1)}, bf16[256,128]{1,0:T(8,128)(2,1)S(1)}, u32[]{:S(2)}, u32[]{:S(2)}) collective-permute-start(bf16[256,128]{1,0:T(8,128)(2,1)S(1)} %get-tuple-element.193.after), channel_id=1, source_target_pairs={{0,3},{1,2},{2,1},{3,0},{4,7},{5,6},{6,5},{7,4},{8,11},{9,10},{10,... | collective-permute-start | bytes 196616 | tf_op jit(solution)/shard_map/while/body/ppermute | solution.py:28
  80.7 2.5 %collective-permute-start.4 = (bf16[256,128]{1,0:T(8,128)(2,1)S(1)}, bf16[256,128]{1,0:T(8,128)(2,1)S(1)}, u32[]{:S(2)}, u32[]{:S(2)}) collective-permute-start(bf16[256,128]{1,0:T(8,128)(2,1)S(1)} %get-tuple-element.193.after), channel_id=1, source_target_pairs={{0,2},{1,3},{2,0},{3,1},{4,6},{5,7},{6,4},{7,5},{8,10},{9,11},{10,... | collective-permute-start | bytes 196616 | tf_op jit(solution)/shard_map/while/body/ppermute | solution.py:28
  83.2 1.3 collective-permute-start.3
  84.5 4.0 %collective-permute-done.4.z2 = bf16[256,128]{1,0:T(8,128)(2,1)S(1)} collective-permute-done((bf16[256,128]{1,0:T(8,128)(2,1)S(1)}, bf16[256,128]{1,0:T(8,128)(2,1)S(1)}, u32[]{:S(2)}, u32[]{:S(2)}) %collective-permute-start.4) | collective-permute-done | bytes 65568 | tf_op jit(solution)/shard_map/while/body/ppermute | solution.py:28
  88.5 3.5 %collective-permute-done.3.z1 = bf16[256,128]{1,0:T(8,128)(2,1)S(1)} collective-permute-done((bf16[256,128]{1,0:T(8,128)(2,1)S(1)}, bf16[256,128]{1,0:T(8,128)(2,1)S(1)}, u32[]{:S(2)}, u32[]{:S(2)}) %collective-permute-start.3) | collective-permute-done | bytes 65568 | tf_op jit(solution)/shard_map/while/body/ppermute | solution.py:28
  92.6 1.3 collective-permute-start.8
  94.0 1.2 collective-permute-start.7
  96.0 3.4 %load.3.s_ref = bf16[1024,3072]{1,0:T(8,128)(2,1)S(1)} custom-call(s32[4]{0:T(128)S(1)} %get-tuple-element.236.place, bf16[1024,3072]{1,0:T(8,128)(2,1)} %get-tuple-element.237.s_hbm, bf16[256,128]{1,0:T(8,128)(2,1)S(1)} %get-tuple-element.193.after), custom_call_target="tpu_custom_call" | custom-call | bytes 12648448 | tf_op jit(solution)/shard_map/while/body/load/pallas_call | solution.py:43
  100.6 1.6 collective-permute-start.9
  106.2 1.9 collective-permute-start.12
  108.3 2.6 %collective-permute-done.11.g2 = bf16[128,384]{1,0:T(8,128)(2,1)S(1)} collective-permute-done((bf16[128,384]{1,0:T(8,128)(2,1)S(1)}, bf16[128,384]{1,0:T(8,128)(2,1)S(1)}, u32[]{:S(2)}, u32[]{:S(2)}) %collective-permute-start.11) | collective-permute-done | bytes 98336 | tf_op jit(solution)/shard_map/while/body/ppermute | solution.py:28
  110.9 2.8 %collective-permute-done.12.g3 = bf16[128,384]{1,0:T(8,128)(2,1)S(1)} collective-permute-done((bf16[128,384]{1,0:T(8,128)(2,1)S(1)}, bf16[128,384]{1,0:T(8,128)(2,1)S(1)}, u32[]{:S(2)}, u32[]{:S(2)}) %collective-permute-start.12) | collective-permute-done | bytes 98336 | tf_op jit(solution)/shard_map/while/body/ppermute | solution.py:28
  114.8 3.4 %collective-permute-done.13.got = bf16[128,384]{1,0:T(8,128)(2,1)S(1)} collective-permute-done((bf16[128,384]{1,0:T(8,128)(2,1)S(1)}, bf16[128,384]{1,0:T(8,128)(2,1)S(1)}, u32[]{:S(2)}, u32[]{:S(2)}) %collective-permute-start.13) | collective-permute-done | bytes 98336 | tf_op jit(solution)/shard_map/while/body/ppermute | solution.py:28
  118.9 1.4 collective-permute-start.16
  120.3 2.0 %collective-permute-start.14 = (bf16[128,384]{1,0:T(8,128)(2,1)S(1)}, bf16[128,384]{1,0:T(8,128)(2,1)S(1)}, u32[]{:S(2)}, u32[]{:S(2)}) collective-permute-start(bf16[128,384]{1,0:T(8,128)(2,1)S(1)} %get-tuple-element.199.w0), channel_id=1, source_target_pairs={{0,64},{16,80},{32,96},{48,112},{64,0},{80,16},{96,32},{112,48},{1... | collective-permute-start | bytes 294920 | tf_op jit(solution)/shard_map/while/body/ppermute | solution.py:28
  122.3 2.2 %collective-permute-start.17 = (bf16[128,384]{1,0:T(8,128)(2,1)S(1)}, bf16[128,384]{1,0:T(8,128)(2,1)S(1)}, u32[]{:S(2)}, u32[]{:S(2)}) collective-permute-start(bf16[128,384]{1,0:T(8,128)(2,1)S(1)} %get-tuple-element.199.w0), channel_id=1, source_target_pairs={{0,16},{16,0},{32,48},{48,32},{64,80},{80,64},{96,112},{112,96},{1... | collective-permute-start | bytes 294920 | tf_op jit(solution)/shard_map/while/body/ppermute | solution.py:28
  124.5 2.5 %collective-permute-start.20 = (bf16[128,384]{1,0:T(8,128)(2,1)S(1)}, bf16[128,384]{1,0:T(8,128)(2,1)S(1)}, u32[]{:S(2)}, u32[]{:S(2)}) collective-permute-start(bf16[128,384]{1,0:T(8,128)(2,1)S(1)} %collective-permute-done.16.w3), channel_id=1, source_target_pairs={{0,16},{16,0},{32,48},{48,32},{64,80},{80,64},{96,112},{112,96},{1... | collective-permute-start | bytes 294920 | tf_op jit(solution)/shard_map/while/body/ppermute | solution.py:28
  127.0 1.4 collective-permute-start.19
  128.5 1.5 own_half.1.acc_ref
  130.1 1.6 other_half.1
  132.6 1.8 collective-permute-start.22
  134.4 1.4 collective-permute-start.23
  135.8 1.9 collective-permute-done.22.g2
  137.7 1.5 collective-permute-done.23.g3
  139.8 1.7 collective-permute-start.26
  141.5 2.4 %collective-permute-start.25 = (bf16[256,128]{1,0:T(8,128)(2,1)S(1)}, bf16[256,128]{1,0:T(8,128)(2,1)S(1)}, u32[]{:S(2)}, u32[]{:S(2)}) collective-permute-start(bf16[256,128]{1,0:T(8,128)(2,1)S(1)} %get-tuple-element.93.after), channel_id=1, source_target_pairs={{0,2},{1,3},{2,0},{3,1},{4,6},{5,7},{6,4},{7,5},{8,10},{9,11},{10,... | collective-permute-start | bytes 196616 | tf_op jit(solution)/shard_map/ppermute | solution.py:28
  143.9 1.6 collective-permute-start.24
  145.5 3.1 %collective-permute-done.25.z2 = bf16[256,128]{1,0:T(8,128)(2,1)S(1)} collective-permute-done((bf16[256,128]{1,0:T(8,128)(2,1)S(1)}, bf16[256,128]{1,0:T(8,128)(2,1)S(1)}, u32[]{:S(2)}, u32[]{:S(2)}) %collective-permute-start.25) | collective-permute-done | bytes 65568 | tf_op jit(solution)/shard_map/ppermute | solution.py:28
  148.6 1.2 residual.2
  149.8 2.1 %collective-permute-start.29 = (bf16[128,256]{1,0:T(8,128)(2,1)S(1)}, bf16[128,256]{1,0:T(8,128)(2,1)S(1)}, u32[]{:S(2)}, u32[]{:S(2)}) collective-permute-start(bf16[128,256]{1,0:T(8,128)(2,1)S(1)} %get-tuple-element.95.r0), channel_id=1, source_target_pairs={{0,12},{1,13},{2,14},{3,15},{4,8},{5,9},{6,10},{7,11},{8,4},{9,5},... | collective-permute-start | bytes 196616 | tf_op jit(solution)/shard_map/ppermute | solution.py:28
  151.9 3.7 %collective-permute-start.28 = (bf16[128,256]{1,0:T(8,128)(2,1)S(1)}, bf16[128,256]{1,0:T(8,128)(2,1)S(1)}, u32[]{:S(2)}, u32[]{:S(2)}) collective-permute-start(bf16[128,256]{1,0:T(8,128)(2,1)S(1)} %get-tuple-element.95.r0), channel_id=1, source_target_pairs={{0,8},{1,9},{2,10},{3,11},{4,12},{5,13},{6,14},{7,15},{8,0},{9,1},... | collective-permute-start | bytes 196616 | tf_op jit(solution)/shard_map/ppermute | solution.py:28
  155.6 3.4 %load.2.s_ref = bf16[1024,3072]{1,0:T(8,128)(2,1)S(1)} custom-call(s32[4]{0:T(128)S(1)} %get-tuple-element.320, bf16[1024,3072]{1,0:T(8,128)(2,1)} %get-tuple-element.318, bf16[256,128]{1,0:T(8,128)(2,1)S(1)} %get-tuple-element.93.after), custom_call_target="tpu_custom_call" | custom-call | bytes 12648448 | tf_op jit(solution)/shard_map/load/pallas_call | solution.py:43
  160.9 1.5 collective-permute-start.30
  164.3 1.2 collective-permute-start.31
  165.5 2.2 %collective-permute-start.32 = (bf16[128,384]{1,0:T(8,128)(2,1)S(1)}, bf16[128,384]{1,0:T(8,128)(2,1)S(1)}, u32[]{:S(2)}, u32[]{:S(2)}) collective-permute-start(bf16[128,384]{1,0:T(8,128)(2,1)S(1)} %get-tuple-element.98), channel_id=1, source_target_pairs={{0,128},{16,144},{32,160},{48,176},{64,192},{80,208},{96,224},{112... | collective-permute-start | bytes 294920 | tf_op jit(solution)/shard_map/ppermute | solution.py:28
  168.4 4.0 %collective-permute-done.32.g2 = bf16[128,384]{1,0:T(8,128)(2,1)S(1)} collective-permute-done((bf16[128,384]{1,0:T(8,128)(2,1)S(1)}, bf16[128,384]{1,0:T(8,128)(2,1)S(1)}, u32[]{:S(2)}, u32[]{:S(2)}) %collective-permute-start.32) | collective-permute-done | bytes 98336 | tf_op jit(solution)/shard_map/ppermute | solution.py:28
  172.4 2.6 %collective-permute-done.33.g3 = bf16[128,384]{1,0:T(8,128)(2,1)S(1)} collective-permute-done((bf16[128,384]{1,0:T(8,128)(2,1)S(1)}, bf16[128,384]{1,0:T(8,128)(2,1)S(1)}, u32[]{:S(2)}, u32[]{:S(2)}) %collective-permute-start.33) | collective-permute-done | bytes 98336 | tf_op jit(solution)/shard_map/ppermute | solution.py:28
  175.7 3.5 %collective-permute-done.34.got = bf16[128,384]{1,0:T(8,128)(2,1)S(1)} collective-permute-done((bf16[128,384]{1,0:T(8,128)(2,1)S(1)}, bf16[128,384]{1,0:T(8,128)(2,1)S(1)}, u32[]{:S(2)}, u32[]{:S(2)}) %collective-permute-start.34) | collective-permute-done | bytes 98336 | tf_op jit(solution)/shard_map/ppermute | solution.py:28
  180.8 2.4 %collective-permute-start.36 = (bf16[128,384]{1,0:T(8,128)(2,1)S(1)}, bf16[128,384]{1,0:T(8,128)(2,1)S(1)}, u32[]{:S(2)}, u32[]{:S(2)}) collective-permute-start(bf16[128,384]{1,0:T(8,128)(2,1)S(1)} %get-tuple-element.101.refs_0_), channel_id=1, source_target_pairs={{0,64},{16,80},{32,96},{48,112},{64,0},{80,16},{96,32},{112,48},{1... | collective-permute-start | bytes 294920 | tf_op jit(solution)/shard_map/ppermute | solution.py:28
  183.2 2.6 %collective-permute-start.35 = (bf16[128,384]{1,0:T(8,128)(2,1)S(1)}, bf16[128,384]{1,0:T(8,128)(2,1)S(1)}, u32[]{:S(2)}, u32[]{:S(2)}) collective-permute-start(bf16[128,384]{1,0:T(8,128)(2,1)S(1)} %get-tuple-element.101.refs_0_), channel_id=1, source_target_pairs={{0,16},{16,0},{32,48},{48,32},{64,80},{80,64},{96,112},{112,96},{1... | collective-permute-start | bytes 294920 | tf_op jit(solution)/shard_map/ppermute | solution.py:28
  185.8 1.7 collective-permute-start.41
  189.4 1.5 place_near.1.refs_4_
  191.0 1.6 place_far.1
  (97 shorter events, 36.9 us)
Async XLA Ops:
  0.6 4.8 %copy-start = (f32[1024,128]{1,0:T(8,128)S(1)}, f32[1024,128]{1,0:T(8,128)}, u32[]{:S(2)}) copy-start(f32[1024,128]{1,0:T(8,128)} %t_ref.1) | copy-start | bytes 1572868
  5.5 5.0 %collective-permute-start.2 = (bf16[256,128]{1,0:T(8,128)(2,1)S(1)}, bf16[256,128]{1,0:T(8,128)(2,1)S(1)}, u32[]{:S(2)}, u32[]{:S(2)}) collective-permute-start(bf16[256,128]{1,0:T(8,128)(2,1)S(1)} %get-tuple-element.224), channel_id=1, source_target_pairs={{0,12},{1,13},{2,14},{3,15},{4,8},{5,9},{6,10},{7,11},{8,4},{9,5},... | collective-permute-start | bytes 196616 | tf_op jit(solution)/shard_map/while/body/ppermute | solution.py:28
  8.9 4.7 %collective-permute-start.1 = (bf16[256,128]{1,0:T(8,128)(2,1)S(1)}, bf16[256,128]{1,0:T(8,128)(2,1)S(1)}, u32[]{:S(2)}, u32[]{:S(2)}) collective-permute-start(bf16[256,128]{1,0:T(8,128)(2,1)S(1)} %get-tuple-element.223), channel_id=1, source_target_pairs={{0,8},{1,9},{2,10},{3,11},{4,12},{5,13},{6,14},{7,15},{8,0},{9,1},... | collective-permute-start | bytes 196616 | tf_op jit(solution)/shard_map/while/body/ppermute | solution.py:28
  9.4 4.2 %collective-permute-start = (bf16[256,128]{1,0:T(8,128)(2,1)S(1)}, bf16[256,128]{1,0:T(8,128)(2,1)S(1)}, u32[]{:S(2)}, u32[]{:S(2)}) collective-permute-start(bf16[256,128]{1,0:T(8,128)(2,1)S(1)} %get-tuple-element.222), channel_id=1, source_target_pairs={{0,4},{1,5},{2,6},{3,7},{4,0},{5,1},{6,2},{7,3},{8,12},{9,13},{10,... | collective-permute-start | bytes 196616 | tf_op jit(solution)/shard_map/while/body/ppermute | solution.py:28
  14.1 8.2 %collective-permute-start.5 = (bf16[256,128]{1,0:T(8,128)(2,1)S(1)}, bf16[256,128]{1,0:T(8,128)(2,1)S(1)}, u32[]{:S(2)}, u32[]{:S(2)}) collective-permute-start(bf16[256,128]{1,0:T(8,128)(2,1)S(1)} %get-tuple-element.193.after), channel_id=1, source_target_pairs={{0,3},{1,2},{2,1},{3,0},{4,7},{5,6},{6,5},{7,4},{8,11},{9,10},{10,... | collective-permute-start | bytes 196616 | tf_op jit(solution)/shard_map/while/body/ppermute | solution.py:28
  20.2 7.6 %collective-permute-start.4 = (bf16[256,128]{1,0:T(8,128)(2,1)S(1)}, bf16[256,128]{1,0:T(8,128)(2,1)S(1)}, u32[]{:S(2)}, u32[]{:S(2)}) collective-permute-start(bf16[256,128]{1,0:T(8,128)(2,1)S(1)} %get-tuple-element.193.after), channel_id=1, source_target_pairs={{0,2},{1,3},{2,0},{3,1},{4,6},{5,7},{6,4},{7,5},{8,10},{9,11},{10,... | collective-permute-start | bytes 196616 | tf_op jit(solution)/shard_map/while/body/ppermute | solution.py:28
  21.2 6.6 %collective-permute-start.3 = (bf16[256,128]{1,0:T(8,128)(2,1)S(1)}, bf16[256,128]{1,0:T(8,128)(2,1)S(1)}, u32[]{:S(2)}, u32[]{:S(2)}) collective-permute-start(bf16[256,128]{1,0:T(8,128)(2,1)S(1)} %get-tuple-element.193.after), channel_id=1, source_target_pairs={{0,1},{1,0},{2,3},{3,2},{4,5},{5,4},{6,7},{7,6},{8,9},{9,8},{10,11... | collective-permute-start | bytes 196616 | tf_op jit(solution)/shard_map/while/body/ppermute | solution.py:28
  28.4 6.8 %collective-permute-start.8 = (bf16[128,256]{1,0:T(8,128)(2,1)S(1)}, bf16[128,256]{1,0:T(8,128)(2,1)S(1)}, u32[]{:S(2)}, u32[]{:S(2)}) collective-permute-start(bf16[128,256]{1,0:T(8,128)(2,1)S(1)} %residual.3.r0), channel_id=1, source_target_pairs={{0,12},{1,13},{2,14},{3,15},{4,8},{5,9},{6,10},{7,11},{8,4},{9,5},... | collective-permute-start | bytes 196616 | tf_op jit(solution)/shard_map/while/body/ppermute | solution.py:28
  29.8 5.4 %collective-permute-start.7 = (bf16[128,256]{1,0:T(8,128)(2,1)S(1)}, bf16[128,256]{1,0:T(8,128)(2,1)S(1)}, u32[]{:S(2)}, u32[]{:S(2)}) collective-permute-start(bf16[128,256]{1,0:T(8,128)(2,1)S(1)} %residual.3.r0), channel_id=1, source_target_pairs={{0,8},{1,9},{2,10},{3,11},{4,12},{5,13},{6,14},{7,15},{8,0},{9,1},... | collective-permute-start | bytes 196616 | tf_op jit(solution)/shard_map/while/body/ppermute | solution.py:28
  30.7 4.5 %collective-permute-start.6 = (bf16[128,256]{1,0:T(8,128)(2,1)S(1)}, bf16[128,256]{1,0:T(8,128)(2,1)S(1)}, u32[]{:S(2)}, u32[]{:S(2)}) collective-permute-start(bf16[128,256]{1,0:T(8,128)(2,1)S(1)} %residual.3.r0), channel_id=1, source_target_pairs={{0,4},{1,5},{2,6},{3,7},{4,0},{5,1},{6,2},{7,3},{8,12},{9,13},{10,... | collective-permute-start | bytes 196616 | tf_op jit(solution)/shard_map/while/body/ppermute | solution.py:28
  36.4 5.7 %collective-permute-start.9 = (bf16[128,1536]{1,0:T(8,128)(2,1)S(1)}, bf16[128,1536]{1,0:T(8,128)(2,1)S(1)}, u32[]{:S(2)}, u32[]{:S(2)}) collective-permute-start(bf16[128,1536]{1,0:T(8,128)(2,1)S(1)} %gradient_sent.3), channel_id=1, source_target_pairs={{0,16},{16,0},{32,48},{48,32},{64,80},{80,64},{96,112},{112,96},{1... | collective-permute-start | bytes 1179656 | tf_op jit(solution)/shard_map/while/body/ppermute | solution.py:28
  42.7 4.1 %collective-permute-start.10 = (bf16[128,384]{1,0:T(8,128)(2,1)S(1)}, bf16[128,384]{1,0:T(8,128)(2,1)S(1)}, u32[]{:S(2)}, u32[]{:S(2)}) collective-permute-start(bf16[128,384]{1,0:T(8,128)(2,1)S(1)} %get-tuple-element.196), channel_id=1, source_target_pairs={{0,64},{16,80},{32,96},{48,112},{64,0},{80,16},{96,32},{112,48},{1... | collective-permute-start | bytes 294920 | tf_op jit(solution)/shard_map/while/body/ppermute | solution.py:28
  44.1 7.3 %collective-permute-start.11 = (bf16[128,384]{1,0:T(8,128)(2,1)S(1)}, bf16[128,384]{1,0:T(8,128)(2,1)S(1)}, u32[]{:S(2)}, u32[]{:S(2)}) collective-permute-start(bf16[128,384]{1,0:T(8,128)(2,1)S(1)} %get-tuple-element.197), channel_id=1, source_target_pairs={{0,128},{16,144},{32,160},{48,176},{64,192},{80,208},{96,224},{112... | collective-permute-start | bytes 294920 | tf_op jit(solution)/shard_map/while/body/ppermute | solution.py:28
  46.7 7.2 %collective-permute-start.12 = (bf16[128,384]{1,0:T(8,128)(2,1)S(1)}, bf16[128,384]{1,0:T(8,128)(2,1)S(1)}, u32[]{:S(2)}, u32[]{:S(2)}) collective-permute-start(bf16[128,384]{1,0:T(8,128)(2,1)S(1)} %get-tuple-element.198), channel_id=1, source_target_pairs={{0,192},{16,208},{32,224},{48,240},{64,128},{80,144},{96,160},{112... | collective-permute-start | bytes 294920 | tf_op jit(solution)/shard_map/while/body/ppermute | solution.py:28
  54.5 3.6 %collective-permute-start.13 = (bf16[128,384]{1,0:T(8,128)(2,1)S(1)}, bf16[128,384]{1,0:T(8,128)(2,1)S(1)}, u32[]{:S(2)}, u32[]{:S(2)}) collective-permute-start(bf16[128,384]{1,0:T(8,128)(2,1)S(1)} %half.3.kept), channel_id=1, source_target_pairs={{0,32},{16,48},{32,0},{48,16},{64,96},{80,112},{96,64},{112,80},{1... | collective-permute-start | bytes 294920 | tf_op jit(solution)/shard_map/while/body/ppermute | solution.py:28
  58.8 5.9 %collective-permute-start.16 = (bf16[128,384]{1,0:T(8,128)(2,1)S(1)}, bf16[128,384]{1,0:T(8,128)(2,1)S(1)}, u32[]{:S(2)}, u32[]{:S(2)}) collective-permute-start(bf16[128,384]{1,0:T(8,128)(2,1)S(1)} %get-tuple-element.199.w0), channel_id=1, source_target_pairs={{0,192},{16,208},{32,224},{48,240},{64,128},{80,144},{96,160},{112... | collective-permute-start | bytes 294920 | tf_op jit(solution)/shard_map/while/body/ppermute | solution.py:28
  59.6 7.9 %collective-permute-start.15 = (bf16[128,384]{1,0:T(8,128)(2,1)S(1)}, bf16[128,384]{1,0:T(8,128)(2,1)S(1)}, u32[]{:S(2)}, u32[]{:S(2)}) collective-permute-start(bf16[128,384]{1,0:T(8,128)(2,1)S(1)} %get-tuple-element.199.w0), channel_id=1, source_target_pairs={{0,128},{16,144},{32,160},{48,176},{64,192},{80,208},{96,224},{112... | collective-permute-start | bytes 294920 | tf_op jit(solution)/shard_map/while/body/ppermute | solution.py:28
  59.6 7.9 %collective-permute-start.14 = (bf16[128,384]{1,0:T(8,128)(2,1)S(1)}, bf16[128,384]{1,0:T(8,128)(2,1)S(1)}, u32[]{:S(2)}, u32[]{:S(2)}) collective-permute-start(bf16[128,384]{1,0:T(8,128)(2,1)S(1)} %get-tuple-element.199.w0), channel_id=1, source_target_pairs={{0,64},{16,80},{32,96},{48,112},{64,0},{80,16},{96,32},{112,48},{1... | collective-permute-start | bytes 294920 | tf_op jit(solution)/shard_map/while/body/ppermute | solution.py:28
  62.1 7.8 %collective-permute-start.17 = (bf16[128,384]{1,0:T(8,128)(2,1)S(1)}, bf16[128,384]{1,0:T(8,128)(2,1)S(1)}, u32[]{:S(2)}, u32[]{:S(2)}) collective-permute-start(bf16[128,384]{1,0:T(8,128)(2,1)S(1)} %get-tuple-element.199.w0), channel_id=1, source_target_pairs={{0,16},{16,0},{32,48},{48,32},{64,80},{80,64},{96,112},{112,96},{1... | collective-permute-start | bytes 294920 | tf_op jit(solution)/shard_map/while/body/ppermute | solution.py:28
  64.7 5.2 %collective-permute-start.20 = (bf16[128,384]{1,0:T(8,128)(2,1)S(1)}, bf16[128,384]{1,0:T(8,128)(2,1)S(1)}, u32[]{:S(2)}, u32[]{:S(2)}) collective-permute-start(bf16[128,384]{1,0:T(8,128)(2,1)S(1)} %collective-permute-done.16.w3), channel_id=1, source_target_pairs={{0,16},{16,0},{32,48},{48,32},{64,80},{80,64},{96,112},{112,96},{1... | collective-permute-start | bytes 294920 | tf_op jit(solution)/shard_map/while/body/ppermute | solution.py:28
  67.5 2.4 %collective-permute-start.19 = (bf16[128,384]{1,0:T(8,128)(2,1)S(1)}, bf16[128,384]{1,0:T(8,128)(2,1)S(1)}, u32[]{:S(2)}, u32[]{:S(2)}) collective-permute-start(bf16[128,384]{1,0:T(8,128)(2,1)S(1)} %collective-permute-done.15.w2), channel_id=1, source_target_pairs={{0,16},{16,0},{32,48},{48,32},{64,80},{80,64},{96,112},{112,96},{1... | collective-permute-start | bytes 294920 | tf_op jit(solution)/shard_map/while/body/ppermute | solution.py:28
  67.5 2.4 %collective-permute-start.18 = (bf16[128,384]{1,0:T(8,128)(2,1)S(1)}, bf16[128,384]{1,0:T(8,128)(2,1)S(1)}, u32[]{:S(2)}, u32[]{:S(2)}) collective-permute-start(bf16[128,384]{1,0:T(8,128)(2,1)S(1)} %collective-permute-done.14.w1), channel_id=1, source_target_pairs={{0,16},{16,0},{32,48},{48,32},{64,80},{80,64},{96,112},{112,96},{1... | collective-permute-start | bytes 294920 | tf_op jit(solution)/shard_map/while/body/ppermute | solution.py:28
  71.5 5.0 %collective-permute-start.2 = (bf16[256,128]{1,0:T(8,128)(2,1)S(1)}, bf16[256,128]{1,0:T(8,128)(2,1)S(1)}, u32[]{:S(2)}, u32[]{:S(2)}) collective-permute-start(bf16[256,128]{1,0:T(8,128)(2,1)S(1)} %get-tuple-element.224), channel_id=1, source_target_pairs={{0,12},{1,13},{2,14},{3,15},{4,8},{5,9},{6,10},{7,11},{8,4},{9,5},... | collective-permute-start | bytes 196616 | tf_op jit(solution)/shard_map/while/body/ppermute | solution.py:28
  72.8 4.6 %collective-permute-start.1 = (bf16[256,128]{1,0:T(8,128)(2,1)S(1)}, bf16[256,128]{1,0:T(8,128)(2,1)S(1)}, u32[]{:S(2)}, u32[]{:S(2)}) collective-permute-start(bf16[256,128]{1,0:T(8,128)(2,1)S(1)} %get-tuple-element.223), channel_id=1, source_target_pairs={{0,8},{1,9},{2,10},{3,11},{4,12},{5,13},{6,14},{7,15},{8,0},{9,1},... | collective-permute-start | bytes 196616 | tf_op jit(solution)/shard_map/while/body/ppermute | solution.py:28
  74.0 4.2 %collective-permute-start = (bf16[256,128]{1,0:T(8,128)(2,1)S(1)}, bf16[256,128]{1,0:T(8,128)(2,1)S(1)}, u32[]{:S(2)}, u32[]{:S(2)}) collective-permute-start(bf16[256,128]{1,0:T(8,128)(2,1)S(1)} %get-tuple-element.222), channel_id=1, source_target_pairs={{0,4},{1,5},{2,6},{3,7},{4,0},{5,1},{6,2},{7,3},{8,12},{9,13},{10,... | collective-permute-start | bytes 196616 | tf_op jit(solution)/shard_map/while/body/ppermute | solution.py:28
  78.8 5.7 %collective-permute-start.5 = (bf16[256,128]{1,0:T(8,128)(2,1)S(1)}, bf16[256,128]{1,0:T(8,128)(2,1)S(1)}, u32[]{:S(2)}, u32[]{:S(2)}) collective-permute-start(bf16[256,128]{1,0:T(8,128)(2,1)S(1)} %get-tuple-element.193.after), channel_id=1, source_target_pairs={{0,3},{1,2},{2,1},{3,0},{4,7},{5,6},{6,5},{7,4},{8,11},{9,10},{10,... | collective-permute-start | bytes 196616 | tf_op jit(solution)/shard_map/while/body/ppermute | solution.py:28
  80.7 7.8 %collective-permute-start.4 = (bf16[256,128]{1,0:T(8,128)(2,1)S(1)}, bf16[256,128]{1,0:T(8,128)(2,1)S(1)}, u32[]{:S(2)}, u32[]{:S(2)}) collective-permute-start(bf16[256,128]{1,0:T(8,128)(2,1)S(1)} %get-tuple-element.193.after), channel_id=1, source_target_pairs={{0,2},{1,3},{2,0},{3,1},{4,6},{5,7},{6,4},{7,5},{8,10},{9,11},{10,... | collective-permute-start | bytes 196616 | tf_op jit(solution)/shard_map/while/body/ppermute | solution.py:28
  83.2 8.8 %collective-permute-start.3 = (bf16[256,128]{1,0:T(8,128)(2,1)S(1)}, bf16[256,128]{1,0:T(8,128)(2,1)S(1)}, u32[]{:S(2)}, u32[]{:S(2)}) collective-permute-start(bf16[256,128]{1,0:T(8,128)(2,1)S(1)} %get-tuple-element.193.after), channel_id=1, source_target_pairs={{0,1},{1,0},{2,3},{3,2},{4,5},{5,4},{6,7},{7,6},{8,9},{9,8},{10,11... | collective-permute-start | bytes 196616 | tf_op jit(solution)/shard_map/while/body/ppermute | solution.py:28
  92.6 6.8 %collective-permute-start.8 = (bf16[128,256]{1,0:T(8,128)(2,1)S(1)}, bf16[128,256]{1,0:T(8,128)(2,1)S(1)}, u32[]{:S(2)}, u32[]{:S(2)}) collective-permute-start(bf16[128,256]{1,0:T(8,128)(2,1)S(1)} %residual.3.r0), channel_id=1, source_target_pairs={{0,12},{1,13},{2,14},{3,15},{4,8},{5,9},{6,10},{7,11},{8,4},{9,5},... | collective-permute-start | bytes 196616 | tf_op jit(solution)/shard_map/while/body/ppermute | solution.py:28
  94.0 5.4 %collective-permute-start.7 = (bf16[128,256]{1,0:T(8,128)(2,1)S(1)}, bf16[128,256]{1,0:T(8,128)(2,1)S(1)}, u32[]{:S(2)}, u32[]{:S(2)}) collective-permute-start(bf16[128,256]{1,0:T(8,128)(2,1)S(1)} %residual.3.r0), channel_id=1, source_target_pairs={{0,8},{1,9},{2,10},{3,11},{4,12},{5,13},{6,14},{7,15},{8,0},{9,1},... | collective-permute-start | bytes 196616 | tf_op jit(solution)/shard_map/while/body/ppermute | solution.py:28
  95.2 4.2 %collective-permute-start.6 = (bf16[128,256]{1,0:T(8,128)(2,1)S(1)}, bf16[128,256]{1,0:T(8,128)(2,1)S(1)}, u32[]{:S(2)}, u32[]{:S(2)}) collective-permute-start(bf16[128,256]{1,0:T(8,128)(2,1)S(1)} %residual.3.r0), channel_id=1, source_target_pairs={{0,4},{1,5},{2,6},{3,7},{4,0},{5,1},{6,2},{7,3},{8,12},{9,13},{10,... | collective-permute-start | bytes 196616 | tf_op jit(solution)/shard_map/while/body/ppermute | solution.py:28
  100.6 3.0 %collective-permute-start.9 = (bf16[128,1536]{1,0:T(8,128)(2,1)S(1)}, bf16[128,1536]{1,0:T(8,128)(2,1)S(1)}, u32[]{:S(2)}, u32[]{:S(2)}) collective-permute-start(bf16[128,1536]{1,0:T(8,128)(2,1)S(1)} %gradient_sent.3), channel_id=1, source_target_pairs={{0,16},{16,0},{32,48},{48,32},{64,80},{80,64},{96,112},{112,96},{1... | collective-permute-start | bytes 1179656 | tf_op jit(solution)/shard_map/while/body/ppermute | solution.py:28
  104.2 4.1 %collective-permute-start.10 = (bf16[128,384]{1,0:T(8,128)(2,1)S(1)}, bf16[128,384]{1,0:T(8,128)(2,1)S(1)}, u32[]{:S(2)}, u32[]{:S(2)}) collective-permute-start(bf16[128,384]{1,0:T(8,128)(2,1)S(1)} %get-tuple-element.196), channel_id=1, source_target_pairs={{0,64},{16,80},{32,96},{48,112},{64,0},{80,16},{96,32},{112,48},{1... | collective-permute-start | bytes 294920 | tf_op jit(solution)/shard_map/while/body/ppermute | solution.py:28
  105.1 5.8 %collective-permute-start.11 = (bf16[128,384]{1,0:T(8,128)(2,1)S(1)}, bf16[128,384]{1,0:T(8,128)(2,1)S(1)}, u32[]{:S(2)}, u32[]{:S(2)}) collective-permute-start(bf16[128,384]{1,0:T(8,128)(2,1)S(1)} %get-tuple-element.197), channel_id=1, source_target_pairs={{0,128},{16,144},{32,160},{48,176},{64,192},{80,208},{96,224},{112... | collective-permute-start | bytes 294920 | tf_op jit(solution)/shard_map/while/body/ppermute | solution.py:28
  106.2 7.5 %collective-permute-start.12 = (bf16[128,384]{1,0:T(8,128)(2,1)S(1)}, bf16[128,384]{1,0:T(8,128)(2,1)S(1)}, u32[]{:S(2)}, u32[]{:S(2)}) collective-permute-start(bf16[128,384]{1,0:T(8,128)(2,1)S(1)} %get-tuple-element.198), channel_id=1, source_target_pairs={{0,192},{16,208},{32,224},{48,240},{64,128},{80,144},{96,160},{112... | collective-permute-start | bytes 294920 | tf_op jit(solution)/shard_map/while/body/ppermute | solution.py:28
  114.3 4.0 %collective-permute-start.13 = (bf16[128,384]{1,0:T(8,128)(2,1)S(1)}, bf16[128,384]{1,0:T(8,128)(2,1)S(1)}, u32[]{:S(2)}, u32[]{:S(2)}) collective-permute-start(bf16[128,384]{1,0:T(8,128)(2,1)S(1)} %half.3.kept), channel_id=1, source_target_pairs={{0,32},{16,48},{32,0},{48,16},{64,96},{80,112},{96,64},{112,80},{1... | collective-permute-start | bytes 294920 | tf_op jit(solution)/shard_map/while/body/ppermute | solution.py:28
  118.9 5.5 %collective-permute-start.16 = (bf16[128,384]{1,0:T(8,128)(2,1)S(1)}, bf16[128,384]{1,0:T(8,128)(2,1)S(1)}, u32[]{:S(2)}, u32[]{:S(2)}) collective-permute-start(bf16[128,384]{1,0:T(8,128)(2,1)S(1)} %get-tuple-element.199.w0), channel_id=1, source_target_pairs={{0,192},{16,208},{32,224},{48,240},{64,128},{80,144},{96,160},{112... | collective-permute-start | bytes 294920 | tf_op jit(solution)/shard_map/while/body/ppermute | solution.py:28
  120.3 6.7 %collective-permute-start.15 = (bf16[128,384]{1,0:T(8,128)(2,1)S(1)}, bf16[128,384]{1,0:T(8,128)(2,1)S(1)}, u32[]{:S(2)}, u32[]{:S(2)}) collective-permute-start(bf16[128,384]{1,0:T(8,128)(2,1)S(1)} %get-tuple-element.199.w0), channel_id=1, source_target_pairs={{0,128},{16,144},{32,160},{48,176},{64,192},{80,208},{96,224},{112... | collective-permute-start | bytes 294920 | tf_op jit(solution)/shard_map/while/body/ppermute | solution.py:28
  120.3 8.2 %collective-permute-start.14 = (bf16[128,384]{1,0:T(8,128)(2,1)S(1)}, bf16[128,384]{1,0:T(8,128)(2,1)S(1)}, u32[]{:S(2)}, u32[]{:S(2)}) collective-permute-start(bf16[128,384]{1,0:T(8,128)(2,1)S(1)} %get-tuple-element.199.w0), channel_id=1, source_target_pairs={{0,64},{16,80},{32,96},{48,112},{64,0},{80,16},{96,32},{112,48},{1... | collective-permute-start | bytes 294920 | tf_op jit(solution)/shard_map/while/body/ppermute | solution.py:28
  122.3 7.7 %collective-permute-start.17 = (bf16[128,384]{1,0:T(8,128)(2,1)S(1)}, bf16[128,384]{1,0:T(8,128)(2,1)S(1)}, u32[]{:S(2)}, u32[]{:S(2)}) collective-permute-start(bf16[128,384]{1,0:T(8,128)(2,1)S(1)} %get-tuple-element.199.w0), channel_id=1, source_target_pairs={{0,16},{16,0},{32,48},{48,32},{64,80},{80,64},{96,112},{112,96},{1... | collective-permute-start | bytes 294920 | tf_op jit(solution)/shard_map/while/body/ppermute | solution.py:28
  124.5 5.6 %collective-permute-start.20 = (bf16[128,384]{1,0:T(8,128)(2,1)S(1)}, bf16[128,384]{1,0:T(8,128)(2,1)S(1)}, u32[]{:S(2)}, u32[]{:S(2)}) collective-permute-start(bf16[128,384]{1,0:T(8,128)(2,1)S(1)} %collective-permute-done.16.w3), channel_id=1, source_target_pairs={{0,16},{16,0},{32,48},{48,32},{64,80},{80,64},{96,112},{112,96},{1... | collective-permute-start | bytes 294920 | tf_op jit(solution)/shard_map/while/body/ppermute | solution.py:28
  127.0 3.0 %collective-permute-start.19 = (bf16[128,384]{1,0:T(8,128)(2,1)S(1)}, bf16[128,384]{1,0:T(8,128)(2,1)S(1)}, u32[]{:S(2)}, u32[]{:S(2)}) collective-permute-start(bf16[128,384]{1,0:T(8,128)(2,1)S(1)} %collective-permute-done.15.w2), channel_id=1, source_target_pairs={{0,16},{16,0},{32,48},{48,32},{64,80},{80,64},{96,112},{112,96},{1... | collective-permute-start | bytes 294920 | tf_op jit(solution)/shard_map/while/body/ppermute | solution.py:28
  128.5 1.6 collective-permute-start.18
  131.8 3.9 %collective-permute-start.21 = (bf16[256,128]{1,0:T(8,128)(2,1)S(1)}, bf16[256,128]{1,0:T(8,128)(2,1)S(1)}, u32[]{:S(2)}, u32[]{:S(2)}) collective-permute-start(bf16[256,128]{1,0:T(8,128)(2,1)S(1)} %get-tuple-element.90), channel_id=1, source_target_pairs={{0,4},{1,5},{2,6},{3,7},{4,0},{5,1},{6,2},{7,3},{8,12},{9,13},{10,... | collective-permute-start | bytes 196616 | tf_op jit(solution)/shard_map/ppermute | solution.py:28
  132.6 5.1 %collective-permute-start.22 = (bf16[256,128]{1,0:T(8,128)(2,1)S(1)}, bf16[256,128]{1,0:T(8,128)(2,1)S(1)}, u32[]{:S(2)}, u32[]{:S(2)}) collective-permute-start(bf16[256,128]{1,0:T(8,128)(2,1)S(1)} %get-tuple-element.91), channel_id=1, source_target_pairs={{0,8},{1,9},{2,10},{3,11},{4,12},{5,13},{6,14},{7,15},{8,0},{9,1},... | collective-permute-start | bytes 196616 | tf_op jit(solution)/shard_map/ppermute | solution.py:28
  134.4 4.8 %collective-permute-start.23 = (bf16[256,128]{1,0:T(8,128)(2,1)S(1)}, bf16[256,128]{1,0:T(8,128)(2,1)S(1)}, u32[]{:S(2)}, u32[]{:S(2)}) collective-permute-start(bf16[256,128]{1,0:T(8,128)(2,1)S(1)} %get-tuple-element.92), channel_id=1, source_target_pairs={{0,12},{1,13},{2,14},{3,15},{4,8},{5,9},{6,10},{7,11},{8,4},{9,5},... | collective-permute-start | bytes 196616 | tf_op jit(solution)/shard_map/ppermute | solution.py:28
  139.8 5.7 %collective-permute-start.26 = (bf16[256,128]{1,0:T(8,128)(2,1)S(1)}, bf16[256,128]{1,0:T(8,128)(2,1)S(1)}, u32[]{:S(2)}, u32[]{:S(2)}) collective-permute-start(bf16[256,128]{1,0:T(8,128)(2,1)S(1)} %get-tuple-element.93.after), channel_id=1, source_target_pairs={{0,3},{1,2},{2,1},{3,0},{4,7},{5,6},{6,5},{7,4},{8,11},{9,10},{10,... | collective-permute-start | bytes 196616 | tf_op jit(solution)/shard_map/ppermute | solution.py:28
  141.5 7.1 %collective-permute-start.25 = (bf16[256,128]{1,0:T(8,128)(2,1)S(1)}, bf16[256,128]{1,0:T(8,128)(2,1)S(1)}, u32[]{:S(2)}, u32[]{:S(2)}) collective-permute-start(bf16[256,128]{1,0:T(8,128)(2,1)S(1)} %get-tuple-element.93.after), channel_id=1, source_target_pairs={{0,2},{1,3},{2,0},{3,1},{4,6},{5,7},{6,4},{7,5},{8,10},{9,11},{10,... | collective-permute-start | bytes 196616 | tf_op jit(solution)/shard_map/ppermute | solution.py:28
  143.9 4.8 %collective-permute-start.24 = (bf16[256,128]{1,0:T(8,128)(2,1)S(1)}, bf16[256,128]{1,0:T(8,128)(2,1)S(1)}, u32[]{:S(2)}, u32[]{:S(2)}) collective-permute-start(bf16[256,128]{1,0:T(8,128)(2,1)S(1)} %get-tuple-element.93.after), channel_id=1, source_target_pairs={{0,1},{1,0},{2,3},{3,2},{4,5},{5,4},{6,7},{7,6},{8,9},{9,8},{10,11... | collective-permute-start | bytes 196616 | tf_op jit(solution)/shard_map/ppermute | solution.py:28
  149.8 9.2 %collective-permute-start.29 = (bf16[128,256]{1,0:T(8,128)(2,1)S(1)}, bf16[128,256]{1,0:T(8,128)(2,1)S(1)}, u32[]{:S(2)}, u32[]{:S(2)}) collective-permute-start(bf16[128,256]{1,0:T(8,128)(2,1)S(1)} %get-tuple-element.95.r0), channel_id=1, source_target_pairs={{0,12},{1,13},{2,14},{3,15},{4,8},{5,9},{6,10},{7,11},{8,4},{9,5},... | collective-permute-start | bytes 196616 | tf_op jit(solution)/shard_map/ppermute | solution.py:28
  151.9 7.1 %collective-permute-start.28 = (bf16[128,256]{1,0:T(8,128)(2,1)S(1)}, bf16[128,256]{1,0:T(8,128)(2,1)S(1)}, u32[]{:S(2)}, u32[]{:S(2)}) collective-permute-start(bf16[128,256]{1,0:T(8,128)(2,1)S(1)} %get-tuple-element.95.r0), channel_id=1, source_target_pairs={{0,8},{1,9},{2,10},{3,11},{4,12},{5,13},{6,14},{7,15},{8,0},{9,1},... | collective-permute-start | bytes 196616 | tf_op jit(solution)/shard_map/ppermute | solution.py:28
  155.6 4.1 %collective-permute-start.27 = (bf16[128,256]{1,0:T(8,128)(2,1)S(1)}, bf16[128,256]{1,0:T(8,128)(2,1)S(1)}, u32[]{:S(2)}, u32[]{:S(2)}) collective-permute-start(bf16[128,256]{1,0:T(8,128)(2,1)S(1)} %get-tuple-element.95.r0), channel_id=1, source_target_pairs={{0,4},{1,5},{2,6},{3,7},{4,0},{5,1},{6,2},{7,3},{8,12},{9,13},{10,... | collective-permute-start | bytes 196616 | tf_op jit(solution)/shard_map/ppermute | solution.py:28
  160.9 2.8 %collective-permute-start.30 = (bf16[128,1536]{1,0:T(8,128)(2,1)S(1)}, bf16[128,1536]{1,0:T(8,128)(2,1)S(1)}, u32[]{:S(2)}, u32[]{:S(2)}) collective-permute-start(bf16[128,1536]{1,0:T(8,128)(2,1)S(1)} %gradient_sent.2), channel_id=1, source_target_pairs={{0,16},{16,0},{32,48},{48,32},{64,80},{80,64},{96,112},{112,96},{1... | collective-permute-start | bytes 1179656 | tf_op jit(solution)/shard_map/ppermute | solution.py:28
  164.3 4.1 %collective-permute-start.31 = (bf16[128,384]{1,0:T(8,128)(2,1)S(1)}, bf16[128,384]{1,0:T(8,128)(2,1)S(1)}, u32[]{:S(2)}, u32[]{:S(2)}) collective-permute-start(bf16[128,384]{1,0:T(8,128)(2,1)S(1)} %get-tuple-element.97), channel_id=1, source_target_pairs={{0,64},{16,80},{32,96},{48,112},{64,0},{80,16},{96,32},{112,48},{1... | collective-permute-start | bytes 294920 | tf_op jit(solution)/shard_map/ppermute | solution.py:28
  165.5 6.9 %collective-permute-start.32 = (bf16[128,384]{1,0:T(8,128)(2,1)S(1)}, bf16[128,384]{1,0:T(8,128)(2,1)S(1)}, u32[]{:S(2)}, u32[]{:S(2)}) collective-permute-start(bf16[128,384]{1,0:T(8,128)(2,1)S(1)} %get-tuple-element.98), channel_id=1, source_target_pairs={{0,128},{16,144},{32,160},{48,176},{64,192},{80,208},{96,224},{112... | collective-permute-start | bytes 294920 | tf_op jit(solution)/shard_map/ppermute | solution.py:28
  167.7 7.2 %collective-permute-start.33 = (bf16[128,384]{1,0:T(8,128)(2,1)S(1)}, bf16[128,384]{1,0:T(8,128)(2,1)S(1)}, u32[]{:S(2)}, u32[]{:S(2)}) collective-permute-start(bf16[128,384]{1,0:T(8,128)(2,1)S(1)} %get-tuple-element.99), channel_id=1, source_target_pairs={{0,192},{16,208},{32,224},{48,240},{64,128},{80,144},{96,160},{112... | collective-permute-start | bytes 294920 | tf_op jit(solution)/shard_map/ppermute | solution.py:28
  175.6 3.6 %collective-permute-start.34 = (bf16[128,384]{1,0:T(8,128)(2,1)S(1)}, bf16[128,384]{1,0:T(8,128)(2,1)S(1)}, u32[]{:S(2)}, u32[]{:S(2)}) collective-permute-start(bf16[128,384]{1,0:T(8,128)(2,1)S(1)} %half.2.kept), channel_id=1, source_target_pairs={{0,32},{16,48},{32,0},{48,16},{64,96},{80,112},{96,64},{112,80},{1... | collective-permute-start | bytes 294920 | tf_op jit(solution)/shard_map/ppermute | solution.py:28
  179.8 5.9 %collective-permute-start.40 = (bf16[128,384]{1,0:T(8,128)(2,1)S(1)}, bf16[128,384]{1,0:T(8,128)(2,1)S(1)}, u32[]{:S(2)}, u32[]{:S(2)}) collective-permute-start(bf16[128,384]{1,0:T(8,128)(2,1)S(1)} %get-tuple-element.101.refs_0_), channel_id=1, source_target_pairs={{0,192},{16,208},{32,224},{48,240},{64,128},{80,144},{96,160},{112... | collective-permute-start | bytes 294920 | tf_op jit(solution)/shard_map/ppermute | solution.py:28
  180.8 6.7 %collective-permute-start.38 = (bf16[128,384]{1,0:T(8,128)(2,1)S(1)}, bf16[128,384]{1,0:T(8,128)(2,1)S(1)}, u32[]{:S(2)}, u32[]{:S(2)}) collective-permute-start(bf16[128,384]{1,0:T(8,128)(2,1)S(1)} %get-tuple-element.101.refs_0_), channel_id=1, source_target_pairs={{0,128},{16,144},{32,160},{48,176},{64,192},{80,208},{96,224},{112... | collective-permute-start | bytes 294920 | tf_op jit(solution)/shard_map/ppermute | solution.py:28
  180.8 7.8 %collective-permute-start.36 = (bf16[128,384]{1,0:T(8,128)(2,1)S(1)}, bf16[128,384]{1,0:T(8,128)(2,1)S(1)}, u32[]{:S(2)}, u32[]{:S(2)}) collective-permute-start(bf16[128,384]{1,0:T(8,128)(2,1)S(1)} %get-tuple-element.101.refs_0_), channel_id=1, source_target_pairs={{0,64},{16,80},{32,96},{48,112},{64,0},{80,16},{96,32},{112,48},{1... | collective-permute-start | bytes 294920 | tf_op jit(solution)/shard_map/ppermute | solution.py:28
  183.2 7.8 %collective-permute-start.35 = (bf16[128,384]{1,0:T(8,128)(2,1)S(1)}, bf16[128,384]{1,0:T(8,128)(2,1)S(1)}, u32[]{:S(2)}, u32[]{:S(2)}) collective-permute-start(bf16[128,384]{1,0:T(8,128)(2,1)S(1)} %get-tuple-element.101.refs_0_), channel_id=1, source_target_pairs={{0,16},{16,0},{32,48},{48,32},{64,80},{80,64},{96,112},{112,96},{1... | collective-permute-start | bytes 294920 | tf_op jit(solution)/shard_map/ppermute | solution.py:28
  185.8 5.2 %collective-permute-start.41 = (bf16[128,384]{1,0:T(8,128)(2,1)S(1)}, bf16[128,384]{1,0:T(8,128)(2,1)S(1)}, u32[]{:S(2)}, u32[]{:S(2)}) collective-permute-start(bf16[128,384]{1,0:T(8,128)(2,1)S(1)} %collective-permute-done.40.refs_3_), channel_id=1, source_target_pairs={{0,16},{16,0},{32,48},{48,32},{64,80},{80,64},{96,112},{112,96},{1... | collective-permute-start | bytes 294920 | tf_op jit(solution)/shard_map/ppermute | solution.py:28
  187.5 3.5 %collective-permute-start.39 = (bf16[128,384]{1,0:T(8,128)(2,1)S(1)}, bf16[128,384]{1,0:T(8,128)(2,1)S(1)}, u32[]{:S(2)}, u32[]{:S(2)}) collective-permute-start(bf16[128,384]{1,0:T(8,128)(2,1)S(1)} %collective-permute-done.38.refs_2_), channel_id=1, source_target_pairs={{0,16},{16,0},{32,48},{48,32},{64,80},{80,64},{96,112},{112,96},{1... | collective-permute-start | bytes 294920 | tf_op jit(solution)/shard_map/ppermute | solution.py:28
  188.6 2.4 %collective-permute-start.37 = (bf16[128,384]{1,0:T(8,128)(2,1)S(1)}, bf16[128,384]{1,0:T(8,128)(2,1)S(1)}, u32[]{:S(2)}, u32[]{:S(2)}) collective-permute-start(bf16[128,384]{1,0:T(8,128)(2,1)S(1)} %collective-permute-done.36.refs_1_), channel_id=1, source_target_pairs={{0,16},{16,0},{32,48},{48,32},{64,80},{80,64},{96,112},{112,96},{1... | collective-permute-start | bytes 294920 | tf_op jit(solution)/shard_map/ppermute | solution.py:28

commit v2 on v1

v2 whole, which is shorter than its diff:
```python
import functools
import math

import jax
import jax.numpy as jnp
from jax import lax
from jax.experimental import pallas as pl
from jax.experimental.pallas import tpu as pltpu
from jax.sharding import PartitionSpec as P

ITERS = 3
BF = jnp.bfloat16
F32 = jnp.float32

X_UNIT, ZHI_UNIT = 4, 1
Y_UNIT, ZLO_UNIT, CORE_UNIT = 4, 2, 1
AT_X, AT_ZHI, AT_Y, AT_CORE = ("blocks", 2, 3), ("blocks", 0, 3), ("runs", 2, 3), ("runs", 0, 1)


def coordinate(at):
    axis, shift, bits = at
    return (lax.axis_index(axis) >> shift) & bits

VMEM_LIMIT = 16 << 20


def shrink(moved, limit_value):
    size = jnp.maximum(jnp.abs(moved) - limit_value, 0.0)
    return jnp.where(moved < 0.0, -size, size)


def swap(array, axis, flip):
    return lax.ppermute(array, axis, [(i, i ^ flip) for i in range(lax.axis_size(axis))])


def swap4(pieces, axis, unit):
    return [swap(pieces[s], axis, s * unit) for s in (1, 2, 3)]


def call(kernel, name, args, outs, scratch=(), flops=0, in_hbm=(), in_vmem=(), outs_in_hbm=False, aliases=None):
    vmem, hbm = (pl.BlockSpec(memory_space=m) for m in (pltpu.VMEM, pltpu.HBM))
    moved = sum(math.prod(a.shape) * a.dtype.itemsize for a in [*args, *outs])
    args = list(args)
    for i in in_hbm:
        args[i] = pltpu.with_memory_space_constraint(args[i], pltpu.HBM)
    for i in in_vmem:
        args[i] = pltpu.with_memory_space_constraint(args[i], pltpu.VMEM)
    return pl.pallas_call(
        kernel,
        in_specs=[hbm if i in in_hbm else vmem for i in range(len(args))],
        out_specs=[hbm if outs_in_hbm else vmem] * len(outs),
        out_shape=list(outs),
        scratch_shapes=list(scratch),
        input_output_aliases=aliases or {},
        compiler_params=pltpu.CompilerParams(vmem_limit_bytes=VMEM_LIMIT),
        cost_estimate=pl.CostEstimate(flops=flops, bytes_accessed=moved, transcendentals=0),
        name=name,
    )(*args)


def shape(dims, dtype):
    return jax.ShapeDtypeStruct(dims, dtype)


def part(index, size):
    return pl.ds(pl.multiple_of(index * size, size), size)


def cut(acc, outs):
    for s, out in enumerate(outs):
        out[...] = acc[part(coordinate(AT_X) ^ s, out.shape[0]), :].astype(out.dtype)


def first_kernel(s_hbm, w_hbm, p0, p1, p2, p3, own_ref, s_ref, w_held, half, sems):
    rows, width = p0.shape[0], own_ref.shape[1]
    load_w = pltpu.make_async_copy(w_hbm, w_held, sems.at[4])
    load_w.start()
    loads = []
    for s in range(4):
        at = part(coordinate(AT_X) ^ s, rows)
        loads.append(pltpu.make_async_copy(s_hbm.at[at, :], s_ref.at[at, :], sems.at[s]))
        loads[s].start()
    load_w.wait()
    half[...] = w_held[...].astype(BF)
    own_ref[...] = w_held[part(coordinate(AT_CORE) * 4 + coordinate(AT_Y), width), :].T
    for s, out in enumerate((p0, p1, p2, p3)):
        loads[s].wait()
        at = part(coordinate(AT_X) ^ s, rows)
        out[...] = jnp.dot(s_ref[at, :], half[...], preferred_element_type=F32).astype(out.dtype)


def load_kernel(s_hbm, after, s_ref, sems):
    rows = s_ref.shape[0] // 4
    loads = [pltpu.make_async_copy(s_hbm.at[part(i, rows), :], s_ref.at[part(i, rows), :], sems.at[i]) for i in range(4)]
    for load in loads:
        load.start()
    for load in loads:
        load.wait()


def half_product(other, s_ref, pieces, held):
    half = held.shape[1]
    for s, piece in enumerate(pieces):
        held[:, part(coordinate(AT_Y) ^ s, half // 4)] = piece[...]
    columns = part(coordinate(AT_CORE) ^ other, half)
    return lax.dot_general(s_ref[:, columns], held[...], (((1,), (1,)), ((), ())), preferred_element_type=F32)


def own_half_kernel(s_ref, w0, w1, w2, w3, acc_ref, held):
    acc_ref[...] = half_product(0, s_ref, (w0, w1, w2, w3), held)


def other_half_kernel(s_ref, acc_ref, w0, w1, w2, w3, p0, p1, p2, p3, held, acc):
    acc[...] = acc_ref[...] + half_product(1, s_ref, (w0, w1, w2, w3), held)
    cut(acc, (p0, p1, p2, p3))


def sum_kernel(p0, g1, g2, g3, sum_ref, half_ref):
    total = (p0[...] + g1[...].astype(F32)) + (g2[...].astype(F32) + g3[...].astype(F32))
    sum_ref[...] = total
    half_ref[...] = total.astype(BF)


def residual_kernel(scale, q_ref, z1, z2, z3, t_ref, half_ref, *own):
    rows = q_ref.shape[0]
    total = (q_ref[...] + z1[...].astype(F32)) + (z2[...].astype(F32) + z3[...].astype(F32))
    residual = total * scale - t_ref[part(coordinate(AT_X), rows), :]
    half_ref[...] = residual.T.astype(BF)
    if own:
        own_ref, held = own
        held[...] = residual
        own_ref[...] = held[part(coordinate(AT_ZHI), own_ref.shape[0]), :]


def gradient_kernel(other, s_ref, r0, r1, r2, r3, out_ref, held):
    rows, half = r0.shape[1], out_ref.shape[1]
    for s, piece in enumerate((r0, r1, r2, r3)):
        held[:, part(coordinate(AT_X) ^ s, rows)] = piece[...]
    columns = part(coordinate(AT_CORE) ^ other, half)
    out_ref[...] = jnp.dot(held[...], s_ref[:, columns], preferred_element_type=F32).astype(out_ref.dtype)


def join_kernel(kept, got, p0, p1, p2, p3):
    width = p0.shape[1]
    for s, out in enumerate((p0, p1, p2, p3)):
        at = part(coordinate(AT_Y) ^ s, width)
        out[...] = (kept[:, at] + got[:, at].astype(F32)).astype(out.dtype)


def half_kernel(p0, g1, g2, g3, half_ref):
    total = (p0[...] + g1[...].astype(F32)) + (g2[...].astype(F32) + g3[...].astype(F32))
    half_ref[...] = total.astype(BF)


def update_kernel(factor, limit_value, kept, got, fitted_ref, new_ref, half_ref):
    gradient = kept[...].astype(F32) + got[...].astype(F32)
    fitted = shrink(fitted_ref[...] - factor * gradient, limit_value)
    new_ref[...] = fitted
    half_ref[...] = fitted.astype(BF)


def place_kernel(other, *refs):
    out_hbm, held, sems = refs[-3:]
    width = held.shape[1]
    copies = []
    for s, piece in enumerate(refs[:4]):
        held[s] = piece[...].astype(F32).T
        rows = part((coordinate(AT_CORE) ^ other) * 4 + (coordinate(AT_Y) ^ s), width)
        copies.append(pltpu.make_async_copy(held.at[s], out_hbm.at[rows, :], sems.at[s]))
        copies[-1].start()
    for copy in copies:
        copy.wait()


def body(signs, targets, weights):
    run_dev, blk_dev = signs.shape
    k = weights.shape[1]
    total_runs = run_dev * lax.axis_size("runs")
    total_blocks = blk_dev * lax.axis_size("blocks")
    scale_factor = 1.0 / math.sqrt(total_blocks)
    step_size = 1.0 / (1.0 + math.sqrt(total_runs / total_blocks)) ** 2
    limit_value = 0.5 * step_size
    rows, width, share = run_dev // 4, blk_dev // 8, run_dev // lax.axis_size("blocks")
    flops = 2 * run_dev * blk_dev * k
    chunk, chunk_half = shape((rows, k), F32), shape((rows, k), BF)
    piece, piece_half = shape((k, width), F32), shape((k, width), BF)
    cuts = [chunk] + [chunk_half] * 3
    acc, acc_held, w_held = shape((run_dev, k), F32), pltpu.VMEM((run_dev, k), F32), pltpu.VMEM((k, blk_dev // 2), BF)

    def load(after):
        (loaded,) = call(
            load_kernel, "load", [signs, after], [pltpu.VMEM(signs.shape, BF)],
            [pltpu.SemaphoreType.DMA((4,))], in_hbm=(0,),
        )
        return loaded

    def step(pieces, fitted_own, last):
        got = swap4(pieces, "blocks", X_UNIT)
        summed, half = call(sum_kernel, "sum", [pieces[0], *got], [chunk, chunk_half])
        got = swap4([half] * 4, "blocks", ZHI_UNIT)
        loaded = load(half)
        half, *residual_own = call(
            functools.partial(residual_kernel, scale_factor), "residual", [summed, *got, targets],
            [shape((k, rows), BF)] + [shape((share, k), F32)] * last, [pltpu.VMEM((rows, k), F32)] * last,
        )
        halves = [half] + swap4([half] * 4, "blocks", X_UNIT)
        held = [pltpu.VMEM((k, run_dev), BF)]
        (sent,) = call(
            functools.partial(gradient_kernel, 1), "gradient_sent", [loaded, *halves],
            [shape((k, blk_dev // 2), BF)], held, flops // 2, in_vmem=(0,),
        )
        got = swap(sent, "runs", CORE_UNIT)
        (kept,) = call(
            functools.partial(gradient_kernel, 0), "gradient_kept", [loaded, *halves],
            [shape((k, blk_dev // 2), F32)], held, flops // 2, in_vmem=(0,),
        )
        pieces = call(join_kernel, "join", [kept, got], [piece] + [piece_half] * 3)
        got = swap4(pieces, "runs", Y_UNIT)
        (half,) = call(half_kernel, "half", [pieces[0], *got], [piece_half])
        got = swap(half, "runs", ZLO_UNIT)
        fitted_own, half = call(
            functools.partial(update_kernel, step_size * scale_factor, limit_value), "update",
            [half, got, fitted_own], [piece, piece_half], aliases={2: 0},
        )
        near = [half] + swap4([half] * 4, "runs", Y_UNIT)
        far = [swap(array, "runs", CORE_UNIT) for array in near]
        return near, far, fitted_own, residual_own, loaded

    def iterate(state):
        turn, pieces, fitted_own = state
        near, far, fitted_own, _, loaded = step(pieces, fitted_own, False)
        (partial,) = call(
            own_half_kernel, "own_half", [loaded, *near], [acc], [w_held], flops // 2, in_vmem=(0,)
        )
        pieces = call(
            other_half_kernel, "other_half", [loaded, partial, *far], cuts, [w_held, acc_held], flops // 2,
            in_vmem=(0,),
        )
        turn, pieces = lax.optimization_barrier((turn, list(pieces)))
        return turn + 1, pieces, fitted_own

    *pieces, fitted_own = call(
        first_kernel, "first", [signs, weights], [*cuts, piece],
        [
            pltpu.VMEM(signs.shape, BF), pltpu.VMEM((blk_dev, k), F32), pltpu.VMEM((blk_dev, k), BF),
            pltpu.SemaphoreType.DMA((5,)),
        ],
        flops, in_hbm=(0, 1),
    )
    _, pieces, fitted_own = lax.while_loop(
        lambda state: state[0] < ITERS - 1, iterate, (jnp.int32(0), pieces, fitted_own)
    )
    near, far, _, residual_own, _ = step(pieces, fitted_own, True)
    held = [pltpu.VMEM((4, width, k), F32), pltpu.SemaphoreType.DMA((4,))]
    whole = [shape((blk_dev, k), F32)]
    fitted = call(functools.partial(place_kernel, 0), "place_near", near, whole, held, outs_in_hbm=True)
    (fitted,) = call(
        functools.partial(place_kernel, 1), "place_far", [*far, *fitted], whole, held,
        in_hbm=(4,), outs_in_hbm=True, aliases={4: 0},
    )
    return (fitted, residual_own[0])


def solution(mesh):
    in_specs = (P("runs", "blocks"), P("runs", None), P("blocks", None))
    out_specs = (P("blocks", None), P(("runs", "blocks"), None))
    return jax.shard_map(body, mesh=mesh, in_specs=in_specs, out_specs=out_specs, check_vma=False)
```

time: 193 us -> 179 us (0.927)
  Pallas kernels: 41.1 us -> 24.5 us
  starting transfers between devices: 92.8 us -> 98.8 us
  waiting for transfers between devices: 57.3 us -> 54 us
    pallas_call x31, Pallas kernels: 41.1 us -> 24.5 us  [call(): pl.pallas_call(kernel, in_specs=[hbm if i in in_hbm else vmem for i in ra...]
    ppermute x63, starting transfers between devices: 92.8 us -> 98.8 us  [swap(): lax.ppermute(array, axis, [(i, i ^ flip) for i in range(lax.axis_size(axi...]
    ppermute x63, waiting for transfers between devices: 57.3 us -> 54 us  [swap(): lax.ppermute(array, axis, [(i, i ^ flip) for i in range(lax.axis_size(axi...]
  transfers between devices with their start and end apart: 63 -> 63, of which waited for: 27 -> 28; matrix products, arithmetic and copies ran while one was open for 0% -> 0% of each run, Pallas kernels for 9% -> 8%
where the time goes in v2:
time: 179 us
  starting transfers between devices  98.8 us (55%)
  waiting for transfers between devices  54 us (30%)
  Pallas kernels  24.5 us (14%)
    ppermute x63, starting transfers between devices, swap(): lax.ppermute(array, axis, [(i, i ^ flip) for i in range(lax.axis_size(axi...  98.8 us
    ppermute x63, waiting for transfers between devices, swap(): lax.ppermute(array, axis, [(i, i ^ flip) for i in range(lax.axis_size(axi...  54 us
    pallas_call x31, Pallas kernels, call(): pl.pallas_call(kernel, in_specs=[hbm if i in in_hbm else vmem for i in ra...  24.5 us
  transfers between devices with their start and end apart: 63, of which 28 were waited for; matrix products, arithmetic and copies ran while one was open for 0% of the time, Pallas kernels for 8%

profile of v2, /device:TPU:1, one launch (start us, length us, event | category | flops | bytes accessed | tf_op | source)
XLA Modules:
  0.0 178.7 jit_solution(18361503347424969654)
XLA Ops:
  0.6 4.2 %first.1 = (f32[256,128]{1,0:T(8,128)S(1)}, bf16[256,128]{1,0:T(8,128)(2,1)S(1)}, bf16[256,128]{1,0:T(8,128)(2,1)S(1)}, bf16[256,128]{1,0:T(8,128)(2,1)S(1)}, f32[128,384]{1,0:T(8,128)S(1)}) custom-call(bf16[1024,3072]{1,0:T(8,128)(2,1)} %s_hbm.3, f32[3072,128]{1,0:T(8,128)} %w_hbm.1), custom_call_target="tpu_custom_call" | custom-call | flops 805306368 | bytes 8388608 | tf_op jit(solution)/shard_map/first/pallas_call | solution.py:48
  4.9 117.3 %while.18 = (s32[]{:T(128)}, f32[256,128]{1,0:T(8,128)S(1)}, bf16[256,128]{1,0:T(8,128)(2,1)S(1)}, bf16[256,128]{1,0:T(8,128)(2,1)S(1)}, bf16[256,128]{1,0:T(8,1...) while((s32[]{:T(128)}, f32[256,128]{1,0:T(8,128)S(1)}, ...), condition=%wide.region_1.0_spmd, body=%wide.region_0.0_spmd.sunk | while | flops 1610612736 | bytes 54330276 | solution.py:250
  4.9 3.4 %collective-permute-start.2 = (bf16[256,128]{1,0:T(8,128)(2,1)S(1)}, bf16[256,128]{1,0:T(8,128)(2,1)S(1)}, u32[]{:S(2)}, u32[]{:S(2)}) collective-permute-start(bf16[256,128]{1,0:T(8,128)(2,1)S(1)} %get-tuple-element.210), channel_id=1, source_target_pairs={{0,12},{1,13},{2,14},{3,15},{4,8},{5,9},{6,10},{7,11},{8,4},{9,5},... | collective-permute-start | bytes 196616 | tf_op jit(solution)/shard_map/while/body/ppermute | solution.py:33
  10.0 3.0 %collective-permute-done.1.g2 = bf16[256,128]{1,0:T(8,128)(2,1)S(1)} collective-permute-done((bf16[256,128]{1,0:T(8,128)(2,1)S(1)}, bf16[256,128]{1,0:T(8,128)(2,1)S(1)}, u32[]{:S(2)}, u32[]{:S(2)}) %collective-permute-start.1) | collective-permute-done | bytes 65568 | tf_op jit(solution)/shard_map/while/body/ppermute | solution.py:33
  13.0 6.0 %collective-permute-start.5 = (bf16[256,128]{1,0:T(8,128)(2,1)S(1)}, bf16[256,128]{1,0:T(8,128)(2,1)S(1)}, u32[]{:S(2)}, u32[]{:S(2)}) collective-permute-start(bf16[256,128]{1,0:T(8,128)(2,1)S(1)} %get-tuple-element.180.after), channel_id=1, source_target_pairs={{0,3},{1,2},{2,1},{3,0},{4,7},{5,6},{6,5},{7,4},{8,11},{9,10},{10,... | collective-permute-start | bytes 196616 | tf_op jit(solution)/shard_map/while/body/ppermute | solution.py:33
  20.1 1.2 collective-permute-start.3
  21.3 5.4 %collective-permute-done.4.z2 = bf16[256,128]{1,0:T(8,128)(2,1)S(1)} collective-permute-done((bf16[256,128]{1,0:T(8,128)(2,1)S(1)}, bf16[256,128]{1,0:T(8,128)(2,1)S(1)}, u32[]{:S(2)}, u32[]{:S(2)}) %collective-permute-start.4) | collective-permute-done | bytes 65568 | tf_op jit(solution)/shard_map/while/body/ppermute | solution.py:33
  26.8 1.4 collective-permute-start.8
  30.1 2.9 %load.3.s_ref = bf16[1024,3072]{1,0:T(8,128)(2,1)S(1)} custom-call(bf16[1024,3072]{1,0:T(8,128)(2,1)} %get-tuple-element.221.s_hbm, bf16[256,128]{1,0:T(8,128)(2,1)S(1)} %get-tuple-element.180.after), custom_call_target="tpu_custom_call" | custom-call | bytes 12648448 | tf_op jit(solution)/shard_map/while/body/load/pallas_call | solution.py:48
  33.6 4.5 %collective-permute-start.9 = (bf16[128,1536]{1,0:T(8,128)(2,1)S(1)}, bf16[128,1536]{1,0:T(8,128)(2,1)S(1)}, u32[]{:S(2)}, u32[]{:S(2)}) collective-permute-start(bf16[128,1536]{1,0:T(8,128)(2,1)S(1)} %gradient_sent.3), channel_id=1, source_target_pairs={{0,16},{16,0},{32,48},{48,32},{64,80},{80,64},{96,112},{112,96},{1... | collective-permute-start | bytes 1179656 | tf_op jit(solution)/shard_map/while/body/ppermute | solution.py:33
  39.6 1.4 collective-permute-start.10
  40.9 2.6 %collective-permute-start.11 = (bf16[128,384]{1,0:T(8,128)(2,1)S(1)}, bf16[128,384]{1,0:T(8,128)(2,1)S(1)}, u32[]{:S(2)}, u32[]{:S(2)}) collective-permute-start(bf16[128,384]{1,0:T(8,128)(2,1)S(1)} %get-tuple-element.184), channel_id=1, source_target_pairs={{0,128},{16,144},{32,160},{48,176},{64,192},{80,208},{96,224},{112... | collective-permute-start | bytes 294920 | tf_op jit(solution)/shard_map/while/body/ppermute | solution.py:33
  43.7 4.6 %collective-permute-done.11.g2 = bf16[128,384]{1,0:T(8,128)(2,1)S(1)} collective-permute-done((bf16[128,384]{1,0:T(8,128)(2,1)S(1)}, bf16[128,384]{1,0:T(8,128)(2,1)S(1)}, u32[]{:S(2)}, u32[]{:S(2)}) %collective-permute-start.11) | collective-permute-done | bytes 98336 | tf_op jit(solution)/shard_map/while/body/ppermute | solution.py:33
  48.2 2.6 %collective-permute-done.12.g3 = bf16[128,384]{1,0:T(8,128)(2,1)S(1)} collective-permute-done((bf16[128,384]{1,0:T(8,128)(2,1)S(1)}, bf16[128,384]{1,0:T(8,128)(2,1)S(1)}, u32[]{:S(2)}, u32[]{:S(2)}) %collective-permute-start.12) | collective-permute-done | bytes 98336 | tf_op jit(solution)/shard_map/while/body/ppermute | solution.py:33
  51.7 2.7 %collective-permute-done.13.got = bf16[128,384]{1,0:T(8,128)(2,1)S(1)} collective-permute-done((bf16[128,384]{1,0:T(8,128)(2,1)S(1)}, bf16[128,384]{1,0:T(8,128)(2,1)S(1)}, u32[]{:S(2)}, u32[]{:S(2)}) %collective-permute-start.13) | collective-permute-done | bytes 98336 | tf_op jit(solution)/shard_map/while/body/ppermute | solution.py:33
  55.4 2.5 %collective-permute-start.14 = (bf16[128,384]{1,0:T(8,128)(2,1)S(1)}, bf16[128,384]{1,0:T(8,128)(2,1)S(1)}, u32[]{:S(2)}, u32[]{:S(2)}) collective-permute-start(bf16[128,384]{1,0:T(8,128)(2,1)S(1)} %get-tuple-element.186.w0), channel_id=1, source_target_pairs={{0,64},{16,80},{32,96},{48,112},{64,0},{80,16},{96,32},{112,48},{1... | collective-permute-start | bytes 294920 | tf_op jit(solution)/shard_map/while/body/ppermute | solution.py:33
  57.9 2.6 %collective-permute-start.17 = (bf16[128,384]{1,0:T(8,128)(2,1)S(1)}, bf16[128,384]{1,0:T(8,128)(2,1)S(1)}, u32[]{:S(2)}, u32[]{:S(2)}) collective-permute-start(bf16[128,384]{1,0:T(8,128)(2,1)S(1)} %get-tuple-element.186.w0), channel_id=1, source_target_pairs={{0,16},{16,0},{32,48},{48,32},{64,80},{80,64},{96,112},{112,96},{1... | collective-permute-start | bytes 294920 | tf_op jit(solution)/shard_map/while/body/ppermute | solution.py:33
  60.5 2.8 %collective-permute-start.20 = (bf16[128,384]{1,0:T(8,128)(2,1)S(1)}, bf16[128,384]{1,0:T(8,128)(2,1)S(1)}, u32[]{:S(2)}, u32[]{:S(2)}) collective-permute-start(bf16[128,384]{1,0:T(8,128)(2,1)S(1)} %collective-permute-done.16.w3), channel_id=1, source_target_pairs={{0,16},{16,0},{32,48},{48,32},{64,80},{80,64},{96,112},{112,96},{1... | collective-permute-start | bytes 294920 | tf_op jit(solution)/shard_map/while/body/ppermute | solution.py:33
  65.2 1.1 other_half.1
  66.3 1.7 collective-permute-start.2
  68.0 1.1 collective-permute-start.1
  69.6 1.1 collective-permute-done.2.g3
  70.7 1.9 %collective-permute-done.1.g2 = bf16[256,128]{1,0:T(8,128)(2,1)S(1)} collective-permute-done((bf16[256,128]{1,0:T(8,128)(2,1)S(1)}, bf16[256,128]{1,0:T(8,128)(2,1)S(1)}, u32[]{:S(2)}, u32[]{:S(2)}) %collective-permute-start.1) | collective-permute-done | bytes 65568 | tf_op jit(solution)/shard_map/while/body/ppermute | solution.py:33
  72.9 1.8 %collective-permute-start.5 = (bf16[256,128]{1,0:T(8,128)(2,1)S(1)}, bf16[256,128]{1,0:T(8,128)(2,1)S(1)}, u32[]{:S(2)}, u32[]{:S(2)}) collective-permute-start(bf16[256,128]{1,0:T(8,128)(2,1)S(1)} %get-tuple-element.180.after), channel_id=1, source_target_pairs={{0,3},{1,2},{2,1},{3,0},{4,7},{5,6},{6,5},{7,4},{8,11},{9,10},{10,... | collective-permute-start | bytes 196616 | tf_op jit(solution)/shard_map/while/body/ppermute | solution.py:33
  74.7 2.5 %collective-permute-start.4 = (bf16[256,128]{1,0:T(8,128)(2,1)S(1)}, bf16[256,128]{1,0:T(8,128)(2,1)S(1)}, u32[]{:S(2)}, u32[]{:S(2)}) collective-permute-start(bf16[256,128]{1,0:T(8,128)(2,1)S(1)} %get-tuple-element.180.after), channel_id=1, source_target_pairs={{0,2},{1,3},{2,0},{3,1},{4,6},{5,7},{6,4},{7,5},{8,10},{9,11},{10,... | collective-permute-start | bytes 196616 | tf_op jit(solution)/shard_map/while/body/ppermute | solution.py:33
  77.2 1.5 collective-permute-start.3
  78.6 3.2 %collective-permute-done.4.z2 = bf16[256,128]{1,0:T(8,128)(2,1)S(1)} collective-permute-done((bf16[256,128]{1,0:T(8,128)(2,1)S(1)}, bf16[256,128]{1,0:T(8,128)(2,1)S(1)}, u32[]{:S(2)}, u32[]{:S(2)}) %collective-permute-start.4) | collective-permute-done | bytes 65568 | tf_op jit(solution)/shard_map/while/body/ppermute | solution.py:33
  81.9 1.5 collective-permute-start.8
  83.4 5.2 %collective-permute-start.7 = (bf16[128,256]{1,0:T(8,128)(2,1)S(1)}, bf16[128,256]{1,0:T(8,128)(2,1)S(1)}, u32[]{:S(2)}, u32[]{:S(2)}) collective-permute-start(bf16[128,256]{1,0:T(8,128)(2,1)S(1)} %residual.3.r0), channel_id=1, source_target_pairs={{0,8},{1,9},{2,10},{3,11},{4,12},{5,13},{6,14},{7,15},{8,0},{9,1},... | collective-permute-start | bytes 196616 | tf_op jit(solution)/shard_map/while/body/ppermute | solution.py:33
  88.6 2.9 %load.3.s_ref = bf16[1024,3072]{1,0:T(8,128)(2,1)S(1)} custom-call(bf16[1024,3072]{1,0:T(8,128)(2,1)} %get-tuple-element.221.s_hbm, bf16[256,128]{1,0:T(8,128)(2,1)S(1)} %get-tuple-element.180.after), custom_call_target="tpu_custom_call" | custom-call | bytes 12648448 | tf_op jit(solution)/shard_map/while/body/load/pallas_call | solution.py:48
  92.5 2.6 %collective-permute-start.9 = (bf16[128,1536]{1,0:T(8,128)(2,1)S(1)}, bf16[128,1536]{1,0:T(8,128)(2,1)S(1)}, u32[]{:S(2)}, u32[]{:S(2)}) collective-permute-start(bf16[128,1536]{1,0:T(8,128)(2,1)S(1)} %gradient_sent.3), channel_id=1, source_target_pairs={{0,16},{16,0},{32,48},{48,32},{64,80},{80,64},{96,112},{112,96},{1... | collective-permute-start | bytes 1179656 | tf_op jit(solution)/shard_map/while/body/ppermute | solution.py:33
  97.2 2.0 %collective-permute-start.11 = (bf16[128,384]{1,0:T(8,128)(2,1)S(1)}, bf16[128,384]{1,0:T(8,128)(2,1)S(1)}, u32[]{:S(2)}, u32[]{:S(2)}) collective-permute-start(bf16[128,384]{1,0:T(8,128)(2,1)S(1)} %get-tuple-element.184), channel_id=1, source_target_pairs={{0,128},{16,144},{32,160},{48,176},{64,192},{80,208},{96,224},{112... | collective-permute-start | bytes 294920 | tf_op jit(solution)/shard_map/while/body/ppermute | solution.py:33
  99.2 1.2 collective-permute-start.12
  100.6 3.3 %collective-permute-done.11.g2 = bf16[128,384]{1,0:T(8,128)(2,1)S(1)} collective-permute-done((bf16[128,384]{1,0:T(8,128)(2,1)S(1)}, bf16[128,384]{1,0:T(8,128)(2,1)S(1)}, u32[]{:S(2)}, u32[]{:S(2)}) %collective-permute-start.11) | collective-permute-done | bytes 98336 | tf_op jit(solution)/shard_map/while/body/ppermute | solution.py:33
  103.8 2.6 %collective-permute-done.12.g3 = bf16[128,384]{1,0:T(8,128)(2,1)S(1)} collective-permute-done((bf16[128,384]{1,0:T(8,128)(2,1)S(1)}, bf16[128,384]{1,0:T(8,128)(2,1)S(1)}, u32[]{:S(2)}, u32[]{:S(2)}) %collective-permute-start.12) | collective-permute-done | bytes 98336 | tf_op jit(solution)/shard_map/while/body/ppermute | solution.py:33
  107.0 3.0 %collective-permute-done.13.got = bf16[128,384]{1,0:T(8,128)(2,1)S(1)} collective-permute-done((bf16[128,384]{1,0:T(8,128)(2,1)S(1)}, bf16[128,384]{1,0:T(8,128)(2,1)S(1)}, u32[]{:S(2)}, u32[]{:S(2)}) %collective-permute-start.13) | collective-permute-done | bytes 98336 | tf_op jit(solution)/shard_map/while/body/ppermute | solution.py:33
  110.2 1.3 collective-permute-start.16
  111.5 2.0 %collective-permute-start.14 = (bf16[128,384]{1,0:T(8,128)(2,1)S(1)}, bf16[128,384]{1,0:T(8,128)(2,1)S(1)}, u32[]{:S(2)}, u32[]{:S(2)}) collective-permute-start(bf16[128,384]{1,0:T(8,128)(2,1)S(1)} %get-tuple-element.186.w0), channel_id=1, source_target_pairs={{0,64},{16,80},{32,96},{48,112},{64,0},{80,16},{96,32},{112,48},{1... | collective-permute-start | bytes 294920 | tf_op jit(solution)/shard_map/while/body/ppermute | solution.py:33
  113.5 2.6 %collective-permute-start.17 = (bf16[128,384]{1,0:T(8,128)(2,1)S(1)}, bf16[128,384]{1,0:T(8,128)(2,1)S(1)}, u32[]{:S(2)}, u32[]{:S(2)}) collective-permute-start(bf16[128,384]{1,0:T(8,128)(2,1)S(1)} %get-tuple-element.186.w0), channel_id=1, source_target_pairs={{0,16},{16,0},{32,48},{48,32},{64,80},{80,64},{96,112},{112,96},{1... | collective-permute-start | bytes 294920 | tf_op jit(solution)/shard_map/while/body/ppermute | solution.py:33
  116.1 2.1 %collective-permute-start.20 = (bf16[128,384]{1,0:T(8,128)(2,1)S(1)}, bf16[128,384]{1,0:T(8,128)(2,1)S(1)}, u32[]{:S(2)}, u32[]{:S(2)}) collective-permute-start(bf16[128,384]{1,0:T(8,128)(2,1)S(1)} %collective-permute-done.16.w3), channel_id=1, source_target_pairs={{0,16},{16,0},{32,48},{48,32},{64,80},{80,64},{96,112},{112,96},{1... | collective-permute-start | bytes 294920 | tf_op jit(solution)/shard_map/while/body/ppermute | solution.py:33
  118.2 1.4 collective-permute-start.19
  121.0 1.1 other_half.1
  122.9 2.3 %collective-permute-start.22 = (bf16[256,128]{1,0:T(8,128)(2,1)S(1)}, bf16[256,128]{1,0:T(8,128)(2,1)S(1)}, u32[]{:S(2)}, u32[]{:S(2)}) collective-permute-start(bf16[256,128]{1,0:T(8,128)(2,1)S(1)} %get-tuple-element.86), channel_id=1, source_target_pairs={{0,8},{1,9},{2,10},{3,11},{4,12},{5,13},{6,14},{7,15},{8,0},{9,1},... | collective-permute-start | bytes 196616 | tf_op jit(solution)/shard_map/ppermute | solution.py:33
  125.2 1.0 collective-permute-start.23
  126.2 2.0 %collective-permute-done.22.g2 = bf16[256,128]{1,0:T(8,128)(2,1)S(1)} collective-permute-done((bf16[256,128]{1,0:T(8,128)(2,1)S(1)}, bf16[256,128]{1,0:T(8,128)(2,1)S(1)}, u32[]{:S(2)}, u32[]{:S(2)}) %collective-permute-start.22) | collective-permute-done | bytes 65568 | tf_op jit(solution)/shard_map/ppermute | solution.py:33
  128.2 1.4 collective-permute-done.23.g3
  129.7 1.8 collective-permute-start.26
  131.4 2.5 %collective-permute-start.25 = (bf16[256,128]{1,0:T(8,128)(2,1)S(1)}, bf16[256,128]{1,0:T(8,128)(2,1)S(1)}, u32[]{:S(2)}, u32[]{:S(2)}) collective-permute-start(bf16[256,128]{1,0:T(8,128)(2,1)S(1)} %get-tuple-element.88.after), channel_id=1, source_target_pairs={{0,2},{1,3},{2,0},{3,1},{4,6},{5,7},{6,4},{7,5},{8,10},{9,11},{10,... | collective-permute-start | bytes 196616 | tf_op jit(solution)/shard_map/ppermute | solution.py:33
  133.9 1.5 collective-permute-start.24
  135.4 3.2 %collective-permute-done.25.z2 = bf16[256,128]{1,0:T(8,128)(2,1)S(1)} collective-permute-done((bf16[256,128]{1,0:T(8,128)(2,1)S(1)}, bf16[256,128]{1,0:T(8,128)(2,1)S(1)}, u32[]{:S(2)}, u32[]{:S(2)}) %collective-permute-start.25) | collective-permute-done | bytes 65568 | tf_op jit(solution)/shard_map/ppermute | solution.py:33
  139.2 1.5 collective-permute-start.29
  140.7 4.8 %collective-permute-start.28 = (bf16[128,256]{1,0:T(8,128)(2,1)S(1)}, bf16[128,256]{1,0:T(8,128)(2,1)S(1)}, u32[]{:S(2)}, u32[]{:S(2)}) collective-permute-start(bf16[128,256]{1,0:T(8,128)(2,1)S(1)} %get-tuple-element.90.r0), channel_id=1, source_target_pairs={{0,8},{1,9},{2,10},{3,11},{4,12},{5,13},{6,14},{7,15},{8,0},{9,1},... | collective-permute-start | bytes 196616 | tf_op jit(solution)/shard_map/ppermute | solution.py:33
  145.5 2.9 %load.2.s_ref = bf16[1024,3072]{1,0:T(8,128)(2,1)S(1)} custom-call(bf16[1024,3072]{1,0:T(8,128)(2,1)} %get-tuple-element.302, bf16[256,128]{1,0:T(8,128)(2,1)S(1)} %get-tuple-element.88.after), custom_call_target="tpu_custom_call" | custom-call | bytes 12648448 | tf_op jit(solution)/shard_map/load/pallas_call | solution.py:48
  149.8 1.7 collective-permute-start.30
  153.8 2.0 %collective-permute-start.32 = (bf16[128,384]{1,0:T(8,128)(2,1)S(1)}, bf16[128,384]{1,0:T(8,128)(2,1)S(1)}, u32[]{:S(2)}, u32[]{:S(2)}) collective-permute-start(bf16[128,384]{1,0:T(8,128)(2,1)S(1)} %get-tuple-element.93), channel_id=1, source_target_pairs={{0,128},{16,144},{32,160},{48,176},{64,192},{80,208},{96,224},{112... | collective-permute-start | bytes 294920 | tf_op jit(solution)/shard_map/ppermute | solution.py:33
  155.9 1.1 collective-permute-start.33
  157.1 3.4 %collective-permute-done.32.g2 = bf16[128,384]{1,0:T(8,128)(2,1)S(1)} collective-permute-done((bf16[128,384]{1,0:T(8,128)(2,1)S(1)}, bf16[128,384]{1,0:T(8,128)(2,1)S(1)}, u32[]{:S(2)}, u32[]{:S(2)}) %collective-permute-start.32) | collective-permute-done | bytes 98336 | tf_op jit(solution)/shard_map/ppermute | solution.py:33
  160.5 2.6 %collective-permute-done.33.g3 = bf16[128,384]{1,0:T(8,128)(2,1)S(1)} collective-permute-done((bf16[128,384]{1,0:T(8,128)(2,1)S(1)}, bf16[128,384]{1,0:T(8,128)(2,1)S(1)}, u32[]{:S(2)}, u32[]{:S(2)}) %collective-permute-start.33) | collective-permute-done | bytes 98336 | tf_op jit(solution)/shard_map/ppermute | solution.py:33
  163.7 3.0 %collective-permute-done.34.got = bf16[128,384]{1,0:T(8,128)(2,1)S(1)} collective-permute-done((bf16[128,384]{1,0:T(8,128)(2,1)S(1)}, bf16[128,384]{1,0:T(8,128)(2,1)S(1)}, u32[]{:S(2)}, u32[]{:S(2)}) %collective-permute-start.34) | collective-permute-done | bytes 98336 | tf_op jit(solution)/shard_map/ppermute | solution.py:33
  166.9 1.2 collective-permute-start.40
  168.1 2.2 %collective-permute-start.36 = (bf16[128,384]{1,0:T(8,128)(2,1)S(1)}, bf16[128,384]{1,0:T(8,128)(2,1)S(1)}, u32[]{:S(2)}, u32[]{:S(2)}) collective-permute-start(bf16[128,384]{1,0:T(8,128)(2,1)S(1)} %get-tuple-element.96.refs_0_), channel_id=1, source_target_pairs={{0,64},{16,80},{32,96},{48,112},{64,0},{80,16},{96,32},{112,48},{1... | collective-permute-start | bytes 294920 | tf_op jit(solution)/shard_map/ppermute | solution.py:33
  170.2 2.6 %collective-permute-start.35 = (bf16[128,384]{1,0:T(8,128)(2,1)S(1)}, bf16[128,384]{1,0:T(8,128)(2,1)S(1)}, u32[]{:S(2)}, u32[]{:S(2)}) collective-permute-start(bf16[128,384]{1,0:T(8,128)(2,1)S(1)} %get-tuple-element.96.refs_0_), channel_id=1, source_target_pairs={{0,16},{16,0},{32,48},{48,32},{64,80},{80,64},{96,112},{112,96},{1... | collective-permute-start | bytes 294920 | tf_op jit(solution)/shard_map/ppermute | solution.py:33
  172.8 2.0 %collective-permute-start.41 = (bf16[128,384]{1,0:T(8,128)(2,1)S(1)}, bf16[128,384]{1,0:T(8,128)(2,1)S(1)}, u32[]{:S(2)}, u32[]{:S(2)}) collective-permute-start(bf16[128,384]{1,0:T(8,128)(2,1)S(1)} %collective-permute-done.40.refs_3_), channel_id=1, source_target_pairs={{0,16},{16,0},{32,48},{48,32},{64,80},{80,64},{96,112},{112,96},{1... | collective-permute-start | bytes 294920 | tf_op jit(solution)/shard_map/ppermute | solution.py:33
  174.8 1.4 collective-permute-start.39
  (96 shorter events, 25.1 us)
Async XLA Ops:
  0.6 4.3 %copy-start = (f32[1024,128]{1,0:T(8,128)S(1)}, f32[1024,128]{1,0:T(8,128)}, u32[]{:S(2)}) copy-start(f32[1024,128]{1,0:T(8,128)} %t_ref.1) | copy-start | bytes 1572868
  4.9 5.0 %collective-permute-start.2 = (bf16[256,128]{1,0:T(8,128)(2,1)S(1)}, bf16[256,128]{1,0:T(8,128)(2,1)S(1)}, u32[]{:S(2)}, u32[]{:S(2)}) collective-permute-start(bf16[256,128]{1,0:T(8,128)(2,1)S(1)} %get-tuple-element.210), channel_id=1, source_target_pairs={{0,12},{1,13},{2,14},{3,15},{4,8},{5,9},{6,10},{7,11},{8,4},{9,5},... | collective-permute-start | bytes 196616 | tf_op jit(solution)/shard_map/while/body/ppermute | solution.py:33
  8.3 4.7 %collective-permute-start.1 = (bf16[256,128]{1,0:T(8,128)(2,1)S(1)}, bf16[256,128]{1,0:T(8,128)(2,1)S(1)}, u32[]{:S(2)}, u32[]{:S(2)}) collective-permute-start(bf16[256,128]{1,0:T(8,128)(2,1)S(1)} %get-tuple-element.209), channel_id=1, source_target_pairs={{0,8},{1,9},{2,10},{3,11},{4,12},{5,13},{6,14},{7,15},{8,0},{9,1},... | collective-permute-start | bytes 196616 | tf_op jit(solution)/shard_map/while/body/ppermute | solution.py:33
  8.8 4.2 %collective-permute-start = (bf16[256,128]{1,0:T(8,128)(2,1)S(1)}, bf16[256,128]{1,0:T(8,128)(2,1)S(1)}, u32[]{:S(2)}, u32[]{:S(2)}) collective-permute-start(bf16[256,128]{1,0:T(8,128)(2,1)S(1)} %get-tuple-element.208), channel_id=1, source_target_pairs={{0,4},{1,5},{2,6},{3,7},{4,0},{5,1},{6,2},{7,3},{8,12},{9,13},{10,... | collective-permute-start | bytes 196616 | tf_op jit(solution)/shard_map/while/body/ppermute | solution.py:33
  13.0 8.2 %collective-permute-start.5 = (bf16[256,128]{1,0:T(8,128)(2,1)S(1)}, bf16[256,128]{1,0:T(8,128)(2,1)S(1)}, u32[]{:S(2)}, u32[]{:S(2)}) collective-permute-start(bf16[256,128]{1,0:T(8,128)(2,1)S(1)} %get-tuple-element.180.after), channel_id=1, source_target_pairs={{0,3},{1,2},{2,1},{3,0},{4,7},{5,6},{6,5},{7,4},{8,11},{9,10},{10,... | collective-permute-start | bytes 196616 | tf_op jit(solution)/shard_map/while/body/ppermute | solution.py:33
  19.1 7.6 %collective-permute-start.4 = (bf16[256,128]{1,0:T(8,128)(2,1)S(1)}, bf16[256,128]{1,0:T(8,128)(2,1)S(1)}, u32[]{:S(2)}, u32[]{:S(2)}) collective-permute-start(bf16[256,128]{1,0:T(8,128)(2,1)S(1)} %get-tuple-element.180.after), channel_id=1, source_target_pairs={{0,2},{1,3},{2,0},{3,1},{4,6},{5,7},{6,4},{7,5},{8,10},{9,11},{10,... | collective-permute-start | bytes 196616 | tf_op jit(solution)/shard_map/while/body/ppermute | solution.py:33
  20.1 6.6 %collective-permute-start.3 = (bf16[256,128]{1,0:T(8,128)(2,1)S(1)}, bf16[256,128]{1,0:T(8,128)(2,1)S(1)}, u32[]{:S(2)}, u32[]{:S(2)}) collective-permute-start(bf16[256,128]{1,0:T(8,128)(2,1)S(1)} %get-tuple-element.180.after), channel_id=1, source_target_pairs={{0,1},{1,0},{2,3},{3,2},{4,5},{5,4},{6,7},{7,6},{8,9},{9,8},{10,11... | collective-permute-start | bytes 196616 | tf_op jit(solution)/shard_map/while/body/ppermute | solution.py:33
  26.8 6.2 %collective-permute-start.8 = (bf16[128,256]{1,0:T(8,128)(2,1)S(1)}, bf16[128,256]{1,0:T(8,128)(2,1)S(1)}, u32[]{:S(2)}, u32[]{:S(2)}) collective-permute-start(bf16[128,256]{1,0:T(8,128)(2,1)S(1)} %residual.3.r0), channel_id=1, source_target_pairs={{0,12},{1,13},{2,14},{3,15},{4,8},{5,9},{6,10},{7,11},{8,4},{9,5},... | collective-permute-start | bytes 196616 | tf_op jit(solution)/shard_map/while/body/ppermute | solution.py:33
  28.1 4.9 %collective-permute-start.7 = (bf16[128,256]{1,0:T(8,128)(2,1)S(1)}, bf16[128,256]{1,0:T(8,128)(2,1)S(1)}, u32[]{:S(2)}, u32[]{:S(2)}) collective-permute-start(bf16[128,256]{1,0:T(8,128)(2,1)S(1)} %residual.3.r0), channel_id=1, source_target_pairs={{0,8},{1,9},{2,10},{3,11},{4,12},{5,13},{6,14},{7,15},{8,0},{9,1},... | collective-permute-start | bytes 196616 | tf_op jit(solution)/shard_map/while/body/ppermute | solution.py:33
  29.1 3.9 %collective-permute-start.6 = (bf16[128,256]{1,0:T(8,128)(2,1)S(1)}, bf16[128,256]{1,0:T(8,128)(2,1)S(1)}, u32[]{:S(2)}, u32[]{:S(2)}) collective-permute-start(bf16[128,256]{1,0:T(8,128)(2,1)S(1)} %residual.3.r0), channel_id=1, source_target_pairs={{0,4},{1,5},{2,6},{3,7},{4,0},{5,1},{6,2},{7,3},{8,12},{9,13},{10,... | collective-permute-start | bytes 196616 | tf_op jit(solution)/shard_map/while/body/ppermute | solution.py:33
  33.6 5.8 %collective-permute-start.9 = (bf16[128,1536]{1,0:T(8,128)(2,1)S(1)}, bf16[128,1536]{1,0:T(8,128)(2,1)S(1)}, u32[]{:S(2)}, u32[]{:S(2)}) collective-permute-start(bf16[128,1536]{1,0:T(8,128)(2,1)S(1)} %gradient_sent.3), channel_id=1, source_target_pairs={{0,16},{16,0},{32,48},{48,32},{64,80},{80,64},{96,112},{112,96},{1... | collective-permute-start | bytes 1179656 | tf_op jit(solution)/shard_map/while/body/ppermute | solution.py:33
  39.6 4.1 %collective-permute-start.10 = (bf16[128,384]{1,0:T(8,128)(2,1)S(1)}, bf16[128,384]{1,0:T(8,128)(2,1)S(1)}, u32[]{:S(2)}, u32[]{:S(2)}) collective-permute-start(bf16[128,384]{1,0:T(8,128)(2,1)S(1)} %get-tuple-element.183), channel_id=1, source_target_pairs={{0,64},{16,80},{32,96},{48,112},{64,0},{80,16},{96,32},{112,48},{1... | collective-permute-start | bytes 294920 | tf_op jit(solution)/shard_map/while/body/ppermute | solution.py:33
  40.9 7.3 %collective-permute-start.11 = (bf16[128,384]{1,0:T(8,128)(2,1)S(1)}, bf16[128,384]{1,0:T(8,128)(2,1)S(1)}, u32[]{:S(2)}, u32[]{:S(2)}) collective-permute-start(bf16[128,384]{1,0:T(8,128)(2,1)S(1)} %get-tuple-element.184), channel_id=1, source_target_pairs={{0,128},{16,144},{32,160},{48,176},{64,192},{80,208},{96,224},{112... | collective-permute-start | bytes 294920 | tf_op jit(solution)/shard_map/while/body/ppermute | solution.py:33
  43.6 7.2 %collective-permute-start.12 = (bf16[128,384]{1,0:T(8,128)(2,1)S(1)}, bf16[128,384]{1,0:T(8,128)(2,1)S(1)}, u32[]{:S(2)}, u32[]{:S(2)}) collective-permute-start(bf16[128,384]{1,0:T(8,128)(2,1)S(1)} %get-tuple-element.185), channel_id=1, source_target_pairs={{0,192},{16,208},{32,224},{48,240},{64,128},{80,144},{96,160},{112... | collective-permute-start | bytes 294920 | tf_op jit(solution)/shard_map/while/body/ppermute | solution.py:33
  50.9 3.6 %collective-permute-start.13 = (bf16[128,384]{1,0:T(8,128)(2,1)S(1)}, bf16[128,384]{1,0:T(8,128)(2,1)S(1)}, u32[]{:S(2)}, u32[]{:S(2)}) collective-permute-start(bf16[128,384]{1,0:T(8,128)(2,1)S(1)} %half.3.kept), channel_id=1, source_target_pairs={{0,32},{16,48},{32,0},{48,16},{64,96},{80,112},{96,64},{112,80},{1... | collective-permute-start | bytes 294920 | tf_op jit(solution)/shard_map/while/body/ppermute | solution.py:33
  54.6 5.9 %collective-permute-start.16 = (bf16[128,384]{1,0:T(8,128)(2,1)S(1)}, bf16[128,384]{1,0:T(8,128)(2,1)S(1)}, u32[]{:S(2)}, u32[]{:S(2)}) collective-permute-start(bf16[128,384]{1,0:T(8,128)(2,1)S(1)} %get-tuple-element.186.w0), channel_id=1, source_target_pairs={{0,192},{16,208},{32,224},{48,240},{64,128},{80,144},{96,160},{112... | collective-permute-start | bytes 294920 | tf_op jit(solution)/shard_map/while/body/ppermute | solution.py:33
  55.4 7.9 %collective-permute-start.15 = (bf16[128,384]{1,0:T(8,128)(2,1)S(1)}, bf16[128,384]{1,0:T(8,128)(2,1)S(1)}, u32[]{:S(2)}, u32[]{:S(2)}) collective-permute-start(bf16[128,384]{1,0:T(8,128)(2,1)S(1)} %get-tuple-element.186.w0), channel_id=1, source_target_pairs={{0,128},{16,144},{32,160},{48,176},{64,192},{80,208},{96,224},{112... | collective-permute-start | bytes 294920 | tf_op jit(solution)/shard_map/while/body/ppermute | solution.py:33
  55.4 7.9 %collective-permute-start.14 = (bf16[128,384]{1,0:T(8,128)(2,1)S(1)}, bf16[128,384]{1,0:T(8,128)(2,1)S(1)}, u32[]{:S(2)}, u32[]{:S(2)}) collective-permute-start(bf16[128,384]{1,0:T(8,128)(2,1)S(1)} %get-tuple-element.186.w0), channel_id=1, source_target_pairs={{0,64},{16,80},{32,96},{48,112},{64,0},{80,16},{96,32},{112,48},{1... | collective-permute-start | bytes 294920 | tf_op jit(solution)/shard_map/while/body/ppermute | solution.py:33
  57.9 7.3 %collective-permute-start.17 = (bf16[128,384]{1,0:T(8,128)(2,1)S(1)}, bf16[128,384]{1,0:T(8,128)(2,1)S(1)}, u32[]{:S(2)}, u32[]{:S(2)}) collective-permute-start(bf16[128,384]{1,0:T(8,128)(2,1)S(1)} %get-tuple-element.186.w0), channel_id=1, source_target_pairs={{0,16},{16,0},{32,48},{48,32},{64,80},{80,64},{96,112},{112,96},{1... | collective-permute-start | bytes 294920 | tf_op jit(solution)/shard_map/while/body/ppermute | solution.py:33
  60.5 4.7 %collective-permute-start.20 = (bf16[128,384]{1,0:T(8,128)(2,1)S(1)}, bf16[128,384]{1,0:T(8,128)(2,1)S(1)}, u32[]{:S(2)}, u32[]{:S(2)}) collective-permute-start(bf16[128,384]{1,0:T(8,128)(2,1)S(1)} %collective-permute-done.16.w3), channel_id=1, source_target_pairs={{0,16},{16,0},{32,48},{48,32},{64,80},{80,64},{96,112},{112,96},{1... | collective-permute-start | bytes 294920 | tf_op jit(solution)/shard_map/while/body/ppermute | solution.py:33
  63.3 1.9 %collective-permute-start.19 = (bf16[128,384]{1,0:T(8,128)(2,1)S(1)}, bf16[128,384]{1,0:T(8,128)(2,1)S(1)}, u32[]{:S(2)}, u32[]{:S(2)}) collective-permute-start(bf16[128,384]{1,0:T(8,128)(2,1)S(1)} %collective-permute-done.15.w2), channel_id=1, source_target_pairs={{0,16},{16,0},{32,48},{48,32},{64,80},{80,64},{96,112},{112,96},{1... | collective-permute-start | bytes 294920 | tf_op jit(solution)/shard_map/while/body/ppermute | solution.py:33
  63.3 1.9 %collective-permute-start.18 = (bf16[128,384]{1,0:T(8,128)(2,1)S(1)}, bf16[128,384]{1,0:T(8,128)(2,1)S(1)}, u32[]{:S(2)}, u32[]{:S(2)}) collective-permute-start(bf16[128,384]{1,0:T(8,128)(2,1)S(1)} %collective-permute-done.14.w1), channel_id=1, source_target_pairs={{0,16},{16,0},{32,48},{48,32},{64,80},{80,64},{96,112},{112,96},{1... | collective-permute-start | bytes 294920 | tf_op jit(solution)/shard_map/while/body/ppermute | solution.py:33
  66.3 4.4 %collective-permute-start.2 = (bf16[256,128]{1,0:T(8,128)(2,1)S(1)}, bf16[256,128]{1,0:T(8,128)(2,1)S(1)}, u32[]{:S(2)}, u32[]{:S(2)}) collective-permute-start(bf16[256,128]{1,0:T(8,128)(2,1)S(1)} %get-tuple-element.210), channel_id=1, source_target_pairs={{0,12},{1,13},{2,14},{3,15},{4,8},{5,9},{6,10},{7,11},{8,4},{9,5},... | collective-permute-start | bytes 196616 | tf_op jit(solution)/shard_map/while/body/ppermute | solution.py:33
  68.0 4.6 %collective-permute-start.1 = (bf16[256,128]{1,0:T(8,128)(2,1)S(1)}, bf16[256,128]{1,0:T(8,128)(2,1)S(1)}, u32[]{:S(2)}, u32[]{:S(2)}) collective-permute-start(bf16[256,128]{1,0:T(8,128)(2,1)S(1)} %get-tuple-element.209), channel_id=1, source_target_pairs={{0,8},{1,9},{2,10},{3,11},{4,12},{5,13},{6,14},{7,15},{8,0},{9,1},... | collective-permute-start | bytes 196616 | tf_op jit(solution)/shard_map/while/body/ppermute | solution.py:33
  69.1 3.8 %collective-permute-start = (bf16[256,128]{1,0:T(8,128)(2,1)S(1)}, bf16[256,128]{1,0:T(8,128)(2,1)S(1)}, u32[]{:S(2)}, u32[]{:S(2)}) collective-permute-start(bf16[256,128]{1,0:T(8,128)(2,1)S(1)} %get-tuple-element.208), channel_id=1, source_target_pairs={{0,4},{1,5},{2,6},{3,7},{4,0},{5,1},{6,2},{7,3},{8,12},{9,13},{10,... | collective-permute-start | bytes 196616 | tf_op jit(solution)/shard_map/while/body/ppermute | solution.py:33
  72.9 5.7 %collective-permute-start.5 = (bf16[256,128]{1,0:T(8,128)(2,1)S(1)}, bf16[256,128]{1,0:T(8,128)(2,1)S(1)}, u32[]{:S(2)}, u32[]{:S(2)}) collective-permute-start(bf16[256,128]{1,0:T(8,128)(2,1)S(1)} %get-tuple-element.180.after), channel_id=1, source_target_pairs={{0,3},{1,2},{2,1},{3,0},{4,7},{5,6},{6,5},{7,4},{8,11},{9,10},{10,... | collective-permute-start | bytes 196616 | tf_op jit(solution)/shard_map/while/body/ppermute | solution.py:33
  74.7 7.1 %collective-permute-start.4 = (bf16[256,128]{1,0:T(8,128)(2,1)S(1)}, bf16[256,128]{1,0:T(8,128)(2,1)S(1)}, u32[]{:S(2)}, u32[]{:S(2)}) collective-permute-start(bf16[256,128]{1,0:T(8,128)(2,1)S(1)} %get-tuple-element.180.after), channel_id=1, source_target_pairs={{0,2},{1,3},{2,0},{3,1},{4,6},{5,7},{6,4},{7,5},{8,10},{9,11},{10,... | collective-permute-start | bytes 196616 | tf_op jit(solution)/shard_map/while/body/ppermute | solution.py:33
  77.2 4.7 %collective-permute-start.3 = (bf16[256,128]{1,0:T(8,128)(2,1)S(1)}, bf16[256,128]{1,0:T(8,128)(2,1)S(1)}, u32[]{:S(2)}, u32[]{:S(2)}) collective-permute-start(bf16[256,128]{1,0:T(8,128)(2,1)S(1)} %get-tuple-element.180.after), channel_id=1, source_target_pairs={{0,1},{1,0},{2,3},{3,2},{4,5},{5,4},{6,7},{7,6},{8,9},{9,8},{10,11... | collective-permute-start | bytes 196616 | tf_op jit(solution)/shard_map/while/body/ppermute | solution.py:33
  81.9 9.5 %collective-permute-start.8 = (bf16[128,256]{1,0:T(8,128)(2,1)S(1)}, bf16[128,256]{1,0:T(8,128)(2,1)S(1)}, u32[]{:S(2)}, u32[]{:S(2)}) collective-permute-start(bf16[128,256]{1,0:T(8,128)(2,1)S(1)} %residual.3.r0), channel_id=1, source_target_pairs={{0,12},{1,13},{2,14},{3,15},{4,8},{5,9},{6,10},{7,11},{8,4},{9,5},... | collective-permute-start | bytes 196616 | tf_op jit(solution)/shard_map/while/body/ppermute | solution.py:33
  83.4 8.1 %collective-permute-start.7 = (bf16[128,256]{1,0:T(8,128)(2,1)S(1)}, bf16[128,256]{1,0:T(8,128)(2,1)S(1)}, u32[]{:S(2)}, u32[]{:S(2)}) collective-permute-start(bf16[128,256]{1,0:T(8,128)(2,1)S(1)} %residual.3.r0), channel_id=1, source_target_pairs={{0,8},{1,9},{2,10},{3,11},{4,12},{5,13},{6,14},{7,15},{8,0},{9,1},... | collective-permute-start | bytes 196616 | tf_op jit(solution)/shard_map/while/body/ppermute | solution.py:33
  88.6 3.2 %collective-permute-start.6 = (bf16[128,256]{1,0:T(8,128)(2,1)S(1)}, bf16[128,256]{1,0:T(8,128)(2,1)S(1)}, u32[]{:S(2)}, u32[]{:S(2)}) collective-permute-start(bf16[128,256]{1,0:T(8,128)(2,1)S(1)} %residual.3.r0), channel_id=1, source_target_pairs={{0,4},{1,5},{2,6},{3,7},{4,0},{5,1},{6,2},{7,3},{8,12},{9,13},{10,... | collective-permute-start | bytes 196616 | tf_op jit(solution)/shard_map/while/body/ppermute | solution.py:33
  92.5 3.9 %collective-permute-start.9 = (bf16[128,1536]{1,0:T(8,128)(2,1)S(1)}, bf16[128,1536]{1,0:T(8,128)(2,1)S(1)}, u32[]{:S(2)}, u32[]{:S(2)}) collective-permute-start(bf16[128,1536]{1,0:T(8,128)(2,1)S(1)} %gradient_sent.3), channel_id=1, source_target_pairs={{0,16},{16,0},{32,48},{48,32},{64,80},{80,64},{96,112},{112,96},{1... | collective-permute-start | bytes 1179656 | tf_op jit(solution)/shard_map/while/body/ppermute | solution.py:33
  96.5 4.1 %collective-permute-start.10 = (bf16[128,384]{1,0:T(8,128)(2,1)S(1)}, bf16[128,384]{1,0:T(8,128)(2,1)S(1)}, u32[]{:S(2)}, u32[]{:S(2)}) collective-permute-start(bf16[128,384]{1,0:T(8,128)(2,1)S(1)} %get-tuple-element.183), channel_id=1, source_target_pairs={{0,64},{16,80},{32,96},{48,112},{64,0},{80,16},{96,32},{112,48},{1... | collective-permute-start | bytes 294920 | tf_op jit(solution)/shard_map/while/body/ppermute | solution.py:33
  97.2 6.6 %collective-permute-start.11 = (bf16[128,384]{1,0:T(8,128)(2,1)S(1)}, bf16[128,384]{1,0:T(8,128)(2,1)S(1)}, u32[]{:S(2)}, u32[]{:S(2)}) collective-permute-start(bf16[128,384]{1,0:T(8,128)(2,1)S(1)} %get-tuple-element.184), channel_id=1, source_target_pairs={{0,128},{16,144},{32,160},{48,176},{64,192},{80,208},{96,224},{112... | collective-permute-start | bytes 294920 | tf_op jit(solution)/shard_map/while/body/ppermute | solution.py:33
  99.2 7.2 %collective-permute-start.12 = (bf16[128,384]{1,0:T(8,128)(2,1)S(1)}, bf16[128,384]{1,0:T(8,128)(2,1)S(1)}, u32[]{:S(2)}, u32[]{:S(2)}) collective-permute-start(bf16[128,384]{1,0:T(8,128)(2,1)S(1)} %get-tuple-element.185), channel_id=1, source_target_pairs={{0,192},{16,208},{32,224},{48,240},{64,128},{80,144},{96,160},{112... | collective-permute-start | bytes 294920 | tf_op jit(solution)/shard_map/while/body/ppermute | solution.py:33
  106.5 3.6 %collective-permute-start.13 = (bf16[128,384]{1,0:T(8,128)(2,1)S(1)}, bf16[128,384]{1,0:T(8,128)(2,1)S(1)}, u32[]{:S(2)}, u32[]{:S(2)}) collective-permute-start(bf16[128,384]{1,0:T(8,128)(2,1)S(1)} %half.3.kept), channel_id=1, source_target_pairs={{0,32},{16,48},{32,0},{48,16},{64,96},{80,112},{96,64},{112,80},{1... | collective-permute-start | bytes 294920 | tf_op jit(solution)/shard_map/while/body/ppermute | solution.py:33
  110.2 5.9 %collective-permute-start.16 = (bf16[128,384]{1,0:T(8,128)(2,1)S(1)}, bf16[128,384]{1,0:T(8,128)(2,1)S(1)}, u32[]{:S(2)}, u32[]{:S(2)}) collective-permute-start(bf16[128,384]{1,0:T(8,128)(2,1)S(1)} %get-tuple-element.186.w0), channel_id=1, source_target_pairs={{0,192},{16,208},{32,224},{48,240},{64,128},{80,144},{96,160},{112... | collective-permute-start | bytes 294920 | tf_op jit(solution)/shard_map/while/body/ppermute | solution.py:33
  111.5 6.7 %collective-permute-start.15 = (bf16[128,384]{1,0:T(8,128)(2,1)S(1)}, bf16[128,384]{1,0:T(8,128)(2,1)S(1)}, u32[]{:S(2)}, u32[]{:S(2)}) collective-permute-start(bf16[128,384]{1,0:T(8,128)(2,1)S(1)} %get-tuple-element.186.w0), channel_id=1, source_target_pairs={{0,128},{16,144},{32,160},{48,176},{64,192},{80,208},{96,224},{112... | collective-permute-start | bytes 294920 | tf_op jit(solution)/shard_map/while/body/ppermute | solution.py:33
  111.5 8.2 %collective-permute-start.14 = (bf16[128,384]{1,0:T(8,128)(2,1)S(1)}, bf16[128,384]{1,0:T(8,128)(2,1)S(1)}, u32[]{:S(2)}, u32[]{:S(2)}) collective-permute-start(bf16[128,384]{1,0:T(8,128)(2,1)S(1)} %get-tuple-element.186.w0), channel_id=1, source_target_pairs={{0,64},{16,80},{32,96},{48,112},{64,0},{80,16},{96,32},{112,48},{1... | collective-permute-start | bytes 294920 | tf_op jit(solution)/shard_map/while/body/ppermute | solution.py:33
  113.5 7.3 %collective-permute-start.17 = (bf16[128,384]{1,0:T(8,128)(2,1)S(1)}, bf16[128,384]{1,0:T(8,128)(2,1)S(1)}, u32[]{:S(2)}, u32[]{:S(2)}) collective-permute-start(bf16[128,384]{1,0:T(8,128)(2,1)S(1)} %get-tuple-element.186.w0), channel_id=1, source_target_pairs={{0,16},{16,0},{32,48},{48,32},{64,80},{80,64},{96,112},{112,96},{1... | collective-permute-start | bytes 294920 | tf_op jit(solution)/shard_map/while/body/ppermute | solution.py:33
  116.1 4.7 %collective-permute-start.20 = (bf16[128,384]{1,0:T(8,128)(2,1)S(1)}, bf16[128,384]{1,0:T(8,128)(2,1)S(1)}, u32[]{:S(2)}, u32[]{:S(2)}) collective-permute-start(bf16[128,384]{1,0:T(8,128)(2,1)S(1)} %collective-permute-done.16.w3), channel_id=1, source_target_pairs={{0,16},{16,0},{32,48},{48,32},{64,80},{80,64},{96,112},{112,96},{1... | collective-permute-start | bytes 294920 | tf_op jit(solution)/shard_map/while/body/ppermute | solution.py:33
  118.2 2.6 %collective-permute-start.19 = (bf16[128,384]{1,0:T(8,128)(2,1)S(1)}, bf16[128,384]{1,0:T(8,128)(2,1)S(1)}, u32[]{:S(2)}, u32[]{:S(2)}) collective-permute-start(bf16[128,384]{1,0:T(8,128)(2,1)S(1)} %collective-permute-done.15.w2), channel_id=1, source_target_pairs={{0,16},{16,0},{32,48},{48,32},{64,80},{80,64},{96,112},{112,96},{1... | collective-permute-start | bytes 294920 | tf_op jit(solution)/shard_map/while/body/ppermute | solution.py:33
  119.7 1.3 collective-permute-start.18
  122.3 3.9 %collective-permute-start.21 = (bf16[256,128]{1,0:T(8,128)(2,1)S(1)}, bf16[256,128]{1,0:T(8,128)(2,1)S(1)}, u32[]{:S(2)}, u32[]{:S(2)}) collective-permute-start(bf16[256,128]{1,0:T(8,128)(2,1)S(1)} %get-tuple-element.85), channel_id=1, source_target_pairs={{0,4},{1,5},{2,6},{3,7},{4,0},{5,1},{6,2},{7,3},{8,12},{9,13},{10,... | collective-permute-start | bytes 196616 | tf_op jit(solution)/shard_map/ppermute | solution.py:33
  122.9 5.3 %collective-permute-start.22 = (bf16[256,128]{1,0:T(8,128)(2,1)S(1)}, bf16[256,128]{1,0:T(8,128)(2,1)S(1)}, u32[]{:S(2)}, u32[]{:S(2)}) collective-permute-start(bf16[256,128]{1,0:T(8,128)(2,1)S(1)} %get-tuple-element.86), channel_id=1, source_target_pairs={{0,8},{1,9},{2,10},{3,11},{4,12},{5,13},{6,14},{7,15},{8,0},{9,1},... | collective-permute-start | bytes 196616 | tf_op jit(solution)/shard_map/ppermute | solution.py:33
  125.2 4.5 %collective-permute-start.23 = (bf16[256,128]{1,0:T(8,128)(2,1)S(1)}, bf16[256,128]{1,0:T(8,128)(2,1)S(1)}, u32[]{:S(2)}, u32[]{:S(2)}) collective-permute-start(bf16[256,128]{1,0:T(8,128)(2,1)S(1)} %get-tuple-element.87), channel_id=1, source_target_pairs={{0,12},{1,13},{2,14},{3,15},{4,8},{5,9},{6,10},{7,11},{8,4},{9,5},... | collective-permute-start | bytes 196616 | tf_op jit(solution)/shard_map/ppermute | solution.py:33
  129.7 5.7 %collective-permute-start.26 = (bf16[256,128]{1,0:T(8,128)(2,1)S(1)}, bf16[256,128]{1,0:T(8,128)(2,1)S(1)}, u32[]{:S(2)}, u32[]{:S(2)}) collective-permute-start(bf16[256,128]{1,0:T(8,128)(2,1)S(1)} %get-tuple-element.88.after), channel_id=1, source_target_pairs={{0,3},{1,2},{2,1},{3,0},{4,7},{5,6},{6,5},{7,4},{8,11},{9,10},{10,... | collective-permute-start | bytes 196616 | tf_op jit(solution)/shard_map/ppermute | solution.py:33
  131.4 7.1 %collective-permute-start.25 = (bf16[256,128]{1,0:T(8,128)(2,1)S(1)}, bf16[256,128]{1,0:T(8,128)(2,1)S(1)}, u32[]{:S(2)}, u32[]{:S(2)}) collective-permute-start(bf16[256,128]{1,0:T(8,128)(2,1)S(1)} %get-tuple-element.88.after), channel_id=1, source_target_pairs={{0,2},{1,3},{2,0},{3,1},{4,6},{5,7},{6,4},{7,5},{8,10},{9,11},{10,... | collective-permute-start | bytes 196616 | tf_op jit(solution)/shard_map/ppermute | solution.py:33
  133.9 4.7 %collective-permute-start.24 = (bf16[256,128]{1,0:T(8,128)(2,1)S(1)}, bf16[256,128]{1,0:T(8,128)(2,1)S(1)}, u32[]{:S(2)}, u32[]{:S(2)}) collective-permute-start(bf16[256,128]{1,0:T(8,128)(2,1)S(1)} %get-tuple-element.88.after), channel_id=1, source_target_pairs={{0,1},{1,0},{2,3},{3,2},{4,5},{5,4},{6,7},{7,6},{8,9},{9,8},{10,11... | collective-permute-start | bytes 196616 | tf_op jit(solution)/shard_map/ppermute | solution.py:33
  139.2 9.2 %collective-permute-start.29 = (bf16[128,256]{1,0:T(8,128)(2,1)S(1)}, bf16[128,256]{1,0:T(8,128)(2,1)S(1)}, u32[]{:S(2)}, u32[]{:S(2)}) collective-permute-start(bf16[128,256]{1,0:T(8,128)(2,1)S(1)} %get-tuple-element.90.r0), channel_id=1, source_target_pairs={{0,12},{1,13},{2,14},{3,15},{4,8},{5,9},{6,10},{7,11},{8,4},{9,5},... | collective-permute-start | bytes 196616 | tf_op jit(solution)/shard_map/ppermute | solution.py:33
  140.7 7.7 %collective-permute-start.28 = (bf16[128,256]{1,0:T(8,128)(2,1)S(1)}, bf16[128,256]{1,0:T(8,128)(2,1)S(1)}, u32[]{:S(2)}, u32[]{:S(2)}) collective-permute-start(bf16[128,256]{1,0:T(8,128)(2,1)S(1)} %get-tuple-element.90.r0), channel_id=1, source_target_pairs={{0,8},{1,9},{2,10},{3,11},{4,12},{5,13},{6,14},{7,15},{8,0},{9,1},... | collective-permute-start | bytes 196616 | tf_op jit(solution)/shard_map/ppermute | solution.py:33
  145.5 3.7 %collective-permute-start.27 = (bf16[128,256]{1,0:T(8,128)(2,1)S(1)}, bf16[128,256]{1,0:T(8,128)(2,1)S(1)}, u32[]{:S(2)}, u32[]{:S(2)}) collective-permute-start(bf16[128,256]{1,0:T(8,128)(2,1)S(1)} %get-tuple-element.90.r0), channel_id=1, source_target_pairs={{0,4},{1,5},{2,6},{3,7},{4,0},{5,1},{6,2},{7,3},{8,12},{9,13},{10,... | collective-permute-start | bytes 196616 | tf_op jit(solution)/shard_map/ppermute | solution.py:33
  149.8 3.1 %collective-permute-start.30 = (bf16[128,1536]{1,0:T(8,128)(2,1)S(1)}, bf16[128,1536]{1,0:T(8,128)(2,1)S(1)}, u32[]{:S(2)}, u32[]{:S(2)}) collective-permute-start(bf16[128,1536]{1,0:T(8,128)(2,1)S(1)} %gradient_sent.2), channel_id=1, source_target_pairs={{0,16},{16,0},{32,48},{48,32},{64,80},{80,64},{96,112},{112,96},{1... | collective-permute-start | bytes 1179656 | tf_op jit(solution)/shard_map/ppermute | solution.py:33
  153.0 4.1 %collective-permute-start.31 = (bf16[128,384]{1,0:T(8,128)(2,1)S(1)}, bf16[128,384]{1,0:T(8,128)(2,1)S(1)}, u32[]{:S(2)}, u32[]{:S(2)}) collective-permute-start(bf16[128,384]{1,0:T(8,128)(2,1)S(1)} %get-tuple-element.92), channel_id=1, source_target_pairs={{0,64},{16,80},{32,96},{48,112},{64,0},{80,16},{96,32},{112,48},{1... | collective-permute-start | bytes 294920 | tf_op jit(solution)/shard_map/ppermute | solution.py:33
  153.8 6.7 %collective-permute-start.32 = (bf16[128,384]{1,0:T(8,128)(2,1)S(1)}, bf16[128,384]{1,0:T(8,128)(2,1)S(1)}, u32[]{:S(2)}, u32[]{:S(2)}) collective-permute-start(bf16[128,384]{1,0:T(8,128)(2,1)S(1)} %get-tuple-element.93), channel_id=1, source_target_pairs={{0,128},{16,144},{32,160},{48,176},{64,192},{80,208},{96,224},{112... | collective-permute-start | bytes 294920 | tf_op jit(solution)/shard_map/ppermute | solution.py:33
  155.9 7.2 %collective-permute-start.33 = (bf16[128,384]{1,0:T(8,128)(2,1)S(1)}, bf16[128,384]{1,0:T(8,128)(2,1)S(1)}, u32[]{:S(2)}, u32[]{:S(2)}) collective-permute-start(bf16[128,384]{1,0:T(8,128)(2,1)S(1)} %get-tuple-element.94), channel_id=1, source_target_pairs={{0,192},{16,208},{32,224},{48,240},{64,128},{80,144},{96,160},{112... | collective-permute-start | bytes 294920 | tf_op jit(solution)/shard_map/ppermute | solution.py:33
  163.2 3.6 %collective-permute-start.34 = (bf16[128,384]{1,0:T(8,128)(2,1)S(1)}, bf16[128,384]{1,0:T(8,128)(2,1)S(1)}, u32[]{:S(2)}, u32[]{:S(2)}) collective-permute-start(bf16[128,384]{1,0:T(8,128)(2,1)S(1)} %half.2.kept), channel_id=1, source_target_pairs={{0,32},{16,48},{32,0},{48,16},{64,96},{80,112},{96,64},{112,80},{1... | collective-permute-start | bytes 294920 | tf_op jit(solution)/shard_map/ppermute | solution.py:33
  166.9 5.9 %collective-permute-start.40 = (bf16[128,384]{1,0:T(8,128)(2,1)S(1)}, bf16[128,384]{1,0:T(8,128)(2,1)S(1)}, u32[]{:S(2)}, u32[]{:S(2)}) collective-permute-start(bf16[128,384]{1,0:T(8,128)(2,1)S(1)} %get-tuple-element.96.refs_0_), channel_id=1, source_target_pairs={{0,192},{16,208},{32,224},{48,240},{64,128},{80,144},{96,160},{112... | collective-permute-start | bytes 294920 | tf_op jit(solution)/shard_map/ppermute | solution.py:33
  168.1 6.7 %collective-permute-start.38 = (bf16[128,384]{1,0:T(8,128)(2,1)S(1)}, bf16[128,384]{1,0:T(8,128)(2,1)S(1)}, u32[]{:S(2)}, u32[]{:S(2)}) collective-permute-start(bf16[128,384]{1,0:T(8,128)(2,1)S(1)} %get-tuple-element.96.refs_0_), channel_id=1, source_target_pairs={{0,128},{16,144},{32,160},{48,176},{64,192},{80,208},{96,224},{112... | collective-permute-start | bytes 294920 | tf_op jit(solution)/shard_map/ppermute | solution.py:33
  168.1 8.2 %collective-permute-start.36 = (bf16[128,384]{1,0:T(8,128)(2,1)S(1)}, bf16[128,384]{1,0:T(8,128)(2,1)S(1)}, u32[]{:S(2)}, u32[]{:S(2)}) collective-permute-start(bf16[128,384]{1,0:T(8,128)(2,1)S(1)} %get-tuple-element.96.refs_0_), channel_id=1, source_target_pairs={{0,64},{16,80},{32,96},{48,112},{64,0},{80,16},{96,32},{112,48},{1... | collective-permute-start | bytes 294920 | tf_op jit(solution)/shard_map/ppermute | solution.py:33
  170.2 7.3 %collective-permute-start.35 = (bf16[128,384]{1,0:T(8,128)(2,1)S(1)}, bf16[128,384]{1,0:T(8,128)(2,1)S(1)}, u32[]{:S(2)}, u32[]{:S(2)}) collective-permute-start(bf16[128,384]{1,0:T(8,128)(2,1)S(1)} %get-tuple-element.96.refs_0_), channel_id=1, source_target_pairs={{0,16},{16,0},{32,48},{48,32},{64,80},{80,64},{96,112},{112,96},{1... | collective-permute-start | bytes 294920 | tf_op jit(solution)/shard_map/ppermute | solution.py:33
  172.8 4.7 %collective-permute-start.41 = (bf16[128,384]{1,0:T(8,128)(2,1)S(1)}, bf16[128,384]{1,0:T(8,128)(2,1)S(1)}, u32[]{:S(2)}, u32[]{:S(2)}) collective-permute-start(bf16[128,384]{1,0:T(8,128)(2,1)S(1)} %collective-permute-done.40.refs_3_), channel_id=1, source_target_pairs={{0,16},{16,0},{32,48},{48,32},{64,80},{80,64},{96,112},{112,96},{1... | collective-permute-start | bytes 294920 | tf_op jit(solution)/shard_map/ppermute | solution.py:33
  174.8 2.7 %collective-permute-start.39 = (bf16[128,384]{1,0:T(8,128)(2,1)S(1)}, bf16[128,384]{1,0:T(8,128)(2,1)S(1)}, u32[]{:S(2)}, u32[]{:S(2)}) collective-permute-start(bf16[128,384]{1,0:T(8,128)(2,1)S(1)} %collective-permute-done.38.refs_2_), channel_id=1, source_target_pairs={{0,16},{16,0},{32,48},{48,32},{64,80},{80,64},{96,112},{112,96},{1... | collective-permute-start | bytes 294920 | tf_op jit(solution)/shard_map/ppermute | solution.py:33
  176.2 1.3 collective-permute-start.37

commit v3 on v2

--- a/solution.py
+++ b/solution.py
@@ -37,7 +37,7 @@
     return [swap(pieces[s], axis, s * unit) for s in (1, 2, 3)]
 
 
-def call(kernel, name, args, outs, scratch=(), flops=0, in_hbm=(), in_vmem=(), outs_in_hbm=False, aliases=None):
+def call(kernel, name, args, outs, scratch=(), flops=0, in_hbm=(), in_vmem=(), outs_in_hbm=(), aliases=None):
     vmem, hbm = (pl.BlockSpec(memory_space=m) for m in (pltpu.VMEM, pltpu.HBM))
     moved = sum(math.prod(a.shape) * a.dtype.itemsize for a in [*args, *outs])
     args = list(args)
@@ -48,7 +48,7 @@
     return pl.pallas_call(
         kernel,
         in_specs=[hbm if i in in_hbm else vmem for i in range(len(args))],
-        out_specs=[hbm if outs_in_hbm else vmem] * len(outs),
+        out_specs=[hbm if i in outs_in_hbm else vmem for i in range(len(outs))],
         out_shape=list(outs),
         scratch_shapes=list(scratch),
         input_output_aliases=aliases or {},
@@ -98,6 +98,14 @@
         load.wait()
 
 
+def load_and_store_kernel(s_hbm, residual_ref, s_ref, own_hbm, sems, store_sem):
+    rows = part(coordinate(AT_ZHI), own_hbm.shape[0])
+    store = pltpu.make_async_copy(residual_ref.at[rows, :], own_hbm, store_sem)
+    store.start()
+    load_kernel(s_hbm, residual_ref, s_ref, sems)
+    store.wait()
+
+
 def half_product(other, s_ref, pieces, held):
     half = held.shape[1]
     for s, piece in enumerate(pieces):
@@ -121,15 +129,12 @@
     half_ref[...] = total.astype(BF)
 
 
-def residual_kernel(scale, q_ref, z1, z2, z3, t_ref, half_ref, *own):
-    rows = q_ref.shape[0]
+def residual_kernel(scale, q_ref, z1, z2, z3, t_ref, half_ref, *whole):
     total = (q_ref[...] + z1[...].astype(F32)) + (z2[...].astype(F32) + z3[...].astype(F32))
-    residual = total * scale - t_ref[part(coordinate(AT_X), rows), :]
+    residual = total * scale - t_ref[part(coordinate(AT_X), q_ref.shape[0]), :]
     half_ref[...] = residual.T.astype(BF)
-    if own:
-        own_ref, held = own
-        held[...] = residual
-        own_ref[...] = held[part(coordinate(AT_ZHI), own_ref.shape[0]), :]
+    for out in whole:
+        out[...] = residual
 
 
 def gradient_kernel(other, s_ref, r0, r1, r2, r3, out_ref, held):
@@ -198,11 +203,19 @@
         got = swap4(pieces, "blocks", X_UNIT)
         summed, half = call(sum_kernel, "sum", [pieces[0], *got], [chunk, chunk_half])
         got = swap4([half] * 4, "blocks", ZHI_UNIT)
-        loaded = load(half)
-        half, *residual_own = call(
+        after = half
+        half, *residual = call(
             functools.partial(residual_kernel, scale_factor), "residual", [summed, *got, targets],
-            [shape((k, rows), BF)] + [shape((share, k), F32)] * last, [pltpu.VMEM((rows, k), F32)] * last,
-        )
+            [shape((k, rows), BF)] + [pltpu.VMEM((rows, k), F32)] * last,
+        )
+        residual_own = None
+        if last:
+            loaded, residual_own = call(
+                load_and_store_kernel, "load", [signs, *residual], [pltpu.VMEM(signs.shape, BF), shape((share, k), F32)],
+                [pltpu.SemaphoreType.DMA((4,)), pltpu.SemaphoreType.DMA], in_hbm=(0,), in_vmem=(1,), outs_in_hbm=(1,),
+            )
+        else:
+            loaded = load(after)
         halves = [half] + swap4([half] * 4, "blocks", X_UNIT)
         held = [pltpu.VMEM((k, run_dev), BF)]
         (sent,) = call(
@@ -253,12 +266,12 @@
     near, far, _, residual_own, _ = step(pieces, fitted_own, True)
     held = [pltpu.VMEM((4, width, k), F32), pltpu.SemaphoreType.DMA((4,))]
     whole = [shape((blk_dev, k), F32)]
-    fitted = call(functools.partial(place_kernel, 0), "place_near", near, whole, held, outs_in_hbm=True)
+    fitted = call(functools.partial(place_kernel, 0), "place_near", near, whole, held, outs_in_hbm=(0,))
     (fitted,) = call(
         functools.partial(place_kernel, 1), "place_far", [*far, *fitted], whole, held,
-        in_hbm=(4,), outs_in_hbm=True, aliases={4: 0},
+        in_hbm=(4,), outs_in_hbm=(0,), aliases={4: 0},
     )
-    return (fitted, residual_own[0])
+    return (fitted, residual_own)
 
 
 def solution(mesh):

time: 179 us -> 178 us (level)
  no operation moved by 1% of the time
where the time goes in v3:
time: 178 us
  starting transfers between devices  98.9 us (56%)
  waiting for transfers between devices  54 us (30%)
  Pallas kernels  24 us (13%)
    ppermute x63, starting transfers between devices, swap(): lax.ppermute(array, axis, [(i, i ^ flip) for i in range(lax.axis_size(axi...  98.9 us
    ppermute x63, waiting for transfers between devices, swap(): lax.ppermute(array, axis, [(i, i ^ flip) for i in range(lax.axis_size(axi...  54 us
    pallas_call x31, Pallas kernels, call(): pl.pallas_call(kernel, in_specs=[hbm if i in in_hbm else vmem for i in ra...  24 us
  transfers between devices with their start and end apart: 63, of which 28 were waited for; matrix products, arithmetic and copies ran while one was open for 0% of the time, Pallas kernels for 8%

profile of v3, /device:TPU:1, one launch (start us, length us, event | category | flops | bytes accessed | tf_op | source)
XLA Modules:
  0.0 178.2 jit_solution(4046439047806665614)
XLA Ops:
  0.6 4.2 %first.1 = (f32[256,128]{1,0:T(8,128)S(1)}, bf16[256,128]{1,0:T(8,128)(2,1)S(1)}, bf16[256,128]{1,0:T(8,128)(2,1)S(1)}, bf16[256,128]{1,0:T(8,128)(2,1)S(1)}, f32[128,384]{1,0:T(8,128)S(1)}) custom-call(bf16[1024,3072]{1,0:T(8,128)(2,1)} %s_hbm.3, f32[3072,128]{1,0:T(8,128)} %w_hbm.1), custom_call_target="tpu_custom_call" | custom-call | flops 805306368 | bytes 8388608 | tf_op jit(solution)/shard_map/first/pallas_call | solution.py:48
  4.9 117.3 %while.18 = (s32[]{:T(128)}, f32[256,128]{1,0:T(8,128)S(1)}, bf16[256,128]{1,0:T(8,128)(2,1)S(1)}, bf16[256,128]{1,0:T(8,128)(2,1)S(1)}, bf16[256,128]{1,0:T(8,1...) while((s32[]{:T(128)}, f32[256,128]{1,0:T(8,128)S(1)}, ...), condition=%wide.region_1.0_spmd, body=%wide.region_0.0_spmd.sunk | while | flops 1610612736 | bytes 54330276 | solution.py:263
  4.9 3.4 %collective-permute-start.2 = (bf16[256,128]{1,0:T(8,128)(2,1)S(1)}, bf16[256,128]{1,0:T(8,128)(2,1)S(1)}, u32[]{:S(2)}, u32[]{:S(2)}) collective-permute-start(bf16[256,128]{1,0:T(8,128)(2,1)S(1)} %get-tuple-element.214), channel_id=1, source_target_pairs={{0,12},{1,13},{2,14},{3,15},{4,8},{5,9},{6,10},{7,11},{8,4},{9,5},... | collective-permute-start | bytes 196616 | tf_op jit(solution)/shard_map/while/body/ppermute | solution.py:33
  10.0 3.0 %collective-permute-done.1.g2 = bf16[256,128]{1,0:T(8,128)(2,1)S(1)} collective-permute-done((bf16[256,128]{1,0:T(8,128)(2,1)S(1)}, bf16[256,128]{1,0:T(8,128)(2,1)S(1)}, u32[]{:S(2)}, u32[]{:S(2)}) %collective-permute-start.1) | collective-permute-done | bytes 65568 | tf_op jit(solution)/shard_map/while/body/ppermute | solution.py:33
  13.0 6.0 %collective-permute-start.5 = (bf16[256,128]{1,0:T(8,128)(2,1)S(1)}, bf16[256,128]{1,0:T(8,128)(2,1)S(1)}, u32[]{:S(2)}, u32[]{:S(2)}) collective-permute-start(bf16[256,128]{1,0:T(8,128)(2,1)S(1)} %get-tuple-element.184.after), channel_id=1, source_target_pairs={{0,3},{1,2},{2,1},{3,0},{4,7},{5,6},{6,5},{7,4},{8,11},{9,10},{10,... | collective-permute-start | bytes 196616 | tf_op jit(solution)/shard_map/while/body/ppermute | solution.py:33
  20.1 1.2 collective-permute-start.3
  21.3 5.4 %collective-permute-done.4.z2 = bf16[256,128]{1,0:T(8,128)(2,1)S(1)} collective-permute-done((bf16[256,128]{1,0:T(8,128)(2,1)S(1)}, bf16[256,128]{1,0:T(8,128)(2,1)S(1)}, u32[]{:S(2)}, u32[]{:S(2)}) %collective-permute-start.4) | collective-permute-done | bytes 65568 | tf_op jit(solution)/shard_map/while/body/ppermute | solution.py:33
  26.8 1.4 collective-permute-start.8
  30.1 2.9 %load.3.s_ref = bf16[1024,3072]{1,0:T(8,128)(2,1)S(1)} custom-call(bf16[1024,3072]{1,0:T(8,128)(2,1)} %get-tuple-element.225.s_hbm, bf16[256,128]{1,0:T(8,128)(2,1)S(1)} %get-tuple-element.184.after), custom_call_target="tpu_custom_call" | custom-call | bytes 12648448 | tf_op jit(solution)/shard_map/while/body/load/pallas_call | solution.py:48
  33.6 4.5 %collective-permute-start.9 = (bf16[128,1536]{1,0:T(8,128)(2,1)S(1)}, bf16[128,1536]{1,0:T(8,128)(2,1)S(1)}, u32[]{:S(2)}, u32[]{:S(2)}) collective-permute-start(bf16[128,1536]{1,0:T(8,128)(2,1)S(1)} %gradient_sent.3), channel_id=1, source_target_pairs={{0,16},{16,0},{32,48},{48,32},{64,80},{80,64},{96,112},{112,96},{1... | collective-permute-start | bytes 1179656 | tf_op jit(solution)/shard_map/while/body/ppermute | solution.py:33
  39.6 1.4 collective-permute-start.10
  40.9 2.6 %collective-permute-start.11 = (bf16[128,384]{1,0:T(8,128)(2,1)S(1)}, bf16[128,384]{1,0:T(8,128)(2,1)S(1)}, u32[]{:S(2)}, u32[]{:S(2)}) collective-permute-start(bf16[128,384]{1,0:T(8,128)(2,1)S(1)} %get-tuple-element.188), channel_id=1, source_target_pairs={{0,128},{16,144},{32,160},{48,176},{64,192},{80,208},{96,224},{112... | collective-permute-start | bytes 294920 | tf_op jit(solution)/shard_map/while/body/ppermute | solution.py:33
  43.7 4.6 %collective-permute-done.11.g2 = bf16[128,384]{1,0:T(8,128)(2,1)S(1)} collective-permute-done((bf16[128,384]{1,0:T(8,128)(2,1)S(1)}, bf16[128,384]{1,0:T(8,128)(2,1)S(1)}, u32[]{:S(2)}, u32[]{:S(2)}) %collective-permute-start.11) | collective-permute-done | bytes 98336 | tf_op jit(solution)/shard_map/while/body/ppermute | solution.py:33
  48.2 2.6 %collective-permute-done.12.g3 = bf16[128,384]{1,0:T(8,128)(2,1)S(1)} collective-permute-done((bf16[128,384]{1,0:T(8,128)(2,1)S(1)}, bf16[128,384]{1,0:T(8,128)(2,1)S(1)}, u32[]{:S(2)}, u32[]{:S(2)}) %collective-permute-start.12) | collective-permute-done | bytes 98336 | tf_op jit(solution)/shard_map/while/body/ppermute | solution.py:33
  51.7 2.7 %collective-permute-done.13.got = bf16[128,384]{1,0:T(8,128)(2,1)S(1)} collective-permute-done((bf16[128,384]{1,0:T(8,128)(2,1)S(1)}, bf16[128,384]{1,0:T(8,128)(2,1)S(1)}, u32[]{:S(2)}, u32[]{:S(2)}) %collective-permute-start.13) | collective-permute-done | bytes 98336 | tf_op jit(solution)/shard_map/while/body/ppermute | solution.py:33
  55.4 2.5 %collective-permute-start.14 = (bf16[128,384]{1,0:T(8,128)(2,1)S(1)}, bf16[128,384]{1,0:T(8,128)(2,1)S(1)}, u32[]{:S(2)}, u32[]{:S(2)}) collective-permute-start(bf16[128,384]{1,0:T(8,128)(2,1)S(1)} %get-tuple-element.190.w0), channel_id=1, source_target_pairs={{0,64},{16,80},{32,96},{48,112},{64,0},{80,16},{96,32},{112,48},{1... | collective-permute-start | bytes 294920 | tf_op jit(solution)/shard_map/while/body/ppermute | solution.py:33
  57.9 2.6 %collective-permute-start.17 = (bf16[128,384]{1,0:T(8,128)(2,1)S(1)}, bf16[128,384]{1,0:T(8,128)(2,1)S(1)}, u32[]{:S(2)}, u32[]{:S(2)}) collective-permute-start(bf16[128,384]{1,0:T(8,128)(2,1)S(1)} %get-tuple-element.190.w0), channel_id=1, source_target_pairs={{0,16},{16,0},{32,48},{48,32},{64,80},{80,64},{96,112},{112,96},{1... | collective-permute-start | bytes 294920 | tf_op jit(solution)/shard_map/while/body/ppermute | solution.py:33
  60.5 2.8 %collective-permute-start.20 = (bf16[128,384]{1,0:T(8,128)(2,1)S(1)}, bf16[128,384]{1,0:T(8,128)(2,1)S(1)}, u32[]{:S(2)}, u32[]{:S(2)}) collective-permute-start(bf16[128,384]{1,0:T(8,128)(2,1)S(1)} %collective-permute-done.16.w3), channel_id=1, source_target_pairs={{0,16},{16,0},{32,48},{48,32},{64,80},{80,64},{96,112},{112,96},{1... | collective-permute-start | bytes 294920 | tf_op jit(solution)/shard_map/while/body/ppermute | solution.py:33
  65.2 1.1 other_half.1
  66.3 1.7 collective-permute-start.2
  68.0 1.1 collective-permute-start.1
  69.6 1.1 collective-permute-done.2.g3
  70.7 1.9 %collective-permute-done.1.g2 = bf16[256,128]{1,0:T(8,128)(2,1)S(1)} collective-permute-done((bf16[256,128]{1,0:T(8,128)(2,1)S(1)}, bf16[256,128]{1,0:T(8,128)(2,1)S(1)}, u32[]{:S(2)}, u32[]{:S(2)}) %collective-permute-start.1) | collective-permute-done | bytes 65568 | tf_op jit(solution)/shard_map/while/body/ppermute | solution.py:33
  72.9 1.8 %collective-permute-start.5 = (bf16[256,128]{1,0:T(8,128)(2,1)S(1)}, bf16[256,128]{1,0:T(8,128)(2,1)S(1)}, u32[]{:S(2)}, u32[]{:S(2)}) collective-permute-start(bf16[256,128]{1,0:T(8,128)(2,1)S(1)} %get-tuple-element.184.after), channel_id=1, source_target_pairs={{0,3},{1,2},{2,1},{3,0},{4,7},{5,6},{6,5},{7,4},{8,11},{9,10},{10,... | collective-permute-start | bytes 196616 | tf_op jit(solution)/shard_map/while/body/ppermute | solution.py:33
  74.7 2.5 %collective-permute-start.4 = (bf16[256,128]{1,0:T(8,128)(2,1)S(1)}, bf16[256,128]{1,0:T(8,128)(2,1)S(1)}, u32[]{:S(2)}, u32[]{:S(2)}) collective-permute-start(bf16[256,128]{1,0:T(8,128)(2,1)S(1)} %get-tuple-element.184.after), channel_id=1, source_target_pairs={{0,2},{1,3},{2,0},{3,1},{4,6},{5,7},{6,4},{7,5},{8,10},{9,11},{10,... | collective-permute-start | bytes 196616 | tf_op jit(solution)/shard_map/while/body/ppermute | solution.py:33
  77.2 1.5 collective-permute-start.3
  78.6 3.2 %collective-permute-done.4.z2 = bf16[256,128]{1,0:T(8,128)(2,1)S(1)} collective-permute-done((bf16[256,128]{1,0:T(8,128)(2,1)S(1)}, bf16[256,128]{1,0:T(8,128)(2,1)S(1)}, u32[]{:S(2)}, u32[]{:S(2)}) %collective-permute-start.4) | collective-permute-done | bytes 65568 | tf_op jit(solution)/shard_map/while/body/ppermute | solution.py:33
  81.9 1.5 collective-permute-start.8
  83.4 5.2 %collective-permute-start.7 = (bf16[128,256]{1,0:T(8,128)(2,1)S(1)}, bf16[128,256]{1,0:T(8,128)(2,1)S(1)}, u32[]{:S(2)}, u32[]{:S(2)}) collective-permute-start(bf16[128,256]{1,0:T(8,128)(2,1)S(1)} %residual.3.r0), channel_id=1, source_target_pairs={{0,8},{1,9},{2,10},{3,11},{4,12},{5,13},{6,14},{7,15},{8,0},{9,1},... | collective-permute-start | bytes 196616 | tf_op jit(solution)/shard_map/while/body/ppermute | solution.py:33
  88.6 2.9 %load.3.s_ref = bf16[1024,3072]{1,0:T(8,128)(2,1)S(1)} custom-call(bf16[1024,3072]{1,0:T(8,128)(2,1)} %get-tuple-element.225.s_hbm, bf16[256,128]{1,0:T(8,128)(2,1)S(1)} %get-tuple-element.184.after), custom_call_target="tpu_custom_call" | custom-call | bytes 12648448 | tf_op jit(solution)/shard_map/while/body/load/pallas_call | solution.py:48
  92.5 2.6 %collective-permute-start.9 = (bf16[128,1536]{1,0:T(8,128)(2,1)S(1)}, bf16[128,1536]{1,0:T(8,128)(2,1)S(1)}, u32[]{:S(2)}, u32[]{:S(2)}) collective-permute-start(bf16[128,1536]{1,0:T(8,128)(2,1)S(1)} %gradient_sent.3), channel_id=1, source_target_pairs={{0,16},{16,0},{32,48},{48,32},{64,80},{80,64},{96,112},{112,96},{1... | collective-permute-start | bytes 1179656 | tf_op jit(solution)/shard_map/while/body/ppermute | solution.py:33
  97.2 2.0 %collective-permute-start.11 = (bf16[128,384]{1,0:T(8,128)(2,1)S(1)}, bf16[128,384]{1,0:T(8,128)(2,1)S(1)}, u32[]{:S(2)}, u32[]{:S(2)}) collective-permute-start(bf16[128,384]{1,0:T(8,128)(2,1)S(1)} %get-tuple-element.188), channel_id=1, source_target_pairs={{0,128},{16,144},{32,160},{48,176},{64,192},{80,208},{96,224},{112... | collective-permute-start | bytes 294920 | tf_op jit(solution)/shard_map/while/body/ppermute | solution.py:33
  99.2 1.2 collective-permute-start.12
  100.6 3.3 %collective-permute-done.11.g2 = bf16[128,384]{1,0:T(8,128)(2,1)S(1)} collective-permute-done((bf16[128,384]{1,0:T(8,128)(2,1)S(1)}, bf16[128,384]{1,0:T(8,128)(2,1)S(1)}, u32[]{:S(2)}, u32[]{:S(2)}) %collective-permute-start.11) | collective-permute-done | bytes 98336 | tf_op jit(solution)/shard_map/while/body/ppermute | solution.py:33
  103.8 2.6 %collective-permute-done.12.g3 = bf16[128,384]{1,0:T(8,128)(2,1)S(1)} collective-permute-done((bf16[128,384]{1,0:T(8,128)(2,1)S(1)}, bf16[128,384]{1,0:T(8,128)(2,1)S(1)}, u32[]{:S(2)}, u32[]{:S(2)}) %collective-permute-start.12) | collective-permute-done | bytes 98336 | tf_op jit(solution)/shard_map/while/body/ppermute | solution.py:33
  107.0 3.0 %collective-permute-done.13.got = bf16[128,384]{1,0:T(8,128)(2,1)S(1)} collective-permute-done((bf16[128,384]{1,0:T(8,128)(2,1)S(1)}, bf16[128,384]{1,0:T(8,128)(2,1)S(1)}, u32[]{:S(2)}, u32[]{:S(2)}) %collective-permute-start.13) | collective-permute-done | bytes 98336 | tf_op jit(solution)/shard_map/while/body/ppermute | solution.py:33
  110.2 1.3 collective-permute-start.16
  111.5 2.0 %collective-permute-start.14 = (bf16[128,384]{1,0:T(8,128)(2,1)S(1)}, bf16[128,384]{1,0:T(8,128)(2,1)S(1)}, u32[]{:S(2)}, u32[]{:S(2)}) collective-permute-start(bf16[128,384]{1,0:T(8,128)(2,1)S(1)} %get-tuple-element.190.w0), channel_id=1, source_target_pairs={{0,64},{16,80},{32,96},{48,112},{64,0},{80,16},{96,32},{112,48},{1... | collective-permute-start | bytes 294920 | tf_op jit(solution)/shard_map/while/body/ppermute | solution.py:33
  113.5 2.6 %collective-permute-start.17 = (bf16[128,384]{1,0:T(8,128)(2,1)S(1)}, bf16[128,384]{1,0:T(8,128)(2,1)S(1)}, u32[]{:S(2)}, u32[]{:S(2)}) collective-permute-start(bf16[128,384]{1,0:T(8,128)(2,1)S(1)} %get-tuple-element.190.w0), channel_id=1, source_target_pairs={{0,16},{16,0},{32,48},{48,32},{64,80},{80,64},{96,112},{112,96},{1... | collective-permute-start | bytes 294920 | tf_op jit(solution)/shard_map/while/body/ppermute | solution.py:33
  116.1 2.1 %collective-permute-start.20 = (bf16[128,384]{1,0:T(8,128)(2,1)S(1)}, bf16[128,384]{1,0:T(8,128)(2,1)S(1)}, u32[]{:S(2)}, u32[]{:S(2)}) collective-permute-start(bf16[128,384]{1,0:T(8,128)(2,1)S(1)} %collective-permute-done.16.w3), channel_id=1, source_target_pairs={{0,16},{16,0},{32,48},{48,32},{64,80},{80,64},{96,112},{112,96},{1... | collective-permute-start | bytes 294920 | tf_op jit(solution)/shard_map/while/body/ppermute | solution.py:33
  118.2 1.4 collective-permute-start.19
  121.0 1.1 other_half.1
  122.9 2.3 %collective-permute-start.22 = (bf16[256,128]{1,0:T(8,128)(2,1)S(1)}, bf16[256,128]{1,0:T(8,128)(2,1)S(1)}, u32[]{:S(2)}, u32[]{:S(2)}) collective-permute-start(bf16[256,128]{1,0:T(8,128)(2,1)S(1)} %get-tuple-element.88), channel_id=1, source_target_pairs={{0,8},{1,9},{2,10},{3,11},{4,12},{5,13},{6,14},{7,15},{8,0},{9,1},... | collective-permute-start | bytes 196616 | tf_op jit(solution)/shard_map/ppermute | solution.py:33
  125.2 1.0 collective-permute-start.23
  126.2 2.0 %collective-permute-done.22.g2 = bf16[256,128]{1,0:T(8,128)(2,1)S(1)} collective-permute-done((bf16[256,128]{1,0:T(8,128)(2,1)S(1)}, bf16[256,128]{1,0:T(8,128)(2,1)S(1)}, u32[]{:S(2)}, u32[]{:S(2)}) %collective-permute-start.22) | collective-permute-done | bytes 65568 | tf_op jit(solution)/shard_map/ppermute | solution.py:33
  128.2 1.4 collective-permute-done.23.g3
  129.7 1.8 %collective-permute-start.26 = (bf16[256,128]{1,0:T(8,128)(2,1)S(1)}, bf16[256,128]{1,0:T(8,128)(2,1)S(1)}, u32[]{:S(2)}, u32[]{:S(2)}) collective-permute-start(bf16[256,128]{1,0:T(8,128)(2,1)S(1)} %get-tuple-element.91), channel_id=1, source_target_pairs={{0,3},{1,2},{2,1},{3,0},{4,7},{5,6},{6,5},{7,4},{8,11},{9,10},{10,... | collective-permute-start | bytes 196616 | tf_op jit(solution)/shard_map/ppermute | solution.py:33
  131.4 2.5 %collective-permute-start.25 = (bf16[256,128]{1,0:T(8,128)(2,1)S(1)}, bf16[256,128]{1,0:T(8,128)(2,1)S(1)}, u32[]{:S(2)}, u32[]{:S(2)}) collective-permute-start(bf16[256,128]{1,0:T(8,128)(2,1)S(1)} %get-tuple-element.91), channel_id=1, source_target_pairs={{0,2},{1,3},{2,0},{3,1},{4,6},{5,7},{6,4},{7,5},{8,10},{9,11},{10,... | collective-permute-start | bytes 196616 | tf_op jit(solution)/shard_map/ppermute | solution.py:33
  133.9 1.5 collective-permute-start.24
  135.4 3.2 %collective-permute-done.25.z2 = bf16[256,128]{1,0:T(8,128)(2,1)S(1)} collective-permute-done((bf16[256,128]{1,0:T(8,128)(2,1)S(1)}, bf16[256,128]{1,0:T(8,128)(2,1)S(1)}, u32[]{:S(2)}, u32[]{:S(2)}) %collective-permute-start.25) | collective-permute-done | bytes 65568 | tf_op jit(solution)/shard_map/ppermute | solution.py:33
  138.7 1.6 collective-permute-start.29
  140.3 4.8 %collective-permute-start.28 = (bf16[128,256]{1,0:T(8,128)(2,1)S(1)}, bf16[128,256]{1,0:T(8,128)(2,1)S(1)}, u32[]{:S(2)}, u32[]{:S(2)}) collective-permute-start(bf16[128,256]{1,0:T(8,128)(2,1)S(1)} %get-tuple-element.94.r0), channel_id=1, source_target_pairs={{0,8},{1,9},{2,10},{3,11},{4,12},{5,13},{6,14},{7,15},{8,0},{9,1},... | collective-permute-start | bytes 196616 | tf_op jit(solution)/shard_map/ppermute | solution.py:33
  145.1 2.9 %load.2 = (bf16[1024,3072]{1,0:T(8,128)(2,1)S(1)}, f32[64,128]{1,0:T(8,128)}) custom-call(bf16[1024,3072]{1,0:T(8,128)(2,1)} %get-tuple-element.306, f32[256,128]{1,0:T(8,128)S(1)} %get-tuple-element.92.residual_ref), custom_call_target="tpu_custom_call" | custom-call | bytes 12746752 | tf_op jit(solution)/shard_map/load/pallas_call | solution.py:48
  149.4 1.7 collective-permute-start.30
  153.4 2.1 %collective-permute-start.32 = (bf16[128,384]{1,0:T(8,128)(2,1)S(1)}, bf16[128,384]{1,0:T(8,128)(2,1)S(1)}, u32[]{:S(2)}, u32[]{:S(2)}) collective-permute-start(bf16[128,384]{1,0:T(8,128)(2,1)S(1)} %get-tuple-element.97), channel_id=1, source_target_pairs={{0,128},{16,144},{32,160},{48,176},{64,192},{80,208},{96,224},{112... | collective-permute-start | bytes 294920 | tf_op jit(solution)/shard_map/ppermute | solution.py:33
  155.4 1.1 collective-permute-start.33
  156.6 3.4 %collective-permute-done.32.g2 = bf16[128,384]{1,0:T(8,128)(2,1)S(1)} collective-permute-done((bf16[128,384]{1,0:T(8,128)(2,1)S(1)}, bf16[128,384]{1,0:T(8,128)(2,1)S(1)}, u32[]{:S(2)}, u32[]{:S(2)}) %collective-permute-start.32) | collective-permute-done | bytes 98336 | tf_op jit(solution)/shard_map/ppermute | solution.py:33
  160.1 2.6 %collective-permute-done.33.g3 = bf16[128,384]{1,0:T(8,128)(2,1)S(1)} collective-permute-done((bf16[128,384]{1,0:T(8,128)(2,1)S(1)}, bf16[128,384]{1,0:T(8,128)(2,1)S(1)}, u32[]{:S(2)}, u32[]{:S(2)}) %collective-permute-start.33) | collective-permute-done | bytes 98336 | tf_op jit(solution)/shard_map/ppermute | solution.py:33
  163.3 3.0 %collective-permute-done.34.got = bf16[128,384]{1,0:T(8,128)(2,1)S(1)} collective-permute-done((bf16[128,384]{1,0:T(8,128)(2,1)S(1)}, bf16[128,384]{1,0:T(8,128)(2,1)S(1)}, u32[]{:S(2)}, u32[]{:S(2)}) %collective-permute-start.34) | collective-permute-done | bytes 98336 | tf_op jit(solution)/shard_map/ppermute | solution.py:33
  166.4 1.2 collective-permute-start.40
  167.6 2.2 %collective-permute-start.36 = (bf16[128,384]{1,0:T(8,128)(2,1)S(1)}, bf16[128,384]{1,0:T(8,128)(2,1)S(1)}, u32[]{:S(2)}, u32[]{:S(2)}) collective-permute-start(bf16[128,384]{1,0:T(8,128)(2,1)S(1)} %get-tuple-element.100.refs_0_), channel_id=1, source_target_pairs={{0,64},{16,80},{32,96},{48,112},{64,0},{80,16},{96,32},{112,48},{1... | collective-permute-start | bytes 294920 | tf_op jit(solution)/shard_map/ppermute | solution.py:33
  169.8 2.6 %collective-permute-start.35 = (bf16[128,384]{1,0:T(8,128)(2,1)S(1)}, bf16[128,384]{1,0:T(8,128)(2,1)S(1)}, u32[]{:S(2)}, u32[]{:S(2)}) collective-permute-start(bf16[128,384]{1,0:T(8,128)(2,1)S(1)} %get-tuple-element.100.refs_0_), channel_id=1, source_target_pairs={{0,16},{16,0},{32,48},{48,32},{64,80},{80,64},{96,112},{112,96},{1... | collective-permute-start | bytes 294920 | tf_op jit(solution)/shard_map/ppermute | solution.py:33
  172.4 1.9 %collective-permute-start.41 = (bf16[128,384]{1,0:T(8,128)(2,1)S(1)}, bf16[128,384]{1,0:T(8,128)(2,1)S(1)}, u32[]{:S(2)}, u32[]{:S(2)}) collective-permute-start(bf16[128,384]{1,0:T(8,128)(2,1)S(1)} %collective-permute-done.40.refs_3_), channel_id=1, source_target_pairs={{0,16},{16,0},{32,48},{48,32},{64,80},{80,64},{96,112},{112,96},{1... | collective-permute-start | bytes 294920 | tf_op jit(solution)/shard_map/ppermute | solution.py:33
  174.3 1.4 collective-permute-start.39
  (96 shorter events, 24.5 us)
Async XLA Ops:
  0.6 4.3 %copy-start = (f32[1024,128]{1,0:T(8,128)S(1)}, f32[1024,128]{1,0:T(8,128)}, u32[]{:S(2)}) copy-start(f32[1024,128]{1,0:T(8,128)} %t_ref.1) | copy-start | bytes 1572868
  4.9 5.0 %collective-permute-start.2 = (bf16[256,128]{1,0:T(8,128)(2,1)S(1)}, bf16[256,128]{1,0:T(8,128)(2,1)S(1)}, u32[]{:S(2)}, u32[]{:S(2)}) collective-permute-start(bf16[256,128]{1,0:T(8,128)(2,1)S(1)} %get-tuple-element.214), channel_id=1, source_target_pairs={{0,12},{1,13},{2,14},{3,15},{4,8},{5,9},{6,10},{7,11},{8,4},{9,5},... | collective-permute-start | bytes 196616 | tf_op jit(solution)/shard_map/while/body/ppermute | solution.py:33
  8.3 4.7 %collective-permute-start.1 = (bf16[256,128]{1,0:T(8,128)(2,1)S(1)}, bf16[256,128]{1,0:T(8,128)(2,1)S(1)}, u32[]{:S(2)}, u32[]{:S(2)}) collective-permute-start(bf16[256,128]{1,0:T(8,128)(2,1)S(1)} %get-tuple-element.213), channel_id=1, source_target_pairs={{0,8},{1,9},{2,10},{3,11},{4,12},{5,13},{6,14},{7,15},{8,0},{9,1},... | collective-permute-start | bytes 196616 | tf_op jit(solution)/shard_map/while/body/ppermute | solution.py:33
  8.8 4.2 %collective-permute-start = (bf16[256,128]{1,0:T(8,128)(2,1)S(1)}, bf16[256,128]{1,0:T(8,128)(2,1)S(1)}, u32[]{:S(2)}, u32[]{:S(2)}) collective-permute-start(bf16[256,128]{1,0:T(8,128)(2,1)S(1)} %get-tuple-element.212), channel_id=1, source_target_pairs={{0,4},{1,5},{2,6},{3,7},{4,0},{5,1},{6,2},{7,3},{8,12},{9,13},{10,... | collective-permute-start | bytes 196616 | tf_op jit(solution)/shard_map/while/body/ppermute | solution.py:33
  13.0 8.2 %collective-permute-start.5 = (bf16[256,128]{1,0:T(8,128)(2,1)S(1)}, bf16[256,128]{1,0:T(8,128)(2,1)S(1)}, u32[]{:S(2)}, u32[]{:S(2)}) collective-permute-start(bf16[256,128]{1,0:T(8,128)(2,1)S(1)} %get-tuple-element.184.after), channel_id=1, source_target_pairs={{0,3},{1,2},{2,1},{3,0},{4,7},{5,6},{6,5},{7,4},{8,11},{9,10},{10,... | collective-permute-start | bytes 196616 | tf_op jit(solution)/shard_map/while/body/ppermute | solution.py:33
  19.1 7.6 %collective-permute-start.4 = (bf16[256,128]{1,0:T(8,128)(2,1)S(1)}, bf16[256,128]{1,0:T(8,128)(2,1)S(1)}, u32[]{:S(2)}, u32[]{:S(2)}) collective-permute-start(bf16[256,128]{1,0:T(8,128)(2,1)S(1)} %get-tuple-element.184.after), channel_id=1, source_target_pairs={{0,2},{1,3},{2,0},{3,1},{4,6},{5,7},{6,4},{7,5},{8,10},{9,11},{10,... | collective-permute-start | bytes 196616 | tf_op jit(solution)/shard_map/while/body/ppermute | solution.py:33
  20.1 6.6 %collective-permute-start.3 = (bf16[256,128]{1,0:T(8,128)(2,1)S(1)}, bf16[256,128]{1,0:T(8,128)(2,1)S(1)}, u32[]{:S(2)}, u32[]{:S(2)}) collective-permute-start(bf16[256,128]{1,0:T(8,128)(2,1)S(1)} %get-tuple-element.184.after), channel_id=1, source_target_pairs={{0,1},{1,0},{2,3},{3,2},{4,5},{5,4},{6,7},{7,6},{8,9},{9,8},{10,11... | collective-permute-start | bytes 196616 | tf_op jit(solution)/shard_map/while/body/ppermute | solution.py:33
  26.8 6.2 %collective-permute-start.8 = (bf16[128,256]{1,0:T(8,128)(2,1)S(1)}, bf16[128,256]{1,0:T(8,128)(2,1)S(1)}, u32[]{:S(2)}, u32[]{:S(2)}) collective-permute-start(bf16[128,256]{1,0:T(8,128)(2,1)S(1)} %residual.3.r0), channel_id=1, source_target_pairs={{0,12},{1,13},{2,14},{3,15},{4,8},{5,9},{6,10},{7,11},{8,4},{9,5},... | collective-permute-start | bytes 196616 | tf_op jit(solution)/shard_map/while/body/ppermute | solution.py:33
  28.1 4.9 %collective-permute-start.7 = (bf16[128,256]{1,0:T(8,128)(2,1)S(1)}, bf16[128,256]{1,0:T(8,128)(2,1)S(1)}, u32[]{:S(2)}, u32[]{:S(2)}) collective-permute-start(bf16[128,256]{1,0:T(8,128)(2,1)S(1)} %residual.3.r0), channel_id=1, source_target_pairs={{0,8},{1,9},{2,10},{3,11},{4,12},{5,13},{6,14},{7,15},{8,0},{9,1},... | collective-permute-start | bytes 196616 | tf_op jit(solution)/shard_map/while/body/ppermute | solution.py:33
  29.1 3.9 %collective-permute-start.6 = (bf16[128,256]{1,0:T(8,128)(2,1)S(1)}, bf16[128,256]{1,0:T(8,128)(2,1)S(1)}, u32[]{:S(2)}, u32[]{:S(2)}) collective-permute-start(bf16[128,256]{1,0:T(8,128)(2,1)S(1)} %residual.3.r0), channel_id=1, source_target_pairs={{0,4},{1,5},{2,6},{3,7},{4,0},{5,1},{6,2},{7,3},{8,12},{9,13},{10,... | collective-permute-start | bytes 196616 | tf_op jit(solution)/shard_map/while/body/ppermute | solution.py:33
  33.6 5.8 %collective-permute-start.9 = (bf16[128,1536]{1,0:T(8,128)(2,1)S(1)}, bf16[128,1536]{1,0:T(8,128)(2,1)S(1)}, u32[]{:S(2)}, u32[]{:S(2)}) collective-permute-start(bf16[128,1536]{1,0:T(8,128)(2,1)S(1)} %gradient_sent.3), channel_id=1, source_target_pairs={{0,16},{16,0},{32,48},{48,32},{64,80},{80,64},{96,112},{112,96},{1... | collective-permute-start | bytes 1179656 | tf_op jit(solution)/shard_map/while/body/ppermute | solution.py:33
  39.6 4.1 %collective-permute-start.10 = (bf16[128,384]{1,0:T(8,128)(2,1)S(1)}, bf16[128,384]{1,0:T(8,128)(2,1)S(1)}, u32[]{:S(2)}, u32[]{:S(2)}) collective-permute-start(bf16[128,384]{1,0:T(8,128)(2,1)S(1)} %get-tuple-element.187), channel_id=1, source_target_pairs={{0,64},{16,80},{32,96},{48,112},{64,0},{80,16},{96,32},{112,48},{1... | collective-permute-start | bytes 294920 | tf_op jit(solution)/shard_map/while/body/ppermute | solution.py:33
  40.9 7.3 %collective-permute-start.11 = (bf16[128,384]{1,0:T(8,128)(2,1)S(1)}, bf16[128,384]{1,0:T(8,128)(2,1)S(1)}, u32[]{:S(2)}, u32[]{:S(2)}) collective-permute-start(bf16[128,384]{1,0:T(8,128)(2,1)S(1)} %get-tuple-element.188), channel_id=1, source_target_pairs={{0,128},{16,144},{32,160},{48,176},{64,192},{80,208},{96,224},{112... | collective-permute-start | bytes 294920 | tf_op jit(solution)/shard_map/while/body/ppermute | solution.py:33
  43.6 7.2 %collective-permute-start.12 = (bf16[128,384]{1,0:T(8,128)(2,1)S(1)}, bf16[128,384]{1,0:T(8,128)(2,1)S(1)}, u32[]{:S(2)}, u32[]{:S(2)}) collective-permute-start(bf16[128,384]{1,0:T(8,128)(2,1)S(1)} %get-tuple-element.189), channel_id=1, source_target_pairs={{0,192},{16,208},{32,224},{48,240},{64,128},{80,144},{96,160},{112... | collective-permute-start | bytes 294920 | tf_op jit(solution)/shard_map/while/body/ppermute | solution.py:33
  50.9 3.6 %collective-permute-start.13 = (bf16[128,384]{1,0:T(8,128)(2,1)S(1)}, bf16[128,384]{1,0:T(8,128)(2,1)S(1)}, u32[]{:S(2)}, u32[]{:S(2)}) collective-permute-start(bf16[128,384]{1,0:T(8,128)(2,1)S(1)} %half.3.kept), channel_id=1, source_target_pairs={{0,32},{16,48},{32,0},{48,16},{64,96},{80,112},{96,64},{112,80},{1... | collective-permute-start | bytes 294920 | tf_op jit(solution)/shard_map/while/body/ppermute | solution.py:33
  54.6 5.9 %collective-permute-start.16 = (bf16[128,384]{1,0:T(8,128)(2,1)S(1)}, bf16[128,384]{1,0:T(8,128)(2,1)S(1)}, u32[]{:S(2)}, u32[]{:S(2)}) collective-permute-start(bf16[128,384]{1,0:T(8,128)(2,1)S(1)} %get-tuple-element.190.w0), channel_id=1, source_target_pairs={{0,192},{16,208},{32,224},{48,240},{64,128},{80,144},{96,160},{112... | collective-permute-start | bytes 294920 | tf_op jit(solution)/shard_map/while/body/ppermute | solution.py:33
  55.4 7.9 %collective-permute-start.15 = (bf16[128,384]{1,0:T(8,128)(2,1)S(1)}, bf16[128,384]{1,0:T(8,128)(2,1)S(1)}, u32[]{:S(2)}, u32[]{:S(2)}) collective-permute-start(bf16[128,384]{1,0:T(8,128)(2,1)S(1)} %get-tuple-element.190.w0), channel_id=1, source_target_pairs={{0,128},{16,144},{32,160},{48,176},{64,192},{80,208},{96,224},{112... | collective-permute-start | bytes 294920 | tf_op jit(solution)/shard_map/while/body/ppermute | solution.py:33
  55.4 7.9 %collective-permute-start.14 = (bf16[128,384]{1,0:T(8,128)(2,1)S(1)}, bf16[128,384]{1,0:T(8,128)(2,1)S(1)}, u32[]{:S(2)}, u32[]{:S(2)}) collective-permute-start(bf16[128,384]{1,0:T(8,128)(2,1)S(1)} %get-tuple-element.190.w0), channel_id=1, source_target_pairs={{0,64},{16,80},{32,96},{48,112},{64,0},{80,16},{96,32},{112,48},{1... | collective-permute-start | bytes 294920 | tf_op jit(solution)/shard_map/while/body/ppermute | solution.py:33
  57.9 7.3 %collective-permute-start.17 = (bf16[128,384]{1,0:T(8,128)(2,1)S(1)}, bf16[128,384]{1,0:T(8,128)(2,1)S(1)}, u32[]{:S(2)}, u32[]{:S(2)}) collective-permute-start(bf16[128,384]{1,0:T(8,128)(2,1)S(1)} %get-tuple-element.190.w0), channel_id=1, source_target_pairs={{0,16},{16,0},{32,48},{48,32},{64,80},{80,64},{96,112},{112,96},{1... | collective-permute-start | bytes 294920 | tf_op jit(solution)/shard_map/while/body/ppermute | solution.py:33
  60.5 4.7 %collective-permute-start.20 = (bf16[128,384]{1,0:T(8,128)(2,1)S(1)}, bf16[128,384]{1,0:T(8,128)(2,1)S(1)}, u32[]{:S(2)}, u32[]{:S(2)}) collective-permute-start(bf16[128,384]{1,0:T(8,128)(2,1)S(1)} %collective-permute-done.16.w3), channel_id=1, source_target_pairs={{0,16},{16,0},{32,48},{48,32},{64,80},{80,64},{96,112},{112,96},{1... | collective-permute-start | bytes 294920 | tf_op jit(solution)/shard_map/while/body/ppermute | solution.py:33
  63.3 1.9 %collective-permute-start.19 = (bf16[128,384]{1,0:T(8,128)(2,1)S(1)}, bf16[128,384]{1,0:T(8,128)(2,1)S(1)}, u32[]{:S(2)}, u32[]{:S(2)}) collective-permute-start(bf16[128,384]{1,0:T(8,128)(2,1)S(1)} %collective-permute-done.15.w2), channel_id=1, source_target_pairs={{0,16},{16,0},{32,48},{48,32},{64,80},{80,64},{96,112},{112,96},{1... | collective-permute-start | bytes 294920 | tf_op jit(solution)/shard_map/while/body/ppermute | solution.py:33
  63.3 1.9 %collective-permute-start.18 = (bf16[128,384]{1,0:T(8,128)(2,1)S(1)}, bf16[128,384]{1,0:T(8,128)(2,1)S(1)}, u32[]{:S(2)}, u32[]{:S(2)}) collective-permute-start(bf16[128,384]{1,0:T(8,128)(2,1)S(1)} %collective-permute-done.14.w1), channel_id=1, source_target_pairs={{0,16},{16,0},{32,48},{48,32},{64,80},{80,64},{96,112},{112,96},{1... | collective-permute-start | bytes 294920 | tf_op jit(solution)/shard_map/while/body/ppermute | solution.py:33
  66.3 4.4 %collective-permute-start.2 = (bf16[256,128]{1,0:T(8,128)(2,1)S(1)}, bf16[256,128]{1,0:T(8,128)(2,1)S(1)}, u32[]{:S(2)}, u32[]{:S(2)}) collective-permute-start(bf16[256,128]{1,0:T(8,128)(2,1)S(1)} %get-tuple-element.214), channel_id=1, source_target_pairs={{0,12},{1,13},{2,14},{3,15},{4,8},{5,9},{6,10},{7,11},{8,4},{9,5},... | collective-permute-start | bytes 196616 | tf_op jit(solution)/shard_map/while/body/ppermute | solution.py:33
  68.0 4.6 %collective-permute-start.1 = (bf16[256,128]{1,0:T(8,128)(2,1)S(1)}, bf16[256,128]{1,0:T(8,128)(2,1)S(1)}, u32[]{:S(2)}, u32[]{:S(2)}) collective-permute-start(bf16[256,128]{1,0:T(8,128)(2,1)S(1)} %get-tuple-element.213), channel_id=1, source_target_pairs={{0,8},{1,9},{2,10},{3,11},{4,12},{5,13},{6,14},{7,15},{8,0},{9,1},... | collective-permute-start | bytes 196616 | tf_op jit(solution)/shard_map/while/body/ppermute | solution.py:33
  69.1 3.8 %collective-permute-start = (bf16[256,128]{1,0:T(8,128)(2,1)S(1)}, bf16[256,128]{1,0:T(8,128)(2,1)S(1)}, u32[]{:S(2)}, u32[]{:S(2)}) collective-permute-start(bf16[256,128]{1,0:T(8,128)(2,1)S(1)} %get-tuple-element.212), channel_id=1, source_target_pairs={{0,4},{1,5},{2,6},{3,7},{4,0},{5,1},{6,2},{7,3},{8,12},{9,13},{10,... | collective-permute-start | bytes 196616 | tf_op jit(solution)/shard_map/while/body/ppermute | solution.py:33
  72.9 5.7 %collective-permute-start.5 = (bf16[256,128]{1,0:T(8,128)(2,1)S(1)}, bf16[256,128]{1,0:T(8,128)(2,1)S(1)}, u32[]{:S(2)}, u32[]{:S(2)}) collective-permute-start(bf16[256,128]{1,0:T(8,128)(2,1)S(1)} %get-tuple-element.184.after), channel_id=1, source_target_pairs={{0,3},{1,2},{2,1},{3,0},{4,7},{5,6},{6,5},{7,4},{8,11},{9,10},{10,... | collective-permute-start | bytes 196616 | tf_op jit(solution)/shard_map/while/body/ppermute | solution.py:33
  74.7 7.1 %collective-permute-start.4 = (bf16[256,128]{1,0:T(8,128)(2,1)S(1)}, bf16[256,128]{1,0:T(8,128)(2,1)S(1)}, u32[]{:S(2)}, u32[]{:S(2)}) collective-permute-start(bf16[256,128]{1,0:T(8,128)(2,1)S(1)} %get-tuple-element.184.after), channel_id=1, source_target_pairs={{0,2},{1,3},{2,0},{3,1},{4,6},{5,7},{6,4},{7,5},{8,10},{9,11},{10,... | collective-permute-start | bytes 196616 | tf_op jit(solution)/shard_map/while/body/ppermute | solution.py:33
  77.2 4.7 %collective-permute-start.3 = (bf16[256,128]{1,0:T(8,128)(2,1)S(1)}, bf16[256,128]{1,0:T(8,128)(2,1)S(1)}, u32[]{:S(2)}, u32[]{:S(2)}) collective-permute-start(bf16[256,128]{1,0:T(8,128)(2,1)S(1)} %get-tuple-element.184.after), channel_id=1, source_target_pairs={{0,1},{1,0},{2,3},{3,2},{4,5},{5,4},{6,7},{7,6},{8,9},{9,8},{10,11... | collective-permute-start | bytes 196616 | tf_op jit(solution)/shard_map/while/body/ppermute | solution.py:33
  81.9 9.5 %collective-permute-start.8 = (bf16[128,256]{1,0:T(8,128)(2,1)S(1)}, bf16[128,256]{1,0:T(8,128)(2,1)S(1)}, u32[]{:S(2)}, u32[]{:S(2)}) collective-permute-start(bf16[128,256]{1,0:T(8,128)(2,1)S(1)} %residual.3.r0), channel_id=1, source_target_pairs={{0,12},{1,13},{2,14},{3,15},{4,8},{5,9},{6,10},{7,11},{8,4},{9,5},... | collective-permute-start | bytes 196616 | tf_op jit(solution)/shard_map/while/body/ppermute | solution.py:33
  83.4 8.1 %collective-permute-start.7 = (bf16[128,256]{1,0:T(8,128)(2,1)S(1)}, bf16[128,256]{1,0:T(8,128)(2,1)S(1)}, u32[]{:S(2)}, u32[]{:S(2)}) collective-permute-start(bf16[128,256]{1,0:T(8,128)(2,1)S(1)} %residual.3.r0), channel_id=1, source_target_pairs={{0,8},{1,9},{2,10},{3,11},{4,12},{5,13},{6,14},{7,15},{8,0},{9,1},... | collective-permute-start | bytes 196616 | tf_op jit(solution)/shard_map/while/body/ppermute | solution.py:33
  88.6 3.2 %collective-permute-start.6 = (bf16[128,256]{1,0:T(8,128)(2,1)S(1)}, bf16[128,256]{1,0:T(8,128)(2,1)S(1)}, u32[]{:S(2)}, u32[]{:S(2)}) collective-permute-start(bf16[128,256]{1,0:T(8,128)(2,1)S(1)} %residual.3.r0), channel_id=1, source_target_pairs={{0,4},{1,5},{2,6},{3,7},{4,0},{5,1},{6,2},{7,3},{8,12},{9,13},{10,... | collective-permute-start | bytes 196616 | tf_op jit(solution)/shard_map/while/body/ppermute | solution.py:33
  92.5 3.9 %collective-permute-start.9 = (bf16[128,1536]{1,0:T(8,128)(2,1)S(1)}, bf16[128,1536]{1,0:T(8,128)(2,1)S(1)}, u32[]{:S(2)}, u32[]{:S(2)}) collective-permute-start(bf16[128,1536]{1,0:T(8,128)(2,1)S(1)} %gradient_sent.3), channel_id=1, source_target_pairs={{0,16},{16,0},{32,48},{48,32},{64,80},{80,64},{96,112},{112,96},{1... | collective-permute-start | bytes 1179656 | tf_op jit(solution)/shard_map/while/body/ppermute | solution.py:33
  96.5 4.1 %collective-permute-start.10 = (bf16[128,384]{1,0:T(8,128)(2,1)S(1)}, bf16[128,384]{1,0:T(8,128)(2,1)S(1)}, u32[]{:S(2)}, u32[]{:S(2)}) collective-permute-start(bf16[128,384]{1,0:T(8,128)(2,1)S(1)} %get-tuple-element.187), channel_id=1, source_target_pairs={{0,64},{16,80},{32,96},{48,112},{64,0},{80,16},{96,32},{112,48},{1... | collective-permute-start | bytes 294920 | tf_op jit(solution)/shard_map/while/body/ppermute | solution.py:33
  97.2 6.6 %collective-permute-start.11 = (bf16[128,384]{1,0:T(8,128)(2,1)S(1)}, bf16[128,384]{1,0:T(8,128)(2,1)S(1)}, u32[]{:S(2)}, u32[]{:S(2)}) collective-permute-start(bf16[128,384]{1,0:T(8,128)(2,1)S(1)} %get-tuple-element.188), channel_id=1, source_target_pairs={{0,128},{16,144},{32,160},{48,176},{64,192},{80,208},{96,224},{112... | collective-permute-start | bytes 294920 | tf_op jit(solution)/shard_map/while/body/ppermute | solution.py:33
  99.2 7.2 %collective-permute-start.12 = (bf16[128,384]{1,0:T(8,128)(2,1)S(1)}, bf16[128,384]{1,0:T(8,128)(2,1)S(1)}, u32[]{:S(2)}, u32[]{:S(2)}) collective-permute-start(bf16[128,384]{1,0:T(8,128)(2,1)S(1)} %get-tuple-element.189), channel_id=1, source_target_pairs={{0,192},{16,208},{32,224},{48,240},{64,128},{80,144},{96,160},{112... | collective-permute-start | bytes 294920 | tf_op jit(solution)/shard_map/while/body/ppermute | solution.py:33
  106.5 3.6 %collective-permute-start.13 = (bf16[128,384]{1,0:T(8,128)(2,1)S(1)}, bf16[128,384]{1,0:T(8,128)(2,1)S(1)}, u32[]{:S(2)}, u32[]{:S(2)}) collective-permute-start(bf16[128,384]{1,0:T(8,128)(2,1)S(1)} %half.3.kept), channel_id=1, source_target_pairs={{0,32},{16,48},{32,0},{48,16},{64,96},{80,112},{96,64},{112,80},{1... | collective-permute-start | bytes 294920 | tf_op jit(solution)/shard_map/while/body/ppermute | solution.py:33
  110.2 5.9 %collective-permute-start.16 = (bf16[128,384]{1,0:T(8,128)(2,1)S(1)}, bf16[128,384]{1,0:T(8,128)(2,1)S(1)}, u32[]{:S(2)}, u32[]{:S(2)}) collective-permute-start(bf16[128,384]{1,0:T(8,128)(2,1)S(1)} %get-tuple-element.190.w0), channel_id=1, source_target_pairs={{0,192},{16,208},{32,224},{48,240},{64,128},{80,144},{96,160},{112... | collective-permute-start | bytes 294920 | tf_op jit(solution)/shard_map/while/body/ppermute | solution.py:33
  111.5 6.7 %collective-permute-start.15 = (bf16[128,384]{1,0:T(8,128)(2,1)S(1)}, bf16[128,384]{1,0:T(8,128)(2,1)S(1)}, u32[]{:S(2)}, u32[]{:S(2)}) collective-permute-start(bf16[128,384]{1,0:T(8,128)(2,1)S(1)} %get-tuple-element.190.w0), channel_id=1, source_target_pairs={{0,128},{16,144},{32,160},{48,176},{64,192},{80,208},{96,224},{112... | collective-permute-start | bytes 294920 | tf_op jit(solution)/shard_map/while/body/ppermute | solution.py:33
  111.5 8.2 %collective-permute-start.14 = (bf16[128,384]{1,0:T(8,128)(2,1)S(1)}, bf16[128,384]{1,0:T(8,128)(2,1)S(1)}, u32[]{:S(2)}, u32[]{:S(2)}) collective-permute-start(bf16[128,384]{1,0:T(8,128)(2,1)S(1)} %get-tuple-element.190.w0), channel_id=1, source_target_pairs={{0,64},{16,80},{32,96},{48,112},{64,0},{80,16},{96,32},{112,48},{1... | collective-permute-start | bytes 294920 | tf_op jit(solution)/shard_map/while/body/ppermute | solution.py:33
  113.5 7.3 %collective-permute-start.17 = (bf16[128,384]{1,0:T(8,128)(2,1)S(1)}, bf16[128,384]{1,0:T(8,128)(2,1)S(1)}, u32[]{:S(2)}, u32[]{:S(2)}) collective-permute-start(bf16[128,384]{1,0:T(8,128)(2,1)S(1)} %get-tuple-element.190.w0), channel_id=1, source_target_pairs={{0,16},{16,0},{32,48},{48,32},{64,80},{80,64},{96,112},{112,96},{1... | collective-permute-start | bytes 294920 | tf_op jit(solution)/shard_map/while/body/ppermute | solution.py:33
  116.1 4.7 %collective-permute-start.20 = (bf16[128,384]{1,0:T(8,128)(2,1)S(1)}, bf16[128,384]{1,0:T(8,128)(2,1)S(1)}, u32[]{:S(2)}, u32[]{:S(2)}) collective-permute-start(bf16[128,384]{1,0:T(8,128)(2,1)S(1)} %collective-permute-done.16.w3), channel_id=1, source_target_pairs={{0,16},{16,0},{32,48},{48,32},{64,80},{80,64},{96,112},{112,96},{1... | collective-permute-start | bytes 294920 | tf_op jit(solution)/shard_map/while/body/ppermute | solution.py:33
  118.2 2.6 %collective-permute-start.19 = (bf16[128,384]{1,0:T(8,128)(2,1)S(1)}, bf16[128,384]{1,0:T(8,128)(2,1)S(1)}, u32[]{:S(2)}, u32[]{:S(2)}) collective-permute-start(bf16[128,384]{1,0:T(8,128)(2,1)S(1)} %collective-permute-done.15.w2), channel_id=1, source_target_pairs={{0,16},{16,0},{32,48},{48,32},{64,80},{80,64},{96,112},{112,96},{1... | collective-permute-start | bytes 294920 | tf_op jit(solution)/shard_map/while/body/ppermute | solution.py:33
  119.7 1.3 collective-permute-start.18
  122.3 3.9 %collective-permute-start.21 = (bf16[256,128]{1,0:T(8,128)(2,1)S(1)}, bf16[256,128]{1,0:T(8,128)(2,1)S(1)}, u32[]{:S(2)}, u32[]{:S(2)}) collective-permute-start(bf16[256,128]{1,0:T(8,128)(2,1)S(1)} %get-tuple-element.87), channel_id=1, source_target_pairs={{0,4},{1,5},{2,6},{3,7},{4,0},{5,1},{6,2},{7,3},{8,12},{9,13},{10,... | collective-permute-start | bytes 196616 | tf_op jit(solution)/shard_map/ppermute | solution.py:33
  122.9 5.3 %collective-permute-start.22 = (bf16[256,128]{1,0:T(8,128)(2,1)S(1)}, bf16[256,128]{1,0:T(8,128)(2,1)S(1)}, u32[]{:S(2)}, u32[]{:S(2)}) collective-permute-start(bf16[256,128]{1,0:T(8,128)(2,1)S(1)} %get-tuple-element.88), channel_id=1, source_target_pairs={{0,8},{1,9},{2,10},{3,11},{4,12},{5,13},{6,14},{7,15},{8,0},{9,1},... | collective-permute-start | bytes 196616 | tf_op jit(solution)/shard_map/ppermute | solution.py:33
  125.2 4.5 %collective-permute-start.23 = (bf16[256,128]{1,0:T(8,128)(2,1)S(1)}, bf16[256,128]{1,0:T(8,128)(2,1)S(1)}, u32[]{:S(2)}, u32[]{:S(2)}) collective-permute-start(bf16[256,128]{1,0:T(8,128)(2,1)S(1)} %get-tuple-element.89), channel_id=1, source_target_pairs={{0,12},{1,13},{2,14},{3,15},{4,8},{5,9},{6,10},{7,11},{8,4},{9,5},... | collective-permute-start | bytes 196616 | tf_op jit(solution)/shard_map/ppermute | solution.py:33
  129.7 5.7 %collective-permute-start.26 = (bf16[256,128]{1,0:T(8,128)(2,1)S(1)}, bf16[256,128]{1,0:T(8,128)(2,1)S(1)}, u32[]{:S(2)}, u32[]{:S(2)}) collective-permute-start(bf16[256,128]{1,0:T(8,128)(2,1)S(1)} %get-tuple-element.91), channel_id=1, source_target_pairs={{0,3},{1,2},{2,1},{3,0},{4,7},{5,6},{6,5},{7,4},{8,11},{9,10},{10,... | collective-permute-start | bytes 196616 | tf_op jit(solution)/shard_map/ppermute | solution.py:33
  131.4 7.1 %collective-permute-start.25 = (bf16[256,128]{1,0:T(8,128)(2,1)S(1)}, bf16[256,128]{1,0:T(8,128)(2,1)S(1)}, u32[]{:S(2)}, u32[]{:S(2)}) collective-permute-start(bf16[256,128]{1,0:T(8,128)(2,1)S(1)} %get-tuple-element.91), channel_id=1, source_target_pairs={{0,2},{1,3},{2,0},{3,1},{4,6},{5,7},{6,4},{7,5},{8,10},{9,11},{10,... | collective-permute-start | bytes 196616 | tf_op jit(solution)/shard_map/ppermute | solution.py:33
  133.9 4.7 %collective-permute-start.24 = (bf16[256,128]{1,0:T(8,128)(2,1)S(1)}, bf16[256,128]{1,0:T(8,128)(2,1)S(1)}, u32[]{:S(2)}, u32[]{:S(2)}) collective-permute-start(bf16[256,128]{1,0:T(8,128)(2,1)S(1)} %get-tuple-element.91), channel_id=1, source_target_pairs={{0,1},{1,0},{2,3},{3,2},{4,5},{5,4},{6,7},{7,6},{8,9},{9,8},{10,11... | collective-permute-start | bytes 196616 | tf_op jit(solution)/shard_map/ppermute | solution.py:33
  138.7 9.3 %collective-permute-start.29 = (bf16[128,256]{1,0:T(8,128)(2,1)S(1)}, bf16[128,256]{1,0:T(8,128)(2,1)S(1)}, u32[]{:S(2)}, u32[]{:S(2)}) collective-permute-start(bf16[128,256]{1,0:T(8,128)(2,1)S(1)} %get-tuple-element.94.r0), channel_id=1, source_target_pairs={{0,12},{1,13},{2,14},{3,15},{4,8},{5,9},{6,10},{7,11},{8,4},{9,5},... | collective-permute-start | bytes 196616 | tf_op jit(solution)/shard_map/ppermute | solution.py:33
  140.3 7.7 %collective-permute-start.28 = (bf16[128,256]{1,0:T(8,128)(2,1)S(1)}, bf16[128,256]{1,0:T(8,128)(2,1)S(1)}, u32[]{:S(2)}, u32[]{:S(2)}) collective-permute-start(bf16[128,256]{1,0:T(8,128)(2,1)S(1)} %get-tuple-element.94.r0), channel_id=1, source_target_pairs={{0,8},{1,9},{2,10},{3,11},{4,12},{5,13},{6,14},{7,15},{8,0},{9,1},... | collective-permute-start | bytes 196616 | tf_op jit(solution)/shard_map/ppermute | solution.py:33
  145.1 3.7 %collective-permute-start.27 = (bf16[128,256]{1,0:T(8,128)(2,1)S(1)}, bf16[128,256]{1,0:T(8,128)(2,1)S(1)}, u32[]{:S(2)}, u32[]{:S(2)}) collective-permute-start(bf16[128,256]{1,0:T(8,128)(2,1)S(1)} %get-tuple-element.94.r0), channel_id=1, source_target_pairs={{0,4},{1,5},{2,6},{3,7},{4,0},{5,1},{6,2},{7,3},{8,12},{9,13},{10,... | collective-permute-start | bytes 196616 | tf_op jit(solution)/shard_map/ppermute | solution.py:33
  149.4 3.1 %collective-permute-start.30 = (bf16[128,1536]{1,0:T(8,128)(2,1)S(1)}, bf16[128,1536]{1,0:T(8,128)(2,1)S(1)}, u32[]{:S(2)}, u32[]{:S(2)}) collective-permute-start(bf16[128,1536]{1,0:T(8,128)(2,1)S(1)} %gradient_sent.2), channel_id=1, source_target_pairs={{0,16},{16,0},{32,48},{48,32},{64,80},{80,64},{96,112},{112,96},{1... | collective-permute-start | bytes 1179656 | tf_op jit(solution)/shard_map/ppermute | solution.py:33
  152.6 4.1 %collective-permute-start.31 = (bf16[128,384]{1,0:T(8,128)(2,1)S(1)}, bf16[128,384]{1,0:T(8,128)(2,1)S(1)}, u32[]{:S(2)}, u32[]{:S(2)}) collective-permute-start(bf16[128,384]{1,0:T(8,128)(2,1)S(1)} %get-tuple-element.96), channel_id=1, source_target_pairs={{0,64},{16,80},{32,96},{48,112},{64,0},{80,16},{96,32},{112,48},{1... | collective-permute-start | bytes 294920 | tf_op jit(solution)/shard_map/ppermute | solution.py:33
  153.4 6.7 %collective-permute-start.32 = (bf16[128,384]{1,0:T(8,128)(2,1)S(1)}, bf16[128,384]{1,0:T(8,128)(2,1)S(1)}, u32[]{:S(2)}, u32[]{:S(2)}) collective-permute-start(bf16[128,384]{1,0:T(8,128)(2,1)S(1)} %get-tuple-element.97), channel_id=1, source_target_pairs={{0,128},{16,144},{32,160},{48,176},{64,192},{80,208},{96,224},{112... | collective-permute-start | bytes 294920 | tf_op jit(solution)/shard_map/ppermute | solution.py:33
  155.4 7.2 %collective-permute-start.33 = (bf16[128,384]{1,0:T(8,128)(2,1)S(1)}, bf16[128,384]{1,0:T(8,128)(2,1)S(1)}, u32[]{:S(2)}, u32[]{:S(2)}) collective-permute-start(bf16[128,384]{1,0:T(8,128)(2,1)S(1)} %get-tuple-element.98), channel_id=1, source_target_pairs={{0,192},{16,208},{32,224},{48,240},{64,128},{80,144},{96,160},{112... | collective-permute-start | bytes 294920 | tf_op jit(solution)/shard_map/ppermute | solution.py:33
  162.7 3.6 %collective-permute-start.34 = (bf16[128,384]{1,0:T(8,128)(2,1)S(1)}, bf16[128,384]{1,0:T(8,128)(2,1)S(1)}, u32[]{:S(2)}, u32[]{:S(2)}) collective-permute-start(bf16[128,384]{1,0:T(8,128)(2,1)S(1)} %half.2.kept), channel_id=1, source_target_pairs={{0,32},{16,48},{32,0},{48,16},{64,96},{80,112},{96,64},{112,80},{1... | collective-permute-start | bytes 294920 | tf_op jit(solution)/shard_map/ppermute | solution.py:33
  166.4 5.9 %collective-permute-start.40 = (bf16[128,384]{1,0:T(8,128)(2,1)S(1)}, bf16[128,384]{1,0:T(8,128)(2,1)S(1)}, u32[]{:S(2)}, u32[]{:S(2)}) collective-permute-start(bf16[128,384]{1,0:T(8,128)(2,1)S(1)} %get-tuple-element.100.refs_0_), channel_id=1, source_target_pairs={{0,192},{16,208},{32,224},{48,240},{64,128},{80,144},{96,160},{112... | collective-permute-start | bytes 294920 | tf_op jit(solution)/shard_map/ppermute | solution.py:33
  167.6 6.7 %collective-permute-start.38 = (bf16[128,384]{1,0:T(8,128)(2,1)S(1)}, bf16[128,384]{1,0:T(8,128)(2,1)S(1)}, u32[]{:S(2)}, u32[]{:S(2)}) collective-permute-start(bf16[128,384]{1,0:T(8,128)(2,1)S(1)} %get-tuple-element.100.refs_0_), channel_id=1, source_target_pairs={{0,128},{16,144},{32,160},{48,176},{64,192},{80,208},{96,224},{112... | collective-permute-start | bytes 294920 | tf_op jit(solution)/shard_map/ppermute | solution.py:33
  167.6 8.2 %collective-permute-start.36 = (bf16[128,384]{1,0:T(8,128)(2,1)S(1)}, bf16[128,384]{1,0:T(8,128)(2,1)S(1)}, u32[]{:S(2)}, u32[]{:S(2)}) collective-permute-start(bf16[128,384]{1,0:T(8,128)(2,1)S(1)} %get-tuple-element.100.refs_0_), channel_id=1, source_target_pairs={{0,64},{16,80},{32,96},{48,112},{64,0},{80,16},{96,32},{112,48},{1... | collective-permute-start | bytes 294920 | tf_op jit(solution)/shard_map/ppermute | solution.py:33
  169.8 7.3 %collective-permute-start.35 = (bf16[128,384]{1,0:T(8,128)(2,1)S(1)}, bf16[128,384]{1,0:T(8,128)(2,1)S(1)}, u32[]{:S(2)}, u32[]{:S(2)}) collective-permute-start(bf16[128,384]{1,0:T(8,128)(2,1)S(1)} %get-tuple-element.100.refs_0_), channel_id=1, source_target_pairs={{0,16},{16,0},{32,48},{48,32},{64,80},{80,64},{96,112},{112,96},{1... | collective-permute-start | bytes 294920 | tf_op jit(solution)/shard_map/ppermute | solution.py:33
  172.4 4.7 %collective-permute-start.41 = (bf16[128,384]{1,0:T(8,128)(2,1)S(1)}, bf16[128,384]{1,0:T(8,128)(2,1)S(1)}, u32[]{:S(2)}, u32[]{:S(2)}) collective-permute-start(bf16[128,384]{1,0:T(8,128)(2,1)S(1)} %collective-permute-done.40.refs_3_), channel_id=1, source_target_pairs={{0,16},{16,0},{32,48},{48,32},{64,80},{80,64},{96,112},{112,96},{1... | collective-permute-start | bytes 294920 | tf_op jit(solution)/shard_map/ppermute | solution.py:33
  174.3 2.7 %collective-permute-start.39 = (bf16[128,384]{1,0:T(8,128)(2,1)S(1)}, bf16[128,384]{1,0:T(8,128)(2,1)S(1)}, u32[]{:S(2)}, u32[]{:S(2)}) collective-permute-start(bf16[128,384]{1,0:T(8,128)(2,1)S(1)} %collective-permute-done.38.refs_2_), channel_id=1, source_target_pairs={{0,16},{16,0},{32,48},{48,32},{64,80},{80,64},{96,112},{112,96},{1... | collective-permute-start | bytes 294920 | tf_op jit(solution)/shard_map/ppermute | solution.py:33
  175.7 1.3 collective-permute-start.37
